TPU v7x, 32 devices: a whole 2x2x4 slice. The times are simulated.
32 devices in a mesh: groups: 2 (over y), fsdp: 4 (over z), dp: 4 (over x, core).
Axes of the slice: x: 2, y: 2, z: 4, core: 2. Of those that a mesh axis runs over, the one named last changes fastest.
Arguments:
- stats: bfloat16 [8, 8, 512, 512], P(('groups', 'dp'), None, 'fsdp'), parts along dimension 0, as said below
- grad: bfloat16 [8, 8, 512, 512], P(('groups', 'dp'), None, 'fsdp'), parts along dimension 0
- due: int32 [8, 8], P(('groups', 'dp')), parts along dimension 0, may hold values 0 or 1
- cost: int32 [8, 8], P(('groups', 'dp')), parts along dimension 0, may hold values from 1 to 4
- assign: int32 [8, 8], P(('groups', 'dp')), parts along dimension 0, may hold values from 0 to 7, each once within a row
- stale: bfloat16 [8, 8, 512, 512], P(('groups', 'dp'), 'fsdp'), parts along dimension 0, as said below
Outputs:
- update: bfloat16 [8, 8, 512, 512], P(('groups', 'dp'), None, 'fsdp'), parts along dimension 0
There are 2 independent parts, one for each index of `groups`. A program takes and returns all parts, laid end to end along the dimension named above; each array names one. Nothing has to cross between parts.
Inputs may be any that keep to these rules, and one draw needn't show every extreme that they name: Each dp index's row of assign is a permutation of the 8 solver slots; slot q belongs to the solver at fsdp index q // 2, and stale[d, q] is the previous root held in that slot. `stats`: every block is symmetric positive definite. `stale`: every block is symmetric positive definite.
All inputs are finite; a program needn't handle non-finite values. No bound on the sum of `due` on one device may be relied on, other than what follows from the above.
Results may differ from a plain program's by a relative error of at most 0.0009.
The roundings to bfloat16 on the way count: a program that leaves them out, or rounds other values in their place, can miss the bound.
Values may be sent and summed in bfloat16 or wider, within the bound.
No kernel may reach another device: no remote copies, remote signals or barrier semaphores. Data moves between devices by JAX's collectives and lax.ppermute only.
A program may use at most 64 MiB of HBM per device.

v0:
```python
import jax
import jax.numpy as jnp
from jax import lax
from jax.sharding import PartitionSpec as P

KL_BOUND = 1.0


def refresh(block_piece, grad_rows, old_root, due_flag, sweep_count):
    full_block = block_piece.astype(jnp.float32)
    frobenius = jnp.sqrt(jnp.sum(full_block * full_block))
    identity = jnp.eye(full_block.shape[0], dtype=jnp.float32)
    root_half = (full_block / frobenius).astype(jnp.bfloat16)
    root_inverse = identity.astype(jnp.bfloat16)

    def sweep(step_index, iterates):
        half_now, inverse_now = iterates
        product = jnp.dot(inverse_now, half_now, preferred_element_type=jnp.float32)
        correction = (1.5 * identity - 0.5 * product).astype(jnp.bfloat16)
        half_next = jnp.dot(half_now, correction, preferred_element_type=jnp.float32).astype(
            jnp.bfloat16
        )
        inverse_next = jnp.dot(correction, inverse_now, preferred_element_type=jnp.float32).astype(
            jnp.bfloat16
        )
        return (half_next, inverse_next)

    root_half, root_inverse = lax.fori_loop(0, sweep_count, sweep, (root_half, root_inverse))
    left_factor = jnp.where(due_flag > 0, root_inverse, old_root)
    factor = jnp.where(due_flag > 0, lax.rsqrt(frobenius), jnp.float32(1.0))
    return (jnp.dot(left_factor, grad_rows, preferred_element_type=jnp.float32) * factor).astype(
        jnp.bfloat16
    )


def local(stats, grad, due, cost, assign, stale):
    own_index = lax.axis_index("fsdp")
    solver_count = lax.axis_size("fsdp")
    dp_count = lax.axis_size("dp")
    table_row = assign[0]
    due_row = due[0]
    cost_row = cost[0]
    total_slots = table_row.shape[0]
    slot_count = total_slots // solver_count
    row_count = stats.shape[2]
    block_order = stats.shape[3]
    column_count = grad.shape[3]
    source = jnp.argsort(table_row, stable=True)
    sent_stats = jnp.take(stats[0], source, axis=0).reshape(
        solver_count, slot_count, row_count, block_order
    )
    sent_grad = jnp.take(grad[0], source, axis=0).reshape(
        solver_count, slot_count, row_count, column_count
    )
    blocks_here, grads_here = (
        lax.all_to_all(sent_stats, "fsdp", split_axis=0, concat_axis=2, tiled=True),
        lax.all_to_all(sent_grad, "fsdp", split_axis=0, concat_axis=2, tiled=True),
    )
    my_blocks = lax.dynamic_slice_in_dim(source, own_index * slot_count, slot_count)
    results = []
    for slot in range(slot_count):
        block_id = my_blocks[slot]
        due_flag = due_row[block_id]
        results.append(
            refresh(
                blocks_here[0, slot],
                grads_here[0, slot],
                stale[0, slot],
                due_flag,
                cost_row[block_id] * due_flag,
            )
        )
    solved = jnp.stack(results)
    returned = lax.all_to_all(
        solved.reshape(slot_count, solver_count, row_count, column_count),
        "fsdp",
        split_axis=1,
        concat_axis=0,
        tiled=True,
    )
    owner_rows = jnp.take(returned.reshape(total_slots, row_count, column_count), table_row, axis=0)
    local_part = jnp.sum(owner_rows.astype(jnp.float32) * grad[0].astype(jnp.float32))
    quadratic = lax.psum(local_part, ("fsdp", "dp"))
    elements = dp_count * total_slots * block_order * column_count
    clip_factor = jnp.minimum(jnp.float32(1.0), jnp.sqrt(KL_BOUND * elements / quadratic))
    return (clip_factor * owner_rows.astype(jnp.float32)).astype(jnp.bfloat16)[None]


def solution(mesh):
    return jax.shard_map(
        local,
        mesh=mesh,
        in_specs=(
            P(("groups", "dp"), None, "fsdp", None),
            P(("groups", "dp"), None, "fsdp", None),
            P(("groups", "dp"), None),
            P(("groups", "dp"), None),
            P(("groups", "dp"), None),
            P(("groups", "dp"), "fsdp", None, None),
        ),
        out_specs=P(("groups", "dp"), None, "fsdp", None),
        check_vma=False,
    )
```

profile of v0, /device:TPU:0, one launch (start us, length us, event | category | flops | bytes accessed | tf_op | source)
XLA Modules:
  0.0 145.6 jit_solution(11612052697901835888)
XLA Ops:
  0.0 0.0 copy-start
  0.0 1.7 %sort.17 = (s32[8]{0:T(128)}, s32[8]{0:T(128)S(1)}) sort(s32[8]{0:T(128)} %bitcast.107, s32[8]{0:T(128)S(1)} %iota.30), dimensions={0}, to_apply=%region_0.0 | sort | flops 24 | bytes 128 | tf_op jit(solution)/shard_map/jit(argsort)/sort | solution.py:48
  1.7 0.0 copy-done
  1.7 0.6 gather_fusion
  2.4 1.8 %gather_fusion.1 = bf16[8,128,512]{2,1,0:T(8,128)(2,1)S(1)} fusion(bf16[8,128,512]{2,1,0:T(8,128)(2,1)} %bitcast.101, s32[1024]{0:T(1024)S(1)} %pad_clamp_fusion.1), kind=kCustom, calls=%fused_computation.1.clone | custom fusion | bytes 2097184 | tf_op jit(solution)/shard_map/jit(_take)/gather | solution.py:52
  4.2 1.6 %broadcast_select_fusion.2 = (bf16[8,128,512]{2,1,0:T(8,128)(2,1)}, bf16[8,128,512]{2,1,0:T(8,128)(2,1)}) fusion(bf16[8,128,512]{2,1,0:T(8,128)(2,1)S(1)} %gather_fusion, pred[8]{0:T(512)(128)(4,1)S(1)} %compare_and_fusion.1, bf16[8,128,512]{2,1,0:T(8,128)(2,1)S(1)} %gather_fusion.1), kind=kLoop, calls=%fused_computation.41 | loop fusion | flops 1048576 | bytes 4194312 | tf_op jit(solution)/shard_map/jit(_take)/select_n | solution.py:49
  5.8 1.6 %copy.19 = bf16[8,128,512]{1,2,0:T(8,128)(2,1)S(1)} copy(bf16[8,128,512]{2,1,0:T(8,128)(2,1)} %get-tuple-element.122) | data formatting | bytes 2097152 | tf_op jit(solution)/shard_map/jit(_take)/select_n | solution.py:49
  7.4 31.9 %all_to_all.51 = bf16[4,2,128,512]{2,3,1,0:T(8,128)(2,1)} all-to-all(bf16[4,2,128,512]{2,3,1,0:T(8,128)(2,1)S(1)} %bitcast.102), channel_id=1, replica_groups=mesh['groups'=2,'fsdp'=4,'dp'=4] {'fsdp'}, dimensions={0} | all-to-all | bytes 2097152 | tf_op jit(solution)/shard_map/all_to_all | solution.py:56
  39.4 4.3 %all-to-all-start.1 = ((bf16[4,2,128,512]{3,2,1,0:T(8,128)(2,1)}), bf16[4,2,128,512]{3,2,1,0:T(8,128)(2,1)}, u32[]{:S(2)}, u32[]{:S(2)}) async-start(bf16[4,2,128,512]{3,2,1,0:T(8,128)(2,1)} %bitcast.12), calls=%async_computation.1 | async-start | bytes 2097152 | tf_op jit(solution)/shard_map/all_to_all | solution.py:57
  43.6 0.0 copy-start.4
  43.6 0.0 copy-start.5
  43.7 0.1 dynamic_slice.15
  43.7 0.6 fusion.25
  48.0 0.0 copy-done.4
  48.0 0.0 copy-done.5
  48.0 0.7 constant_dynamic-slice_fusion.2
  52.4 1.5 %copy.20 = bf16[4,2,128,512]{3,2,0,1:T(8,128)(2,1)S(1)} copy(bf16[4,2,128,512]{2,3,1,0:T(8,128)(2,1)} %all_to_all.51) | data formatting | bytes 2097152 | tf_op jit(solution)/shard_map/all_to_all | solution.py:56
  53.9 0.9 fusion.14
  56.3 1.2 fusion.20
  57.5 11.1 %all-to-all-done.1 = bf16[4,2,128,512]{3,2,1,0:T(8,128)(2,1)} async-done(((bf16[4,2,128,512]{3,2,1,0:T(8,128)(2,1)}), bf16[4,2,128,512]{3,2,1,0:T(8,128)(2,1)}, u32[]{:S(2)}, u32[]{:S(2)}) %all-to-all-start.1) | async-done | bytes 1048608 | tf_op jit(solution)/shard_map/all_to_all | solution.py:57
  68.6 0.0 copy-start.2
  68.6 2.3 %copy.22 = bf16[1,2,4,128,512]{4,3,2,1,0:T(8,128)(2,1)} copy(bf16[1,2,4,128,512]{4,3,1,2,0:T(8,128)(2,1)} %bitcast.14) | data formatting | bytes 2097152 | tf_op jit(solution)/shard_map/all_to_all | solution.py:57
  70.9 0.0 copy-done.2
  70.9 0.2 copy.23
  71.1 0.0 copy-start.1
  71.1 1.0 copy-done.1
  72.2 0.2 copy.21
  72.4 0.0 copy-start.3
  72.4 0.0 copy-start.6
  72.4 1.8 %fusion.13 = bf16[512,512]{1,0:T(8,128)(2,1)S(1)} fusion(bf16[1,2,512,512]{3,2,1,0:T(8,128)(2,1)} %bitcast.103, bf16[512,512]{1,0:T(8,128)(2,1)S(1)} %get-tuple-element.65, f32[]{:T(128)S(6)} %select_n.47, bf16[1,2,512,512]{3,2,1,0:T(8,128)(2,1)} %param.17, pred[]{:T(512)} %bitcast.20), kind=kOutput, calls=%fused_computation.30 | convolution fusion | flops 269221888 | bytes 2097668 | tf_op jit(solution)/shard_map/dot_general | solution.py:31
  74.2 0.0 copy-done.3
  74.2 0.0 copy-done.6
  74.3 0.4 fusion.12
  74.7 1.1 pad_maximum_fusion
  75.8 0.0 copy-start.7
  75.8 10.8 %all-to-all-start.2 = ((bf16[2,4,128,512]{3,2,0,1:T(8,128)(2,1)}), bf16[2,4,128,512]{3,2,0,1:T(8,128)(2,1)S(1)}, u32[]{:S(2)}, u32[]{:S(2)}) async-start(bf16[2,4,128,512]{3,2,0,1:T(8,128)(2,1)} %pad_maximum_fusion), calls=%async_computation.2 | async-start | bytes 2097152 | tf_op jit(solution)/shard_map/all_to_all | solution.py:74
  86.6 0.0 copy-done.7
  86.6 23.8 %all-to-all-done.2 = bf16[2,4,128,512]{3,2,0,1:T(8,128)(2,1)S(1)} async-done(((bf16[2,4,128,512]{3,2,0,1:T(8,128)(2,1)}), bf16[2,4,128,512]{3,2,0,1:T(8,128)(2,1)S(1)}, u32[]{:S(2)}, u32[]{:S(2)}) %all-to-all-start.2) | async-done | bytes 1048608 | tf_op jit(solution)/shard_map/all_to_all | solution.py:74
  110.4 0.6 gather_fusion.2
  111.0 2.4 %fusion.10 = f32[]{:T(128)} fusion(bf16[8,128,512]{2,1,0:T(8,128)(2,1)S(1)} %gather_fusion.2, pred[8]{0:T(512)(128)(4,1)S(1)} %compare_and_fusion, bf16[1,8,128,512]{3,2,1,0:T(8,128)(2,1)} %param.13), kind=kLoop, calls=%fused_computation.21 | loop fusion | flops 2621439 | bytes 2097164 | tf_op jit(solution)/shard_map/reduce_sum | solution.py:82
  113.5 30.1 %psum.7 = f32[]{:T(128)} all-reduce(f32[]{:T(128)} %fusion.10), channel_id=1, replica_groups=mesh['groups'=2,'fsdp'=4,'dp'=4] {'fsdp','dp'}, use_global_device_ids=true, to_apply=%region_8.10 | all-reduce | flops 1 | bytes 8 | tf_op jit(solution)/shard_map/psum | solution.py:83
  144.3 1.3 fusion.18
  (11 shorter events, 0.1 us)
Async XLA Ops:
  0.0 1.7 %copy-start = (bf16[1,8,128,512]{3,2,1,0:T(8,128)(2,1)S(1)}, bf16[1,8,128,512]{3,2,1,0:T(8,128)(2,1)}, u32[]{:S(2)}) copy-start(bf16[1,8,128,512]{3,2,1,0:T(8,128)(2,1)} %param.12) | copy-start | bytes 3145732
  39.4 29.2 %all-to-all-start.1 = ((bf16[4,2,128,512]{3,2,1,0:T(8,128)(2,1)}), bf16[4,2,128,512]{3,2,1,0:T(8,128)(2,1)}, u32[]{:S(2)}, u32[]{:S(2)}) async-start(bf16[4,2,128,512]{3,2,1,0:T(8,128)(2,1)} %bitcast.12), calls=%async_computation.1 | async-start | bytes 2097152 | tf_op jit(solution)/shard_map/all_to_all | solution.py:57
  43.6 4.3 %copy-start.4 = (s32[1,8]{1,0:T(1,128)S(1)}, s32[1,8]{1,0:T(1,128)}, u32[]{:S(2)}) copy-start(s32[1,8]{1,0:T(1,128)} %param.15) | copy-start | bytes 100
  43.6 4.3 %copy-start.5 = (s32[1,8]{1,0:T(1,128)S(1)}, s32[1,8]{1,0:T(1,128)}, u32[]{:S(2)}) copy-start(s32[1,8]{1,0:T(1,128)} %param.14) | copy-start | bytes 100
  68.6 2.3 %copy-start.2 = (bf16[512,512]{1,0:T(8,128)(2,1)S(1)}, bf16[512,512]{1,0:T(8,128)(2,1)}, u32[]{:S(2)}) copy-start(bf16[512,512]{1,0:T(8,128)(2,1)} %get-tuple-element.115) | copy-start | bytes 1572868
  71.1 1.0 copy-start.1
  72.4 1.8 %copy-start.3 = (bf16[1,2,4,128,512]{4,3,2,1,0:T(8,128)(2,1)S(1)}, bf16[1,2,4,128,512]{4,3,2,1,0:T(8,128)(2,1)}, u32[]{:S(2)}) copy-start(bf16[1,2,4,128,512]{4,3,2,1,0:T(8,128)(2,1)} %copy.22) | copy-start | bytes 3145732
  72.4 1.8 %copy-start.6 = (bf16[1,2,512,512]{3,2,1,0:T(8,128)(2,1)S(1)}, bf16[1,2,512,512]{3,2,1,0:T(8,128)(2,1)}, u32[]{:S(2)}) copy-start(bf16[1,2,512,512]{3,2,1,0:T(8,128)(2,1)} %param.17) | copy-start | bytes 3145732
  75.8 10.8 %copy-start.7 = (s32[1,8]{1,0:T(1,128)S(1)}, s32[1,8]{1,0:T(1,128)}, u32[]{:S(2)}) copy-start(s32[1,8]{1,0:T(1,128)} %param.16) | copy-start | bytes 100
  75.8 34.6 %all-to-all-start.2 = ((bf16[2,4,128,512]{3,2,0,1:T(8,128)(2,1)}), bf16[2,4,128,512]{3,2,0,1:T(8,128)(2,1)S(1)}, u32[]{:S(2)}, u32[]{:S(2)}) async-start(bf16[2,4,128,512]{3,2,0,1:T(8,128)(2,1)} %pad_maximum_fusion), calls=%async_computation.2 | async-start | bytes 2097152 | tf_op jit(solution)/shard_map/all_to_all | solution.py:74
where the time goes:
time: 146 us
  blocking collectives  62.1 us (43%)
  waiting for transfers between devices  34.9 us (24%)
  starting transfers between devices  15.1 us (10%)
  local copies, waits for them, and re-layouts  11.3 us (8%)
  other arithmetic  10.2 us (7%)
  between operations  9.75 us (7%)
  matrix products  2.21 us (2%)
    all_to_all x1, blocking collectives, local(): lax.all_to_all(sent_stats, 'fsdp', split_axis=0, concat_axis=2, tiled=True)  31.9 us
    psum x1, blocking collectives, local(): quadratic = lax.psum(local_part, ('fsdp', 'dp'))  30.1 us
    all_to_all x1, waiting for transfers between devices, local(): lax.all_to_all(solved.reshape(slot_count, solver_count, row_count, column...  23.8 us
    all_to_all x1, waiting for transfers between devices, local(): lax.all_to_all(sent_grad, 'fsdp', split_axis=0, concat_axis=2, tiled=True)  11.1 us
    all_to_all x1, starting transfers between devices, local(): lax.all_to_all(solved.reshape(slot_count, solver_count, row_count, column...  10.8 us
    all_to_all x1, starting transfers between devices, local(): lax.all_to_all(sent_grad, 'fsdp', split_axis=0, concat_axis=2, tiled=True)  4.26 us
  transfers between devices with their start and end apart: 2, of which 2 were waited for; matrix products, arithmetic and copies ran while one was open for 3% of the time, Pallas kernels for 0%

commit v1 on v0

--- a/solution.py
+++ b/solution.py
@@ -1,39 +1,40 @@
+import functools
+
 import jax
 import jax.numpy as jnp
 from jax import lax
+from jax.experimental import pallas as pl
+from jax.experimental.pallas import tpu as pltpu
 from jax.sharding import PartitionSpec as P
 
 KL_BOUND = 1.0
+VMEM_BYTES = 40 * 2**20
+F32 = jnp.float32
+BF16 = jnp.bfloat16
 
 
 def refresh(block_piece, grad_rows, old_root, due_flag, sweep_count):
-    full_block = block_piece.astype(jnp.float32)
+    full_block = block_piece.astype(F32)
     frobenius = jnp.sqrt(jnp.sum(full_block * full_block))
-    identity = jnp.eye(full_block.shape[0], dtype=jnp.float32)
-    root_half = (full_block / frobenius).astype(jnp.bfloat16)
-    root_inverse = identity.astype(jnp.bfloat16)
+    identity = jnp.eye(full_block.shape[0], dtype=F32)
+    root_half = (full_block / frobenius).astype(BF16)
+    root_inverse = identity.astype(BF16)
 
     def sweep(step_index, iterates):
         half_now, inverse_now = iterates
-        product = jnp.dot(inverse_now, half_now, preferred_element_type=jnp.float32)
-        correction = (1.5 * identity - 0.5 * product).astype(jnp.bfloat16)
-        half_next = jnp.dot(half_now, correction, preferred_element_type=jnp.float32).astype(
-            jnp.bfloat16
-        )
-        inverse_next = jnp.dot(correction, inverse_now, preferred_element_type=jnp.float32).astype(
-            jnp.bfloat16
-        )
+        product = jnp.dot(inverse_now, half_now, preferred_element_type=F32)
+        correction = (1.5 * identity - 0.5 * product).astype(BF16)
+        half_next = jnp.dot(half_now, correction, preferred_element_type=F32).astype(BF16)
+        inverse_next = jnp.dot(correction, inverse_now, preferred_element_type=F32).astype(BF16)
         return (half_next, inverse_next)
 
     root_half, root_inverse = lax.fori_loop(0, sweep_count, sweep, (root_half, root_inverse))
     left_factor = jnp.where(due_flag > 0, root_inverse, old_root)
-    factor = jnp.where(due_flag > 0, lax.rsqrt(frobenius), jnp.float32(1.0))
-    return (jnp.dot(left_factor, grad_rows, preferred_element_type=jnp.float32) * factor).astype(
-        jnp.bfloat16
-    )
-
-
-def local(stats, grad, due, cost, assign, stale):
+    factor = jnp.where(due_flag > 0, lax.rsqrt(frobenius), F32(1.0))
+    return (jnp.dot(left_factor, grad_rows, preferred_element_type=F32) * factor).astype(BF16)
+
+
+def exchange_all(stats, grad, due, cost, assign, stale):
     own_index = lax.axis_index("fsdp")
     solver_count = lax.axis_size("fsdp")
     dp_count = lax.axis_size("dp")
@@ -79,16 +80,379 @@
         tiled=True,
     )
     owner_rows = jnp.take(returned.reshape(total_slots, row_count, column_count), table_row, axis=0)
-    local_part = jnp.sum(owner_rows.astype(jnp.float32) * grad[0].astype(jnp.float32))
+    local_part = jnp.sum(owner_rows.astype(F32) * grad[0].astype(F32))
     quadratic = lax.psum(local_part, ("fsdp", "dp"))
     elements = dp_count * total_slots * block_order * column_count
-    clip_factor = jnp.minimum(jnp.float32(1.0), jnp.sqrt(KL_BOUND * elements / quadratic))
-    return (clip_factor * owner_rows.astype(jnp.float32)).astype(jnp.bfloat16)[None]
+    clip_factor = jnp.minimum(F32(1.0), jnp.sqrt(KL_BOUND * elements / quadratic))
+    return (clip_factor * owner_rows.astype(F32)).astype(BF16)[None]
+
+
+def call(kernel, out_shape, in_specs, out_specs, name, scratch=(), flops=0, moved=0):
+    return pl.pallas_call(
+        kernel,
+        out_shape=out_shape,
+        in_specs=in_specs,
+        out_specs=out_specs,
+        scratch_shapes=list(scratch),
+        compiler_params=pltpu.CompilerParams(vmem_limit_bytes=VMEM_BYTES),
+        cost_estimate=pl.CostEstimate(flops=flops, bytes_accessed=moved, transcendentals=0),
+        name=name,
+    )
+
+
+IN_VMEM = pl.BlockSpec(memory_space=pltpu.VMEM)
+IN_SMEM = pl.BlockSpec(memory_space=pltpu.SMEM)
+ANYWHERE = pl.BlockSpec(memory_space=pl.ANY)
+
+
+def block_in_slot(assign_ref, slot):
+    found = jnp.int32(0)
+    for block in range(assign_ref.shape[1]):
+        found = jnp.where(assign_ref[0, block] == slot, jnp.int32(block), found)
+    return found
+
+
+def tile_at(index, width):
+    return pl.ds(pl.multiple_of(index * width, width), width)
+
+
+def pack_stats_kernel(slots, me_ref, assign_ref, stats_ref, near_ref, far2_ref, far3_ref):
+    me = me_ref[0]
+    width = stats_ref.shape[2]
+    half = width // 2
+    odd = me % 2
+    for slot in range(slots):
+        for far, out in ((2, far2_ref), (3, far3_ref)):
+            block = block_in_slot(assign_ref, (me ^ far) * slots + slot)
+            out[slot, :width, :] = stats_ref[0, block, :, tile_at(me, width)]
+            between = stats_ref[0, block, :, tile_at(me ^ 1, width)].astype(F32)
+            out[slot, width:, :] = jnp.where(
+                odd == 1, between.T[half:, :], between[:half, :]
+            ).astype(BF16)
+    for slot in range(slots):
+        block = block_in_slot(assign_ref, (me ^ 1) * slots + slot)
+        for place, other in enumerate((0, 2, 3)):
+            near_ref[slot, :, place * width : (place + 1) * width] = stats_ref[
+                0, block, :, tile_at(me ^ other, width)
+            ]
+
+
+def pack_stats(me, assign, stats, slots):
+    width, order = stats.shape[2:]
+    near = jax.ShapeDtypeStruct((slots, width, order - width), BF16)
+    far = jax.ShapeDtypeStruct((slots, width + width // 2, width), BF16)
+    return call(
+        functools.partial(pack_stats_kernel, slots),
+        (near, far, far),
+        [IN_SMEM, IN_SMEM, IN_VMEM],
+        (IN_VMEM,) * 3,
+        "pack_stats",
+        moved=2 * stats.size * 2,
+    )(me, assign, stats)
+
+
+def pack_grad_kernel(slots, me_ref, assign_ref, grad_ref, *rest):
+    outs, sems = rest[:-1], rest[-1]
+    me = me_ref[0]
+    copies = []
+    for slot in range(slots):
+        for far in range(4):
+            at = slot * 4 + far
+            block = block_in_slot(assign_ref, (me ^ far) * slots + slot)
+            copy = pltpu.make_async_copy(grad_ref.at[0, block], outs[at], sems.at[at])
+            copy.start()
+            copies.append(copy)
+    for copy in copies:
+        copy.wait()
+
+
+def pack_grad(me, assign, grad, slots):
+    out = jax.ShapeDtypeStruct(grad.shape[2:], BF16)
+    count = 4 * slots
+    flat = call(
+        functools.partial(pack_grad_kernel, slots),
+        (out,) * count,
+        [IN_SMEM, IN_SMEM, ANYWHERE],
+        (ANYWHERE,) * count,
+        "pack_grad",
+        scratch=[pltpu.SemaphoreType.DMA((count,))],
+        moved=2 * grad.size * 2,
+    )(me, assign, grad)
+    return [flat[slot * 4 : slot * 4 + 4] for slot in range(slots)]
+
+
+def root_kernel(
+    slots,
+    me_ref,
+    assign_ref,
+    due_ref,
+    cost_ref,
+    stats_ref,
+    near_ref,
+    far2_ref,
+    far3_ref,
+    stale_ref,
+    root_ref,
+    factor_ref,
+    own,
+    full,
+    half_root,
+    correction,
+    sem,
+    stale_sem,
+):
+    me = me_ref[0]
+    order = full.shape[0]
+    width = near_ref.shape[1]
+    half = width // 2
+    chunk = order // 2
+    rows = [pl.ds(start, chunk) for start in range(0, order, chunk)]
+
+    def eye_rows(start):
+        r = lax.broadcasted_iota(jnp.int32, (chunk, order), 0) + start
+        c = lax.broadcasted_iota(jnp.int32, (chunk, order), 1)
+        return jnp.where(r == c, F32(1.5), F32(0.0))
+
+    def assemble(slot, block):
+        copy = pltpu.make_async_copy(stats_ref.at[0, block], own, sem)
+        copy.start()
+        even, odd = (me ^ 2) & 2, ((me ^ 2) & 2) + 1
+        at = lambda index: tile_at(index, width)
+        two, three = me ^ 2, me ^ 3
+        full[at(two), at(two)] = far2_ref[slot, :width, :].astype(F32)
+        full[at(three), at(three)] = far3_ref[slot, :width, :].astype(F32)
+        from_two = far2_ref[slot, width:, :].astype(F32)
+        from_three = far3_ref[slot, width:, :].astype(F32)
+        two_is_even = me % 2 == 0
+        between = jnp.concatenate(
+            [
+                jnp.where(two_is_even, from_two, from_three),
+                jnp.where(two_is_even, from_three, from_two),
+            ],
+            axis=0,
+        )
+        full[at(even), at(odd)] = between
+        full[at(odd), at(even)] = between.T
+        near = me ^ 1
+        for place, other in enumerate((0, 2, 3)):
+            tile = near_ref[slot, :, place * width : (place + 1) * width].astype(F32)
+            full[at(near), at(near ^ other)] = tile
+            if other:
+                full[at(near ^ other), at(near)] = tile.T
+        copy.wait()
+        full[at(me), :] = own[...].astype(F32)
+        for other in (1, 2, 3):
+            full[at(me ^ other), at(me)] = own[:, at(me ^ other)].astype(F32).T
+
+    for slot in range(slots):
+        block = block_in_slot(assign_ref, me * slots + slot)
+        due = due_ref[0, block]
+        cost = cost_ref[0, block]
+        factor_ref[slot] = F32(1.0)
+
+        @pl.when(due <= 0)
+        def _():
+            copy = pltpu.make_async_copy(stale_ref.at[0, slot], root_ref.at[slot], stale_sem)
+            copy.start()
+            copy.wait()
+
+        @pl.when(due > 0)
+        def _():
+            assemble(slot, block)
+            total = jnp.zeros((8, order), F32)
+            for start in range(0, order, 8):
+                piece = full[start : start + 8, :]
+                total = total + piece * piece
+            norm = jnp.sqrt(jnp.full((8, 128), jnp.sum(total), F32))
+            factor_ref[slot] = lax.rsqrt(norm)[0, 0]
+            divisor = jnp.max(norm)
+            for i, start in enumerate(range(0, order, chunk)):
+                scaled = (full[rows[i], :] / divisor).astype(BF16)
+                half_root[rows[i], :] = scaled
+                root_ref[slot, rows[i], :] = (eye_rows(start) - 0.5 * scaled.astype(F32)).astype(
+                    BF16
+                )
+
+            @pl.when(cost > 1)
+            def _():
+                first = [
+                    jnp.dot(half_root[r, :], root_ref[slot], preferred_element_type=F32).astype(BF16)
+                    for r in rows
+                ]
+                for r, value in zip(rows, first):
+                    half_root[r, :] = value
+
+                def correct():
+                    for i, start in enumerate(range(0, order, chunk)):
+                        product = jnp.dot(
+                            root_ref[slot, rows[i], :], half_root[...], preferred_element_type=F32
+                        )
+                        correction[rows[i], :] = (eye_rows(start) - 0.5 * product).astype(BF16)
+
+                def next_root():
+                    values = [
+                        jnp.dot(
+                            correction[r, :], root_ref[slot], preferred_element_type=F32
+                        ).astype(BF16)
+                        for r in rows
+                    ]
+                    for r, value in zip(rows, values):
+                        root_ref[slot, r, :] = value
+
+                def sweep(step, carry):
+                    correct()
+                    values = [
+                        jnp.dot(
+                            half_root[r, :], correction[...], preferred_element_type=F32
+                        ).astype(BF16)
+                        for r in rows
+                    ]
+                    for r, value in zip(rows, values):
+                        half_root[r, :] = value
+                    next_root()
+                    return carry
+
+                lax.fori_loop(0, cost - 2, sweep, 0)
+                correct()
+                next_root()
+
+
+def roots(me, assign, due, cost, stats, received, stale, slots):
+    order = stats.shape[3]
+    width = stats.shape[2]
+    return call(
+        functools.partial(root_kernel, slots),
+        (
+            jax.ShapeDtypeStruct((slots, order, order), BF16),
+            jax.ShapeDtypeStruct((slots,), F32),
+        ),
+        [IN_SMEM] * 4 + [ANYWHERE] + [IN_VMEM] * 3 + [ANYWHERE],
+        (IN_VMEM, IN_SMEM),
+        "roots",
+        scratch=[
+            pltpu.VMEM((width, order), BF16),
+            pltpu.VMEM((order, order), F32),
+            pltpu.VMEM((order, order), BF16),
+            pltpu.VMEM((order, order), BF16),
+            pltpu.SemaphoreType.DMA,
+            pltpu.SemaphoreType.DMA,
+        ],
+        flops=slots * 9 * 2 * order**3,
+        moved=slots * order * order * 6,
+    )(me, assign, due, cost, stats, *received, stale)
+
+
+def product_kernel(slot, me_ref, root_ref, factor_ref, *rest):
+    sum_in_ref = rest[0] if slot else None
+    pieces = rest[1 if slot else 0 :][:4]
+    outs = rest[-6:-2]
+    sum_ref, whole = rest[-2:]
+    me = me_ref[0]
+    width = pieces[0].shape[0]
+    for far in range(4):
+        whole[tile_at(me ^ far, width), :] = pieces[far][...]
+    total = sum_in_ref[...] if slot else jnp.zeros(sum_ref.shape, F32)
+    for far in (2, 3, 1, 0):
+        piece = jnp.dot(
+            root_ref[slot, tile_at(me ^ far, width), :], whole[...], preferred_element_type=F32
+        )
+        rounded = (piece * factor_ref[slot]).astype(BF16)
+        outs[far][...] = rounded
+        terms = rounded.astype(F32) * pieces[far][...].astype(F32)
+        for start in range(0, width, 8):
+            for column in range(0, terms.shape[1], 128):
+                total = total + terms[start : start + 8, column : column + 128]
+    sum_ref[...] = total
+
+
+def product(slot, me, root, factor, pieces, so_far):
+    width, columns = pieces[0].shape
+    order = root.shape[1]
+    before = [] if so_far is None else [so_far]
+    *rows, total = call(
+        functools.partial(product_kernel, slot),
+        (jax.ShapeDtypeStruct((width, columns), BF16),) * 4
+        + (jax.ShapeDtypeStruct((8, 128), F32),),
+        [IN_SMEM, IN_VMEM, IN_SMEM] + [IN_VMEM] * (len(before) + 4),
+        (IN_VMEM,) * 5,
+        "product",
+        scratch=[pltpu.VMEM((order, columns), BF16)],
+        flops=2 * order * order * columns,
+        moved=3 * order * order * 2,
+    )(me, root, factor, *before, *pieces)
+    return rows, total
+
+
+def clip_kernel(slots, elements, me_ref, assign_ref, *rest):
+    sums, rows, out_ref = rest[:4], rest[4:-1], rest[-1]
+    me = me_ref[0]
+    quadratic = jnp.sum(sums[0][...] + sums[1][...] + sums[2][...] + sums[3][...])
+    ratio = jnp.full((8, 128), F32(KL_BOUND * elements)) / quadratic
+    clip_factor = jnp.max(jnp.minimum(F32(1.0), jnp.sqrt(ratio)))
+    for slot in range(slots):
+        for far in range(4):
+            block = block_in_slot(assign_ref, (me ^ far) * slots + slot)
+            out_ref[0, block] = (clip_factor * rows[slot * 4 + far][...].astype(F32)).astype(BF16)
+
+
+def clip(me, assign, sums, rows, shape, slots, elements):
+    return call(
+        functools.partial(clip_kernel, slots, elements),
+        jax.ShapeDtypeStruct(shape, BF16),
+        [IN_SMEM, IN_SMEM] + [IN_VMEM] * (len(sums) + len(rows)),
+        IN_VMEM,
+        "clip",
+        moved=4 * shape[1] * shape[2] * shape[3],
+    )(me, assign, *sums, *rows)
+
+
+def partner_of(value, axis, far):
+    count = lax.axis_size(axis)
+    return lax.ppermute(value, axis, [(i, i ^ far) for i in range(count)])
+
+
+def sum_over(value, axis):
+    count = lax.axis_size(axis)
+    total = value
+    for shift in range(1, count):
+        total = total + lax.ppermute(
+            value, axis, [(i, (i + shift) % count) for i in range(count)]
+        )
+    return total
+
+
+def exchange_four(stats, grad, due, cost, assign, stale):
+    me = lax.axis_index("fsdp").astype(jnp.int32).reshape(1)
+    slots = assign.shape[1] // 4
+    near, far2, far3 = pack_stats(me, assign, stats, slots)
+    received = [None] * 3
+    received[1] = partner_of(far2, "fsdp", 2)
+    received[2] = partner_of(far3, "fsdp", 3)
+    received[0] = partner_of(near, "fsdp", 1)
+    sent = pack_grad(me, assign, grad, slots)
+    pieces = []
+    for slot in range(slots):
+        here = {0: sent[slot][0]}
+        for far in (3, 2, 1):
+            here[far] = partner_of(sent[slot][far], "fsdp", far)
+        pieces.append([here[far] for far in range(4)])
+    root, factor = roots(me, assign, due, cost, stats, received, stale, slots)
+    rows, total = [], None
+    for slot in range(slots):
+        solved, total = product(slot, me, root, factor, pieces[slot], total)
+        back = {0: solved[0]}
+        for far in (3, 2, 1):
+            back[far] = partner_of(solved[far], "fsdp", far)
+        rows += [back[far] for far in range(4)]
+    total = sum_over(total, "dp")
+    sums = [total] + [partner_of(total, "fsdp", far) for far in (1, 2, 3)]
+    elements = lax.axis_size("dp") * assign.shape[1] * stats.shape[3] * grad.shape[3]
+    return clip(me, assign, sums, rows, grad.shape, slots, elements)
 
 
 def solution(mesh):
     return jax.shard_map(
-        local,
+        exchange_four if mesh.shape["fsdp"] == 4 else exchange_all,
         mesh=mesh,
         in_specs=(
             P(("groups", "dp"), None, "fsdp", None),

time: 146 us -> 76.2 us (0.52)
  blocking collectives: 62.1 us -> 0 us
  starting transfers between devices: 15.1 us -> 41.2 us
  waiting for transfers between devices: 34.9 us -> 20.5 us
  Pallas kernels: 0 us -> 12.3 us
  other arithmetic: 10.2 us -> 0.01 us
  between operations: 9.75 us -> 0.1 us
  local copies, waits for them, and re-layouts: 11.3 us -> 1.99 us
  matrix products: 2.21 us -> 0 us
    ppermute x0 -> x21, starting transfers between devices: none -> 41.2 us  [the longest x18 39.1 us: partner_of(): return lax.ppermute(value, axis, [(i, i ^ far) for i in range(count)])]
    all_to_all x2 -> x0, waiting for transfers between devices: 34.9 us -> none  [the longest x1 23.8 us: local(): lax.all_to_all(solved.reshape(slot_count, solver_count, row_count, column...]
    all_to_all x1 -> x0, blocking collectives: 31.9 us -> none  [local(): lax.all_to_all(sent_stats, 'fsdp', split_axis=0, concat_axis=2, tiled=True)]
    psum x1 -> x0, blocking collectives: 30.1 us -> none  [local(): quadratic = lax.psum(local_part, ('fsdp', 'dp'))]
    ppermute x0 -> x21, waiting for transfers between devices: none -> 20.5 us  [the longest x18 19.6 us: partner_of(): return lax.ppermute(value, axis, [(i, i ^ far) for i in range(count)])]
    all_to_all x2 -> x0, starting transfers between devices: 15.1 us -> none  [the longest x1 10.8 us: local(): lax.all_to_all(solved.reshape(slot_count, solver_count, row_count, column...]
    pallas_call x0 -> x6, Pallas kernels: none -> 12.3 us  [the longest x1 5.5 us: roots(): call(functools.partial(root_kernel, slots), (jax.ShapeDtypeStruct((slots,...]
    all_to_all x2 -> x0, local copies, waits for them, and re-layouts: 3.82 us -> none  [the longest x1 2.32 us: local(): lax.all_to_all(sent_grad, 'fsdp', split_axis=0, concat_axis=2, tiled=True)]
  transfers between devices with their start and end apart: 2 -> 21, of which waited for: 2 -> 6; matrix products, arithmetic and copies ran while one was open for 3% -> 0% of each run, Pallas kernels for 0% -> 11%
where the time goes in v1:
time: 76.2 us; the launch traced here: 76.1 us
  starting transfers between devices  41.2 us (54%)
  waiting for transfers between devices  20.5 us (27%)
  Pallas kernels  12.3 us (16%)
  local copies, waits for them, and re-layouts  1.99 us (3%)
    ppermute x18, starting transfers between devices, partner_of(): return lax.ppermute(value, axis, [(i, i ^ far) for i in range(count)])  39.1 us
    ppermute x18, waiting for transfers between devices, partner_of(): return lax.ppermute(value, axis, [(i, i ^ far) for i in range(count)])  19.6 us
    pallas_call x1, Pallas kernels, roots(): call(functools.partial(root_kernel, slots), (jax.ShapeDtypeStruct((slots,...  5.5 us
    pallas_call x2, Pallas kernels, product(): call(functools.partial(product_kernel, slot), (jax.ShapeDtypeStruct((widt...  2.15 us
    ppermute x3, starting transfers between devices, sum_over(): lax.ppermute(value, axis, [(i, (i + shift) % count) for i in range(count)])  2.1 us
    pallas_call x1, Pallas kernels, pack_grad(): call(functools.partial(pack_grad_kernel, slots), (out,) * count, [IN_SMEM...  2.04 us
    unnamed x12, local copies, waits for them, and re-layouts  1.99 us
    pallas_call x1, Pallas kernels, clip(): call(functools.partial(clip_kernel, slots, elements), jax.ShapeDtypeStruc...  1.88 us
  transfers between devices with their start and end apart: 21, of which 6 were waited for; matrix products, arithmetic and copies ran while one was open for 0% of the time, Pallas kernels for 11%

profile of v1, /device:TPU:0, one launch (start us, length us, event | category | flops | bytes accessed | tf_op | source)
XLA Modules:
  0.0 76.1 jit_solution(5662718642728603222)
XLA Ops:
  0.0 1.3 %copy-done.1 = bf16[1,8,128,512]{3,2,1,0:T(8,128)(2,1)S(1)} copy-done((bf16[1,8,128,512]{3,2,1,0:T(8,128)(2,1)S(1)}, bf16[1,8,128,512]{3,2,1,0:T(8,128)(2,1)}, u32[]{:S(2)}) %copy-start.1) | copy-done | bytes 1048600
  1.3 0.7 copy-done.2
  2.0 0.7 pack_stats.1
  2.7 3.1 %collective-permute-start = (bf16[2,128,384]{2,1,0:T(8,128)(2,1)S(1)}, bf16[2,128,384]{2,1,0:T(8,128)(2,1)S(1)}, u32[]{:S(2)}, u32[]{:S(2)}) collective-permute-start(bf16[2,128,384]{2,1,0:T(8,128)(2,1)S(1)} %get-tuple-element.28), channel_id=1, source_target_pairs={{0,4},{4,0},{8,12},{12,8},{1,5},{5,1},{9,13},{13,9},{2,6},{6,2},{1... | collective-permute-start | bytes 589832 | tf_op jit(solution)/shard_map/ppermute | solution.py:411
  5.8 2.0 %pack_grad.1 = (bf16[128,512]{1,0:T(8,128)(2,1)S(1)}, bf16[128,512]{1,0:T(8,128)(2,1)S(1)}, bf16[128,512]{1,0:T(8,128)(2,1)S(1)}, bf16[128,512]{1,0:T(8,128)(2,1...) custom-call(s32[1]{0:T(128)} %bitcast.me_ref, ...), custom_call_target="tpu_custom_call" | custom-call | bytes 2097152 | tf_op jit(solution)/shard_map/pack_grad/pallas_call | solution.py:172
  7.8 0.1 collective-permute-start.3
  7.9 3.0 %collective-permute-start.1 = (bf16[2,192,128]{2,1,0:T(8,128)(2,1)S(1)}, bf16[2,192,128]{2,1,0:T(8,128)(2,1)S(1)}, u32[]{:S(2)}, u32[]{:S(2)}) collective-permute-start(bf16[2,192,128]{2,1,0:T(8,128)(2,1)S(1)} %get-tuple-element.29), channel_id=1, source_target_pairs={{0,8},{4,12},{8,0},{12,4},{1,9},{5,13},{9,1},{13,5},{2,10},{6,14},... | collective-permute-start | bytes 294920 | tf_op jit(solution)/shard_map/ppermute | solution.py:411
  11.0 1.3 %collective-permute-start.2 = (bf16[2,192,128]{2,1,0:T(8,128)(2,1)S(1)}, bf16[2,192,128]{2,1,0:T(8,128)(2,1)S(1)}, u32[]{:S(2)}, u32[]{:S(2)}) collective-permute-start(bf16[2,192,128]{2,1,0:T(8,128)(2,1)S(1)} %get-tuple-element.30), channel_id=1, source_target_pairs={{0,12},{4,8},{8,4},{12,0},{1,13},{5,9},{9,5},{13,1},{2,14},{6,10},... | collective-permute-start | bytes 294920 | tf_op jit(solution)/shard_map/ppermute | solution.py:411
  12.3 1.7 %collective-permute-start.4 = (bf16[128,512]{1,0:T(8,128)(2,1)S(1)}, bf16[128,512]{1,0:T(8,128)(2,1)S(1)}, u32[]{:S(2)}, u32[]{:S(2)}) collective-permute-start(bf16[128,512]{1,0:T(8,128)(2,1)S(1)} %get-tuple-element.35), channel_id=1, source_target_pairs={{0,8},{4,12},{8,0},{12,4},{1,9},{5,13},{9,1},{13,5},{2,10},{6,14},... | collective-permute-start | bytes 393224 | tf_op jit(solution)/shard_map/ppermute | solution.py:411
  14.0 2.1 %collective-permute-done.1.far2_ref = bf16[2,192,128]{2,1,0:T(8,128)(2,1)S(1)} collective-permute-done((bf16[2,192,128]{2,1,0:T(8,128)(2,1)S(1)}, bf16[2,192,128]{2,1,0:T(8,128)(2,1)S(1)}, u32[]{:S(2)}, u32[]{:S(2)}) %collective-permute-start.1) | collective-permute-done | bytes 98336 | tf_op jit(solution)/shard_map/ppermute | solution.py:411
  16.1 10.7 %collective-permute-start.5 = (bf16[128,512]{1,0:T(8,128)(2,1)S(1)}, bf16[128,512]{1,0:T(8,128)(2,1)S(1)}, u32[]{:S(2)}, u32[]{:S(2)}) collective-permute-start(bf16[128,512]{1,0:T(8,128)(2,1)S(1)} %get-tuple-element.36), channel_id=1, source_target_pairs={{0,12},{4,8},{8,4},{12,0},{1,13},{5,9},{9,5},{13,1},{2,14},{6,10},... | collective-permute-start | bytes 393224 | tf_op jit(solution)/shard_map/ppermute | solution.py:411
  26.8 0.0 collective-permute-done.2.far3_ref
  26.8 0.0 collective-permute-start.6
  26.8 0.0 collective-permute-done.3.rest_1_
  26.8 0.0 copy-start.4
  26.8 0.0 copy-start.5
  26.8 1.3 %collective-permute-start.7 = (bf16[128,512]{1,0:T(8,128)(2,1)S(1)}, bf16[128,512]{1,0:T(8,128)(2,1)S(1)}, u32[]{:S(2)}, u32[]{:S(2)}) collective-permute-start(bf16[128,512]{1,0:T(8,128)(2,1)S(1)} %get-tuple-element.40), channel_id=1, source_target_pairs={{0,8},{4,12},{8,0},{12,4},{1,9},{5,13},{9,1},{13,5},{2,10},{6,14},... | collective-permute-start | bytes 393224 | tf_op jit(solution)/shard_map/ppermute | solution.py:411
  28.1 0.0 collective-permute-done.near_ref
  28.1 3.1 %collective-permute-start.8 = (bf16[128,512]{1,0:T(8,128)(2,1)S(1)}, bf16[128,512]{1,0:T(8,128)(2,1)S(1)}, u32[]{:S(2)}, u32[]{:S(2)}) collective-permute-start(bf16[128,512]{1,0:T(8,128)(2,1)S(1)} %get-tuple-element.41), channel_id=1, source_target_pairs={{0,12},{4,8},{8,4},{12,0},{1,13},{5,9},{9,5},{13,1},{2,14},{6,10},... | collective-permute-start | bytes 393224 | tf_op jit(solution)/shard_map/ppermute | solution.py:411
  31.2 5.5 %roots.1 = (bf16[2,512,512]{2,1,0:T(8,128)(2,1)S(1)}, f32[2]{0:T(128)S(1)}) custom-call(s32[1]{0:T(128)} %bitcast.me_ref, s32[1,8]{1,0:T(1,128)S(1)} %copy-done.2, s32[1,8]{1,0:T(1,128)S(1)} %copy-done.4, s32[1,8]{1,0:T(1,128)S(1)} %copy-done.5, bf16[1,8,128,512]{3,2,1,0:T(8,128)(2,1)S(1)} %copy-done.1, ...), custom_call_target="tpu_custom_call" | custom-call | flops 4831838208 | bytes 3145728 | tf_op jit(solution)/shard_map/roots/pallas_call | solution.py:323
  36.7 0.0 collective-permute-done.4.rest_2_
  36.7 0.0 collective-permute-done.5.rest_3_
  36.7 1.1 %product.2 = (bf16[128,512]{1,0:T(8,128)(2,1)S(1)}, bf16[128,512]{1,0:T(8,128)(2,1)S(1)}, bf16[128,512]{1,0:T(8,128)(2,1)S(1)}, bf16[128,512]{1,0:T(8,128)(2,1)S(1)}, f32[8,128]{1,0:T(8,128)S(1)}) custom-call(s32[1]{0:T(128)} %bitcast.me_ref, bf16[2,512,512]{2,1,0:T(8,128)(2,1)S(1)} %get-tuple-element.31.root_ref, f32[2]{0:T(128)S(1)} %get-tuple-element.32.factor_ref, ...), custom_call_target="tpu_custom_call" | custom-call | flops 268435456 | bytes 1572864 | tf_op jit(solution)/shard_map/product/pallas_call | solution.py:372
  37.8 0.0 collective-permute-done.6.rest_2_
  37.8 3.2 %collective-permute-done.7.rest_3_ = bf16[128,512]{1,0:T(8,128)(2,1)S(1)} collective-permute-done((bf16[128,512]{1,0:T(8,128)(2,1)S(1)}, bf16[128,512]{1,0:T(8,128)(2,1)S(1)}, u32[]{:S(2)}, u32[]{:S(2)}) %collective-permute-start.7) | collective-permute-done | bytes 131104 | tf_op jit(solution)/shard_map/ppermute | solution.py:411
  40.9 1.1 %product.3 = (bf16[128,512]{1,0:T(8,128)(2,1)S(1)}, bf16[128,512]{1,0:T(8,128)(2,1)S(1)}, bf16[128,512]{1,0:T(8,128)(2,1)S(1)}, bf16[128,512]{1,0:T(8,128)(2,1)S(1)}, f32[8,128]{1,0:T(8,128)S(1)}) custom-call(s32[1]{0:T(128)} %bitcast.me_ref, bf16[2,512,512]{2,1,0:T(8,128)(2,1)S(1)} %get-tuple-element.31.root_ref, f32[2]{0:T(128)S(1)} %get-tuple-element.32.factor_ref, ...), custom_call_target="tpu_custom_call" | custom-call | flops 268435456 | bytes 1572864 | tf_op jit(solution)/shard_map/product/pallas_call | solution.py:372
  42.0 0.1 collective-permute-start.11
  42.1 1.9 %collective-permute-start.10 = (f32[8,128]{1,0:T(8,128)S(1)}, f32[8,128]{1,0:T(8,128)S(1)}, u32[]{:S(2)}, u32[]{:S(2)}) collective-permute-start(f32[8,128]{1,0:T(8,128)S(1)} %get-tuple-element.42), channel_id=1, source_target_pairs={{0,2},{1,3},{2,0},{3,1},{4,6},{5,7},{6,4},{7,5},{8,10},{9,11},{10,... | collective-permute-start | bytes 12296 | tf_op jit(solution)/shard_map/ppermute | solution.py:418
  44.0 0.2 collective-permute-start.9
  44.1 2.0 %collective-permute-start.15 = (bf16[128,512]{1,0:T(8,128)(2,1)S(1)}, bf16[128,512]{1,0:T(8,128)(2,1)S(1)}, u32[]{:S(2)}, u32[]{:S(2)}) collective-permute-start(bf16[128,512]{1,0:T(8,128)(2,1)S(1)} %get-tuple-element.44), channel_id=1, source_target_pairs={{0,4},{4,0},{8,12},{12,8},{1,5},{5,1},{9,13},{13,9},{2,6},{6,2},{1... | collective-permute-start | bytes 393224 | tf_op jit(solution)/shard_map/ppermute | solution.py:411
  46.1 0.9 %collective-permute-done.9 = f32[8,128]{1,0:T(8,128)S(1)} collective-permute-done((f32[8,128]{1,0:T(8,128)S(1)}, f32[8,128]{1,0:T(8,128)S(1)}, u32[]{:S(2)}, u32[]{:S(2)}) %collective-permute-start.9) | collective-permute-done | bytes 4128 | tf_op jit(solution)/shard_map/ppermute | solution.py:418
  47.0 3.0 %collective-permute-start.14 = (f32[8,128]{1,0:T(8,128)S(1)}, f32[8,128]{1,0:T(8,128)S(1)}, u32[]{:S(2)}, u32[]{:S(2)}) collective-permute-start(f32[8,128]{1,0:T(8,128)S(1)} %add_add_fusion.rest_0_), channel_id=1, source_target_pairs={{0,12},{4,8},{8,4},{12,0},{1,13},{5,9},{9,5},{13,1},{2,14},{6,10},... | collective-permute-start | bytes 12296 | tf_op jit(solution)/shard_map/ppermute | solution.py:411
  50.0 0.6 collective-permute-start.13
  50.6 0.8 %collective-permute-start.12 = (f32[8,128]{1,0:T(8,128)S(1)}, f32[8,128]{1,0:T(8,128)S(1)}, u32[]{:S(2)}, u32[]{:S(2)}) collective-permute-start(f32[8,128]{1,0:T(8,128)S(1)} %add_add_fusion.rest_0_), channel_id=1, source_target_pairs={{0,4},{4,0},{8,12},{12,8},{1,5},{5,1},{9,13},{13,9},{2,6},{6,2},{1... | collective-permute-start | bytes 12296 | tf_op jit(solution)/shard_map/ppermute | solution.py:411
  51.4 2.6 %collective-permute-start.16 = (bf16[128,512]{1,0:T(8,128)(2,1)S(1)}, bf16[128,512]{1,0:T(8,128)(2,1)S(1)}, u32[]{:S(2)}, u32[]{:S(2)}) collective-permute-start(bf16[128,512]{1,0:T(8,128)(2,1)S(1)} %get-tuple-element.45), channel_id=1, source_target_pairs={{0,8},{4,12},{8,0},{12,4},{1,9},{5,13},{9,1},{13,5},{2,10},{6,14},... | collective-permute-start | bytes 393224 | tf_op jit(solution)/shard_map/ppermute | solution.py:411
  54.0 0.0 collective-permute-done.14.rest_3_
  54.0 1.4 %collective-permute-start.17 = (bf16[128,512]{1,0:T(8,128)(2,1)S(1)}, bf16[128,512]{1,0:T(8,128)(2,1)S(1)}, u32[]{:S(2)}, u32[]{:S(2)}) collective-permute-start(bf16[128,512]{1,0:T(8,128)(2,1)S(1)} %get-tuple-element.46), channel_id=1, source_target_pairs={{0,12},{4,8},{8,4},{12,0},{1,13},{5,9},{9,5},{13,1},{2,14},{6,10},... | collective-permute-start | bytes 393224 | tf_op jit(solution)/shard_map/ppermute | solution.py:411
  55.4 0.1 collective-permute-done.13.rest_2_
  55.6 0.2 collective-permute-start.18
  55.7 2.7 %collective-permute-start.19 = (bf16[128,512]{1,0:T(8,128)(2,1)S(1)}, bf16[128,512]{1,0:T(8,128)(2,1)S(1)}, u32[]{:S(2)}, u32[]{:S(2)}) collective-permute-start(bf16[128,512]{1,0:T(8,128)(2,1)S(1)} %get-tuple-element.49), channel_id=1, source_target_pairs={{0,8},{4,12},{8,0},{12,4},{1,9},{5,13},{9,1},{13,5},{2,10},{6,14},... | collective-permute-start | bytes 393224 | tf_op jit(solution)/shard_map/ppermute | solution.py:411
  58.4 0.0 collective-permute-done.15.rest_5_
  58.4 1.5 %collective-permute-start.20 = (bf16[128,512]{1,0:T(8,128)(2,1)S(1)}, bf16[128,512]{1,0:T(8,128)(2,1)S(1)}, u32[]{:S(2)}, u32[]{:S(2)}) collective-permute-start(bf16[128,512]{1,0:T(8,128)(2,1)S(1)} %get-tuple-element.50), channel_id=1, source_target_pairs={{0,12},{4,8},{8,4},{12,0},{1,13},{5,9},{9,5},{13,1},{2,14},{6,10},... | collective-permute-start | bytes 393224 | tf_op jit(solution)/shard_map/ppermute | solution.py:411
  60.0 3.8 %collective-permute-done.16.rest_6_ = bf16[128,512]{1,0:T(8,128)(2,1)S(1)} collective-permute-done((bf16[128,512]{1,0:T(8,128)(2,1)S(1)}, bf16[128,512]{1,0:T(8,128)(2,1)S(1)}, u32[]{:S(2)}, u32[]{:S(2)}) %collective-permute-start.16) | collective-permute-done | bytes 131104 | tf_op jit(solution)/shard_map/ppermute | solution.py:411
  63.7 0.0 collective-permute-done.17.rest_7_
  63.7 0.0 collective-permute-done.18.rest_9_
  63.8 10.4 %collective-permute-done.19.rest_10_ = bf16[128,512]{1,0:T(8,128)(2,1)S(1)} collective-permute-done((bf16[128,512]{1,0:T(8,128)(2,1)S(1)}, bf16[128,512]{1,0:T(8,128)(2,1)S(1)}, u32[]{:S(2)}, u32[]{:S(2)}) %collective-permute-start.19) | collective-permute-done | bytes 131104 | tf_op jit(solution)/shard_map/ppermute | solution.py:411
  74.2 0.0 collective-permute-done.20.rest_11_
  74.2 1.9 %clip.1 = bf16[1,8,128,512]{3,2,1,0:T(8,128)(2,1)} custom-call(s32[1]{0:T(128)} %bitcast.me_ref, s32[1,8]{1,0:T(1,128)S(1)} %copy-done.2, f32[8,128]{1,0:T(8,128)S(1)} %add_add_fusion.rest_0_, f32[8,128]{1,0:T(8,128)S(1)} %collective-permute-done.12.rest_1_, f32[8,128]{1,0:T(8,128)S(1)} %collective-permute-done.13.rest_2_, ...), custom_call_target="tpu_custom_call" | custom-call | bytes 2097152 | tf_op jit(solution)/shard_map/clip/pallas_call | solution.py:399
  (13 shorter events, 0.0 us)
Async XLA Ops:
  0.0 5.8 %copy-start = (bf16[1,8,128,512]{3,2,1,0:T(8,128)(2,1)S(1)}, bf16[1,8,128,512]{3,2,1,0:T(8,128)(2,1)}, u32[]{:S(2)}) copy-start(bf16[1,8,128,512]{3,2,1,0:T(8,128)(2,1)} %grad_ref.1) | copy-start | bytes 3145732
  0.0 1.3 %copy-start.1 = (bf16[1,8,128,512]{3,2,1,0:T(8,128)(2,1)S(1)}, bf16[1,8,128,512]{3,2,1,0:T(8,128)(2,1)}, u32[]{:S(2)}) copy-start(bf16[1,8,128,512]{3,2,1,0:T(8,128)(2,1)} %stats_ref.3) | copy-start | bytes 3145732
  1.3 0.7 copy-start.2
  2.0 29.2 %copy-start.3 = (bf16[1,2,512,512]{3,2,1,0:T(8,128)(2,1)S(1)}, bf16[1,2,512,512]{3,2,1,0:T(8,128)(2,1)}, u32[]{:S(2)}) copy-start(bf16[1,2,512,512]{3,2,1,0:T(8,128)(2,1)} %stale_ref.1) | copy-start | bytes 3145732
  2.7 25.3 %collective-permute-start = (bf16[2,128,384]{2,1,0:T(8,128)(2,1)S(1)}, bf16[2,128,384]{2,1,0:T(8,128)(2,1)S(1)}, u32[]{:S(2)}, u32[]{:S(2)}) collective-permute-start(bf16[2,128,384]{2,1,0:T(8,128)(2,1)S(1)} %get-tuple-element.28), channel_id=1, source_target_pairs={{0,4},{4,0},{8,12},{12,8},{1,5},{5,1},{9,13},{13,9},{2,6},{6,2},{1... | collective-permute-start | bytes 589832 | tf_op jit(solution)/shard_map/ppermute | solution.py:411
  7.8 18.9 %collective-permute-start.3 = (bf16[128,512]{1,0:T(8,128)(2,1)S(1)}, bf16[128,512]{1,0:T(8,128)(2,1)S(1)}, u32[]{:S(2)}, u32[]{:S(2)}) collective-permute-start(bf16[128,512]{1,0:T(8,128)(2,1)S(1)} %get-tuple-element.34), channel_id=1, source_target_pairs={{0,4},{4,0},{8,12},{12,8},{1,5},{5,1},{9,13},{13,9},{2,6},{6,2},{1... | collective-permute-start | bytes 393224 | tf_op jit(solution)/shard_map/ppermute | solution.py:411
  7.9 8.1 %collective-permute-start.1 = (bf16[2,192,128]{2,1,0:T(8,128)(2,1)S(1)}, bf16[2,192,128]{2,1,0:T(8,128)(2,1)S(1)}, u32[]{:S(2)}, u32[]{:S(2)}) collective-permute-start(bf16[2,192,128]{2,1,0:T(8,128)(2,1)S(1)} %get-tuple-element.29), channel_id=1, source_target_pairs={{0,8},{4,12},{8,0},{12,4},{1,9},{5,13},{9,1},{13,5},{2,10},{6,14},... | collective-permute-start | bytes 294920 | tf_op jit(solution)/shard_map/ppermute | solution.py:411
  11.0 15.8 %collective-permute-start.2 = (bf16[2,192,128]{2,1,0:T(8,128)(2,1)S(1)}, bf16[2,192,128]{2,1,0:T(8,128)(2,1)S(1)}, u32[]{:S(2)}, u32[]{:S(2)}) collective-permute-start(bf16[2,192,128]{2,1,0:T(8,128)(2,1)S(1)} %get-tuple-element.30), channel_id=1, source_target_pairs={{0,12},{4,8},{8,4},{12,0},{1,13},{5,9},{9,5},{13,1},{2,14},{6,10},... | collective-permute-start | bytes 294920 | tf_op jit(solution)/shard_map/ppermute | solution.py:411
  12.3 24.4 %collective-permute-start.4 = (bf16[128,512]{1,0:T(8,128)(2,1)S(1)}, bf16[128,512]{1,0:T(8,128)(2,1)S(1)}, u32[]{:S(2)}, u32[]{:S(2)}) collective-permute-start(bf16[128,512]{1,0:T(8,128)(2,1)S(1)} %get-tuple-element.35), channel_id=1, source_target_pairs={{0,8},{4,12},{8,0},{12,4},{1,9},{5,13},{9,1},{13,5},{2,10},{6,14},... | collective-permute-start | bytes 393224 | tf_op jit(solution)/shard_map/ppermute | solution.py:411
  16.1 20.6 %collective-permute-start.5 = (bf16[128,512]{1,0:T(8,128)(2,1)S(1)}, bf16[128,512]{1,0:T(8,128)(2,1)S(1)}, u32[]{:S(2)}, u32[]{:S(2)}) collective-permute-start(bf16[128,512]{1,0:T(8,128)(2,1)S(1)} %get-tuple-element.36), channel_id=1, source_target_pairs={{0,12},{4,8},{8,4},{12,0},{1,13},{5,9},{9,5},{13,1},{2,14},{6,10},... | collective-permute-start | bytes 393224 | tf_op jit(solution)/shard_map/ppermute | solution.py:411
  26.8 11.0 %collective-permute-start.6 = (bf16[128,512]{1,0:T(8,128)(2,1)S(1)}, bf16[128,512]{1,0:T(8,128)(2,1)S(1)}, u32[]{:S(2)}, u32[]{:S(2)}) collective-permute-start(bf16[128,512]{1,0:T(8,128)(2,1)S(1)} %get-tuple-element.39), channel_id=1, source_target_pairs={{0,4},{4,0},{8,12},{12,8},{1,5},{5,1},{9,13},{13,9},{2,6},{6,2},{1... | collective-permute-start | bytes 393224 | tf_op jit(solution)/shard_map/ppermute | solution.py:411
  26.8 4.4 %copy-start.4 = (s32[1,8]{1,0:T(1,128)S(1)}, s32[1,8]{1,0:T(1,128)}, u32[]{:S(2)}) copy-start(s32[1,8]{1,0:T(1,128)} %due_ref.1) | copy-start | bytes 100
  26.8 4.4 %copy-start.5 = (s32[1,8]{1,0:T(1,128)S(1)}, s32[1,8]{1,0:T(1,128)}, u32[]{:S(2)}) copy-start(s32[1,8]{1,0:T(1,128)} %cost_ref.1) | copy-start | bytes 100
  26.8 14.1 %collective-permute-start.7 = (bf16[128,512]{1,0:T(8,128)(2,1)S(1)}, bf16[128,512]{1,0:T(8,128)(2,1)S(1)}, u32[]{:S(2)}, u32[]{:S(2)}) collective-permute-start(bf16[128,512]{1,0:T(8,128)(2,1)S(1)} %get-tuple-element.40), channel_id=1, source_target_pairs={{0,8},{4,12},{8,0},{12,4},{1,9},{5,13},{9,1},{13,5},{2,10},{6,14},... | collective-permute-start | bytes 393224 | tf_op jit(solution)/shard_map/ppermute | solution.py:411
  28.1 12.9 %collective-permute-start.8 = (bf16[128,512]{1,0:T(8,128)(2,1)S(1)}, bf16[128,512]{1,0:T(8,128)(2,1)S(1)}, u32[]{:S(2)}, u32[]{:S(2)}) collective-permute-start(bf16[128,512]{1,0:T(8,128)(2,1)S(1)} %get-tuple-element.41), channel_id=1, source_target_pairs={{0,12},{4,8},{8,4},{12,0},{1,13},{5,9},{9,5},{13,1},{2,14},{6,10},... | collective-permute-start | bytes 393224 | tf_op jit(solution)/shard_map/ppermute | solution.py:411
  42.0 4.1 %collective-permute-start.11 = (f32[8,128]{1,0:T(8,128)S(1)}, f32[8,128]{1,0:T(8,128)S(1)}, u32[]{:S(2)}, u32[]{:S(2)}) collective-permute-start(f32[8,128]{1,0:T(8,128)S(1)} %get-tuple-element.42), channel_id=1, source_target_pairs={{0,3},{1,0},{2,1},{3,2},{4,7},{5,4},{6,5},{7,6},{8,11},{9,8},{10,9... | collective-permute-start | bytes 12296 | tf_op jit(solution)/shard_map/ppermute | solution.py:418
  42.1 4.0 %collective-permute-start.10 = (f32[8,128]{1,0:T(8,128)S(1)}, f32[8,128]{1,0:T(8,128)S(1)}, u32[]{:S(2)}, u32[]{:S(2)}) collective-permute-start(f32[8,128]{1,0:T(8,128)S(1)} %get-tuple-element.42), channel_id=1, source_target_pairs={{0,2},{1,3},{2,0},{3,1},{4,6},{5,7},{6,4},{7,5},{8,10},{9,11},{10,... | collective-permute-start | bytes 12296 | tf_op jit(solution)/shard_map/ppermute | solution.py:418
  44.0 3.0 %collective-permute-start.9 = (f32[8,128]{1,0:T(8,128)S(1)}, f32[8,128]{1,0:T(8,128)S(1)}, u32[]{:S(2)}, u32[]{:S(2)}) collective-permute-start(f32[8,128]{1,0:T(8,128)S(1)} %get-tuple-element.42), channel_id=1, source_target_pairs={{0,1},{1,2},{2,3},{3,0},{4,5},{5,6},{6,7},{7,4},{8,9},{9,10},{10,1... | collective-permute-start | bytes 12296 | tf_op jit(solution)/shard_map/ppermute | solution.py:418
  44.1 14.3 %collective-permute-start.15 = (bf16[128,512]{1,0:T(8,128)(2,1)S(1)}, bf16[128,512]{1,0:T(8,128)(2,1)S(1)}, u32[]{:S(2)}, u32[]{:S(2)}) collective-permute-start(bf16[128,512]{1,0:T(8,128)(2,1)S(1)} %get-tuple-element.44), channel_id=1, source_target_pairs={{0,4},{4,0},{8,12},{12,8},{1,5},{5,1},{9,13},{13,9},{2,6},{6,2},{1... | collective-permute-start | bytes 393224 | tf_op jit(solution)/shard_map/ppermute | solution.py:411
  47.0 7.0 %collective-permute-start.14 = (f32[8,128]{1,0:T(8,128)S(1)}, f32[8,128]{1,0:T(8,128)S(1)}, u32[]{:S(2)}, u32[]{:S(2)}) collective-permute-start(f32[8,128]{1,0:T(8,128)S(1)} %add_add_fusion.rest_0_), channel_id=1, source_target_pairs={{0,12},{4,8},{8,4},{12,0},{1,13},{5,9},{9,5},{13,1},{2,14},{6,10},... | collective-permute-start | bytes 12296 | tf_op jit(solution)/shard_map/ppermute | solution.py:411
  50.0 5.5 %collective-permute-start.13 = (f32[8,128]{1,0:T(8,128)S(1)}, f32[8,128]{1,0:T(8,128)S(1)}, u32[]{:S(2)}, u32[]{:S(2)}) collective-permute-start(f32[8,128]{1,0:T(8,128)S(1)} %add_add_fusion.rest_0_), channel_id=1, source_target_pairs={{0,8},{4,12},{8,0},{12,4},{1,9},{5,13},{9,1},{13,5},{2,10},{6,14},... | collective-permute-start | bytes 12296 | tf_op jit(solution)/shard_map/ppermute | solution.py:411
  50.6 5.1 %collective-permute-start.12 = (f32[8,128]{1,0:T(8,128)S(1)}, f32[8,128]{1,0:T(8,128)S(1)}, u32[]{:S(2)}, u32[]{:S(2)}) collective-permute-start(f32[8,128]{1,0:T(8,128)S(1)} %add_add_fusion.rest_0_), channel_id=1, source_target_pairs={{0,4},{4,0},{8,12},{12,8},{1,5},{5,1},{9,13},{13,9},{2,6},{6,2},{1... | collective-permute-start | bytes 12296 | tf_op jit(solution)/shard_map/ppermute | solution.py:411
  51.4 12.4 %collective-permute-start.16 = (bf16[128,512]{1,0:T(8,128)(2,1)S(1)}, bf16[128,512]{1,0:T(8,128)(2,1)S(1)}, u32[]{:S(2)}, u32[]{:S(2)}) collective-permute-start(bf16[128,512]{1,0:T(8,128)(2,1)S(1)} %get-tuple-element.45), channel_id=1, source_target_pairs={{0,8},{4,12},{8,0},{12,4},{1,9},{5,13},{9,1},{13,5},{2,10},{6,14},... | collective-permute-start | bytes 393224 | tf_op jit(solution)/shard_map/ppermute | solution.py:411
  54.0 9.7 %collective-permute-start.17 = (bf16[128,512]{1,0:T(8,128)(2,1)S(1)}, bf16[128,512]{1,0:T(8,128)(2,1)S(1)}, u32[]{:S(2)}, u32[]{:S(2)}) collective-permute-start(bf16[128,512]{1,0:T(8,128)(2,1)S(1)} %get-tuple-element.46), channel_id=1, source_target_pairs={{0,12},{4,8},{8,4},{12,0},{1,13},{5,9},{9,5},{13,1},{2,14},{6,10},... | collective-permute-start | bytes 393224 | tf_op jit(solution)/shard_map/ppermute | solution.py:411
  55.6 8.2 %collective-permute-start.18 = (bf16[128,512]{1,0:T(8,128)(2,1)S(1)}, bf16[128,512]{1,0:T(8,128)(2,1)S(1)}, u32[]{:S(2)}, u32[]{:S(2)}) collective-permute-start(bf16[128,512]{1,0:T(8,128)(2,1)S(1)} %get-tuple-element.48), channel_id=1, source_target_pairs={{0,4},{4,0},{8,12},{12,8},{1,5},{5,1},{9,13},{13,9},{2,6},{6,2},{1... | collective-permute-start | bytes 393224 | tf_op jit(solution)/shard_map/ppermute | solution.py:411
  55.7 18.4 %collective-permute-start.19 = (bf16[128,512]{1,0:T(8,128)(2,1)S(1)}, bf16[128,512]{1,0:T(8,128)(2,1)S(1)}, u32[]{:S(2)}, u32[]{:S(2)}) collective-permute-start(bf16[128,512]{1,0:T(8,128)(2,1)S(1)} %get-tuple-element.49), channel_id=1, source_target_pairs={{0,8},{4,12},{8,0},{12,4},{1,9},{5,13},{9,1},{13,5},{2,10},{6,14},... | collective-permute-start | bytes 393224 | tf_op jit(solution)/shard_map/ppermute | solution.py:411
  58.4 15.7 %collective-permute-start.20 = (bf16[128,512]{1,0:T(8,128)(2,1)S(1)}, bf16[128,512]{1,0:T(8,128)(2,1)S(1)}, u32[]{:S(2)}, u32[]{:S(2)}) collective-permute-start(bf16[128,512]{1,0:T(8,128)(2,1)S(1)} %get-tuple-element.50), channel_id=1, source_target_pairs={{0,12},{4,8},{8,4},{12,0},{1,13},{5,9},{9,5},{13,1},{2,14},{6,10},... | collective-permute-start | bytes 393224 | tf_op jit(solution)/shard_map/ppermute | solution.py:411

commit v2 on v1

--- a/solution.py
+++ b/solution.py
@@ -9,6 +9,7 @@
 
 KL_BOUND = 1.0
 VMEM_BYTES = 40 * 2**20
+DIAGONAL_ROWS = 16
 F32 = jnp.float32
 BF16 = jnp.bfloat16
 
@@ -116,19 +117,53 @@
     return pl.ds(pl.multiple_of(index * width, width), width)
 
 
-def pack_stats_kernel(slots, me_ref, assign_ref, stats_ref, near_ref, far2_ref, far3_ref):
+def fold(tile):
+    half = tile.shape[0] // 2
+    row = lax.broadcasted_iota(jnp.int32, (half, 2 * half), 0)
+    lane = lax.broadcasted_iota(jnp.int32, (half, 2 * half), 1)
+    top, bottom = tile[:half, :], tile[half:, :]
+    folded = jnp.where((lane < half) & (row > lane), pltpu.roll(bottom, half, 1), top)
+    diagonal = jnp.sum(jnp.where(lane - half == row, bottom, 0.0), axis=0, keepdims=True)
+    return folded, diagonal
+
+
+def unfold(folded, diagonal):
+    half = folded.shape[0]
+    row = lax.broadcasted_iota(jnp.int32, (half, 2 * half), 0)
+    lane = lax.broadcasted_iota(jnp.int32, (half, 2 * half), 1)
+    turned = jnp.concatenate([folded, jnp.zeros_like(folded)], axis=0).T
+    top = jnp.where((lane < half) & (row > lane), turned[:half, :], folded)
+    last = jnp.where(
+        lane - half < row,
+        pltpu.roll(folded, half, 1),
+        jnp.where(lane - half > row, pltpu.roll(turned[:half, :], half, 1), diagonal),
+    )
+    return jnp.concatenate([top, jnp.where(lane < half, turned[half:, :], last)], axis=0)
+
+
+def pack_stats_kernel(
+    slots, me_ref, assign_hbm, stats_hbm, near_ref, far2_ref, far3_ref, assign_ref, stats_ref, sems
+):
+    table = pltpu.make_async_copy(assign_hbm, assign_ref, sems.at[0])
+    table.start()
+    blocks = pltpu.make_async_copy(stats_hbm, stats_ref, sems.at[1])
+    blocks.start()
     me = me_ref[0]
     width = stats_ref.shape[2]
     half = width // 2
     odd = me % 2
+    table.wait()
+    blocks.wait()
     for slot in range(slots):
         for far, out in ((2, far2_ref), (3, far3_ref)):
             block = block_in_slot(assign_ref, (me ^ far) * slots + slot)
-            out[slot, :width, :] = stats_ref[0, block, :, tile_at(me, width)]
             between = stats_ref[0, block, :, tile_at(me ^ 1, width)].astype(F32)
-            out[slot, width:, :] = jnp.where(
-                odd == 1, between.T[half:, :], between[:half, :]
-            ).astype(BF16)
+            out[slot, :half, :] = jnp.where(odd == 1, between.T[half:, :], between[:half, :]).astype(
+                BF16
+            )
+            folded, diagonal = fold(stats_ref[0, block, :, tile_at(me, width)].astype(F32))
+            out[slot, half:width, :] = folded.astype(BF16)
+            out[slot, width:, :] = jnp.broadcast_to(diagonal, (DIAGONAL_ROWS, width)).astype(BF16)
     for slot in range(slots):
         block = block_in_slot(assign_ref, (me ^ 1) * slots + slot)
         for place, other in enumerate((0, 2, 3)):
@@ -140,45 +175,40 @@
 def pack_stats(me, assign, stats, slots):
     width, order = stats.shape[2:]
     near = jax.ShapeDtypeStruct((slots, width, order - width), BF16)
-    far = jax.ShapeDtypeStruct((slots, width + width // 2, width), BF16)
+    far = jax.ShapeDtypeStruct((slots, width + DIAGONAL_ROWS, width), BF16)
     return call(
         functools.partial(pack_stats_kernel, slots),
         (near, far, far),
+        [IN_SMEM, ANYWHERE, ANYWHERE],
+        (IN_VMEM,) * 3,
+        "pack_stats",
+        scratch=[
+            pltpu.SMEM(assign.shape, jnp.int32),
+            pltpu.VMEM(stats.shape, BF16),
+            pltpu.SemaphoreType.DMA((2,)),
+        ],
+        moved=2 * stats.size * 2,
+    )(me, assign, stats)
+
+
+def pack_grad_kernel(slots, me_ref, assign_ref, grad_ref, *outs):
+    me = me_ref[0]
+    for far in (3, 2, 1):
+        for slot in range(slots):
+            block = block_in_slot(assign_ref, (me ^ far) * slots + slot)
+            outs[far - 1][slot] = grad_ref[0, block]
+
+
+def pack_grad(me, assign, grad, slots):
+    out = jax.ShapeDtypeStruct((slots, *grad.shape[2:]), BF16)
+    return call(
+        functools.partial(pack_grad_kernel, slots),
+        (out,) * 3,
         [IN_SMEM, IN_SMEM, IN_VMEM],
         (IN_VMEM,) * 3,
-        "pack_stats",
-        moved=2 * stats.size * 2,
-    )(me, assign, stats)
-
-
-def pack_grad_kernel(slots, me_ref, assign_ref, grad_ref, *rest):
-    outs, sems = rest[:-1], rest[-1]
-    me = me_ref[0]
-    copies = []
-    for slot in range(slots):
-        for far in range(4):
-            at = slot * 4 + far
-            block = block_in_slot(assign_ref, (me ^ far) * slots + slot)
-            copy = pltpu.make_async_copy(grad_ref.at[0, block], outs[at], sems.at[at])
-            copy.start()
-            copies.append(copy)
-    for copy in copies:
-        copy.wait()
-
-
-def pack_grad(me, assign, grad, slots):
-    out = jax.ShapeDtypeStruct(grad.shape[2:], BF16)
-    count = 4 * slots
-    flat = call(
-        functools.partial(pack_grad_kernel, slots),
-        (out,) * count,
-        [IN_SMEM, IN_SMEM, ANYWHERE],
-        (ANYWHERE,) * count,
         "pack_grad",
-        scratch=[pltpu.SemaphoreType.DMA((count,))],
         moved=2 * grad.size * 2,
     )(me, assign, grad)
-    return [flat[slot * 4 : slot * 4 + 4] for slot in range(slots)]
 
 
 def root_kernel(
@@ -219,10 +249,13 @@
         even, odd = (me ^ 2) & 2, ((me ^ 2) & 2) + 1
         at = lambda index: tile_at(index, width)
         two, three = me ^ 2, me ^ 3
-        full[at(two), at(two)] = far2_ref[slot, :width, :].astype(F32)
-        full[at(three), at(three)] = far3_ref[slot, :width, :].astype(F32)
-        from_two = far2_ref[slot, width:, :].astype(F32)
-        from_three = far3_ref[slot, width:, :].astype(F32)
+        for index, far_ref in ((two, far2_ref), (three, far3_ref)):
+            full[at(index), at(index)] = unfold(
+                far_ref[slot, half:width, :].astype(F32),
+                far_ref[slot, width : width + 1, :].astype(F32),
+            )
+        from_two = far2_ref[slot, :half, :].astype(F32)
+        from_three = far3_ref[slot, :half, :].astype(F32)
         two_is_even = me % 2 == 0
         between = jnp.concatenate(
             [
@@ -342,57 +375,103 @@
     )(me, assign, due, cost, stats, *received, stale)
 
 
-def product_kernel(slot, me_ref, root_ref, factor_ref, *rest):
-    sum_in_ref = rest[0] if slot else None
-    pieces = rest[1 if slot else 0 :][:4]
-    outs = rest[-6:-2]
-    sum_ref, whole = rest[-2:]
-    me = me_ref[0]
-    width = pieces[0].shape[0]
-    for far in range(4):
-        whole[tile_at(me ^ far, width), :] = pieces[far][...]
-    total = sum_in_ref[...] if slot else jnp.zeros(sum_ref.shape, F32)
-    for far in (2, 3, 1, 0):
-        piece = jnp.dot(
-            root_ref[slot, tile_at(me ^ far, width), :], whole[...], preferred_element_type=F32
-        )
+def pair_product(slots, pair, odd, root_ref, factor_ref, whole_ref, first_ref, second_ref, sum_ref):
+    rows, columns = first_ref.shape[1:]
+    at = tile_at(pair, 2 * rows)
+    total = jnp.zeros(sum_ref.shape, F32)
+    for slot in range(slots):
+        piece = jnp.dot(root_ref[slot, at, :], whole_ref[slot], preferred_element_type=F32)
         rounded = (piece * factor_ref[slot]).astype(BF16)
-        outs[far][...] = rounded
-        terms = rounded.astype(F32) * pieces[far][...].astype(F32)
-        for start in range(0, width, 8):
-            for column in range(0, terms.shape[1], 128):
+        low, high = rounded[:rows, :], rounded[rows:, :]
+        first_ref[slot] = jnp.where(odd, high, low)
+        second_ref[slot] = jnp.where(odd, low, high)
+        terms = rounded.astype(F32) * whole_ref[slot, at, :].astype(F32)
+        for start in range(0, 2 * rows, 8):
+            for column in range(0, columns, 128):
                 total = total + terms[start : start + 8, column : column + 128]
     sum_ref[...] = total
 
 
-def product(slot, me, root, factor, pieces, so_far):
-    width, columns = pieces[0].shape
+def far_kernel(
+    slots,
+    me_ref,
+    assign_ref,
+    root_ref,
+    factor_ref,
+    grad_ref,
+    near_ref,
+    far2_ref,
+    far3_ref,
+    out2_ref,
+    out3_ref,
+    sum_ref,
+    whole_ref,
+):
+    me = me_ref[0]
+    rows = near_ref.shape[1]
+    for slot in range(slots):
+        block = block_in_slot(assign_ref, me * slots + slot)
+        whole_ref[slot, tile_at(me, rows), :] = grad_ref[0, block]
+        for far, piece_ref in ((1, near_ref), (2, far2_ref), (3, far3_ref)):
+            whole_ref[slot, tile_at(me ^ far, rows), :] = piece_ref[slot]
+    pair_product(
+        slots, 1 - me // 2, me % 2 == 1, root_ref, factor_ref, whole_ref, out2_ref, out3_ref, sum_ref
+    )
+
+
+def near_kernel(
+    slots, me_ref, root_ref, factor_ref, whole_ref, far_sum_ref, own_ref, out1_ref, sum_ref
+):
+    me = me_ref[0]
+    pair_product(
+        slots, me // 2, me % 2 == 1, root_ref, factor_ref, whole_ref, own_ref, out1_ref, sum_ref
+    )
+    sum_ref[...] += far_sum_ref[...]
+
+
+def products(slots, me, assign, root, factor, grad, pieces):
+    rows, columns = pieces[0].shape[1:]
     order = root.shape[1]
-    before = [] if so_far is None else [so_far]
-    *rows, total = call(
-        functools.partial(product_kernel, slot),
-        (jax.ShapeDtypeStruct((width, columns), BF16),) * 4
-        + (jax.ShapeDtypeStruct((8, 128), F32),),
-        [IN_SMEM, IN_VMEM, IN_SMEM] + [IN_VMEM] * (len(before) + 4),
-        (IN_VMEM,) * 5,
-        "product",
-        scratch=[pltpu.VMEM((order, columns), BF16)],
-        flops=2 * order * order * columns,
-        moved=3 * order * order * 2,
-    )(me, root, factor, *before, *pieces)
-    return rows, total
+    half = jax.ShapeDtypeStruct((slots, rows, columns), BF16)
+    part = jax.ShapeDtypeStruct((8, 128), F32)
+    cost = dict(
+        flops=slots * order * order * columns, moved=slots * (order + columns) * order * 2
+    )
+    out2, out3, far_sum, whole = call(
+        functools.partial(far_kernel, slots),
+        (half, half, part, jax.ShapeDtypeStruct((slots, order, columns), BF16)),
+        [IN_SMEM, IN_SMEM, IN_VMEM, IN_SMEM] + [IN_VMEM] * 4,
+        (IN_VMEM,) * 4,
+        "far_product",
+        **cost,
+    )(me, assign, root, factor, grad, *pieces)
+    own, out1, total = call(
+        functools.partial(near_kernel, slots),
+        (half, half, part),
+        [IN_SMEM, IN_VMEM, IN_SMEM, IN_VMEM, IN_VMEM],
+        (IN_VMEM,) * 3,
+        "near_product",
+        **cost,
+    )(me, root, factor, whole, far_sum)
+    return (own, out1, out2, out3), total
 
 
 def clip_kernel(slots, elements, me_ref, assign_ref, *rest):
-    sums, rows, out_ref = rest[:4], rest[4:-1], rest[-1]
+    sums, rows, out_hbm, out_ref, sems = rest[:4], rest[4:8], *rest[8:]
     me = me_ref[0]
     quadratic = jnp.sum(sums[0][...] + sums[1][...] + sums[2][...] + sums[3][...])
     ratio = jnp.full((8, 128), F32(KL_BOUND * elements)) / quadratic
     clip_factor = jnp.max(jnp.minimum(F32(1.0), jnp.sqrt(ratio)))
-    for slot in range(slots):
-        for far in range(4):
+    copies = []
+    for far in range(4):
+        for slot in range(slots):
+            at = far * slots + slot
             block = block_in_slot(assign_ref, (me ^ far) * slots + slot)
-            out_ref[0, block] = (clip_factor * rows[slot * 4 + far][...].astype(F32)).astype(BF16)
+            out_ref[at] = (clip_factor * rows[far][slot].astype(F32)).astype(BF16)
+            copies.append(pltpu.make_async_copy(out_ref.at[at], out_hbm.at[0, block], sems.at[at]))
+            copies[-1].start()
+    for copy in copies:
+        copy.wait()
 
 
 def clip(me, assign, sums, rows, shape, slots, elements):
@@ -400,10 +479,25 @@
         functools.partial(clip_kernel, slots, elements),
         jax.ShapeDtypeStruct(shape, BF16),
         [IN_SMEM, IN_SMEM] + [IN_VMEM] * (len(sums) + len(rows)),
-        IN_VMEM,
+        ANYWHERE,
         "clip",
+        scratch=[pltpu.VMEM(shape[1:], BF16), pltpu.SemaphoreType.DMA((shape[1],))],
         moved=4 * shape[1] * shape[2] * shape[3],
     )(me, assign, *sums, *rows)
+
+
+def after_kernel(value_ref, landed_ref, out_ref):
+    out_ref[...] = value_ref[...]
+
+
+def after(value, landed):
+    return call(
+        after_kernel,
+        jax.ShapeDtypeStruct(value.shape, value.dtype),
+        [IN_VMEM, ANYWHERE],
+        IN_VMEM,
+        "after",
+    )(value, landed)
 
 
 def partner_of(value, axis, far):
@@ -425,27 +519,15 @@
     me = lax.axis_index("fsdp").astype(jnp.int32).reshape(1)
     slots = assign.shape[1] // 4
     near, far2, far3 = pack_stats(me, assign, stats, slots)
-    received = [None] * 3
-    received[1] = partner_of(far2, "fsdp", 2)
-    received[2] = partner_of(far3, "fsdp", 3)
-    received[0] = partner_of(near, "fsdp", 1)
+    received = [partner_of(near, "fsdp", 1), partner_of(far2, "fsdp", 2), partner_of(far3, "fsdp", 3)]
     sent = pack_grad(me, assign, grad, slots)
-    pieces = []
-    for slot in range(slots):
-        here = {0: sent[slot][0]}
-        for far in (3, 2, 1):
-            here[far] = partner_of(sent[slot][far], "fsdp", far)
-        pieces.append([here[far] for far in range(4)])
+    pieces = [partner_of(piece, "fsdp", far) for far, piece in enumerate(sent, 1)]
     root, factor = roots(me, assign, due, cost, stats, received, stale, slots)
-    rows, total = [], None
-    for slot in range(slots):
-        solved, total = product(slot, me, root, factor, pieces[slot], total)
-        back = {0: solved[0]}
-        for far in (3, 2, 1):
-            back[far] = partner_of(solved[far], "fsdp", far)
-        rows += [back[far] for far in range(4)]
+    solved, total = products(slots, me, assign, root, factor, grad, pieces)
+    rows = [solved[0]] + [partner_of(solved[far], "fsdp", far) for far in (1, 2, 3)]
     total = sum_over(total, "dp")
-    sums = [total] + [partner_of(total, "fsdp", far) for far in (1, 2, 3)]
+    sums = [total, partner_of(after(total, rows[1]), "fsdp", 1)]
+    sums += [partner_of(total, "fsdp", far) for far in (2, 3)]
     elements = lax.axis_size("dp") * assign.shape[1] * stats.shape[3] * grad.shape[3]
     return clip(me, assign, sums, rows, grad.shape, slots, elements)
 

time: 76.2 us -> 68.7 us (0.902)
  starting transfers between devices: 41.2 us -> 26.6 us
  waiting for transfers between devices: 20.5 us -> 25.7 us
  Pallas kernels: 12.3 us -> 14.2 us
    ppermute x18 -> x12, starting transfers between devices: 39.1 us -> 23.4 us  [partner_of(): return lax.ppermute(value, axis, [(i, i ^ far) for i in range(count)])]
    ppermute x18 -> x12, waiting for transfers between devices: 19.6 us -> 24.1 us  [partner_of(): return lax.ppermute(value, axis, [(i, i ^ far) for i in range(count)])]
    pallas_call x1, Pallas kernels: 5.5 us -> 8.87 us  [roots(): call(functools.partial(root_kernel, slots), (jax.ShapeDtypeStruct((slots,...]
    pallas_call x3 -> x4, Pallas kernels: 4.19 us -> 2.81 us  [the longest x1 1.15 us: products(): call(functools.partial(far_kernel, slots), (half, half, part, jax.ShapeDt...]
    ppermute x3, starting transfers between devices: 2.1 us -> 3.18 us  [sum_over(): lax.ppermute(value, axis, [(i, (i + shift) % count) for i in range(count)])]
  transfers between devices with their start and end apart: 21 -> 15, of which waited for: 6 -> 7; matrix products, arithmetic and copies ran while one was open for 0% -> 0% of each run, Pallas kernels for 11% -> 14%
where the time goes in v2:
time: 68.7 us; the launch traced here: 68.6 us
  starting transfers between devices  26.6 us (39%)
  waiting for transfers between devices  25.7 us (37%)
  Pallas kernels  14.2 us (21%)
  local copies, waits for them, and re-layouts  1.98 us (3%)
    ppermute x12, waiting for transfers between devices, partner_of(): return lax.ppermute(value, axis, [(i, i ^ far) for i in range(count)])  24.1 us
    ppermute x12, starting transfers between devices, partner_of(): return lax.ppermute(value, axis, [(i, i ^ far) for i in range(count)])  23.4 us
    pallas_call x1, Pallas kernels, roots(): call(functools.partial(root_kernel, slots), (jax.ShapeDtypeStruct((slots,...  8.87 us
    ppermute x3, starting transfers between devices, sum_over(): lax.ppermute(value, axis, [(i, (i + shift) % count) for i in range(count)])  3.18 us
    unnamed x12, local copies, waits for them, and re-layouts  1.98 us
    pallas_call x1, Pallas kernels, clip(): call(functools.partial(clip_kernel, slots, elements), jax.ShapeDtypeStruc...  1.76 us
    ppermute x3, waiting for transfers between devices, sum_over(): lax.ppermute(value, axis, [(i, (i + shift) % count) for i in range(count)])  1.61 us
  transfers between devices with their start and end apart: 15, of which 7 were waited for; matrix products, arithmetic and copies ran while one was open for 0% of the time, Pallas kernels for 14%

profile of v2, /device:TPU:0, one launch (start us, length us, event | category | flops | bytes accessed | tf_op | source)
XLA Modules:
  0.0 68.6 jit_solution(4951986016895273382)
XLA Ops:
  0.0 0.0 copy-start
  0.0 0.0 copy-start.1
  0.0 1.3 %copy-done.1 = bf16[1,8,128,512]{3,2,1,0:T(8,128)(2,1)S(1)} copy-done((bf16[1,8,128,512]{3,2,1,0:T(8,128)(2,1)S(1)}, bf16[1,8,128,512]{3,2,1,0:T(8,128)(2,1)}, u32[]{:S(2)}) %copy-start.1) | copy-done | bytes 1048600
  1.3 0.0 copy-start.2
  1.3 0.7 copy-done.2
  2.0 0.0 copy-start.3
  2.0 0.7 %pack_stats.1 = (bf16[2,128,384]{2,1,0:T(8,128)(2,1)S(1)}, bf16[2,144,128]{2,1,0:T(8,128)(2,1)S(1)}, bf16[2,144,128]{2,1,0:T(8,128)(2,1)S(1)}) custom-call(s32[1]{0:T(128)} %bitcast.me_ref, s32[1,8]{1,0:T(1,128)S(1)} %copy-done.2, bf16[1,8,128,512]{3,2,1,0:T(8,128)(2,1)S(1)} %copy-done.1), custom_call_target="tpu_custom_call" | custom-call | bytes 2097152 | tf_op jit(solution)/shard_map/pack_stats/pallas_call | solution.py:179
  2.7 3.1 %collective-permute-start = (bf16[2,128,384]{2,1,0:T(8,128)(2,1)S(1)}, bf16[2,128,384]{2,1,0:T(8,128)(2,1)S(1)}, u32[]{:S(2)}, u32[]{:S(2)}) collective-permute-start(bf16[2,128,384]{2,1,0:T(8,128)(2,1)S(1)} %get-tuple-element.20), channel_id=1, source_target_pairs={{0,4},{4,0},{8,12},{12,8},{1,5},{5,1},{9,13},{13,9},{2,6},{6,2},{1... | collective-permute-start | bytes 589832 | tf_op jit(solution)/shard_map/ppermute | solution.py:505
  5.8 2.6 %collective-permute-start.1 = (bf16[2,144,128]{2,1,0:T(8,128)(2,1)S(1)}, bf16[2,144,128]{2,1,0:T(8,128)(2,1)S(1)}, u32[]{:S(2)}, u32[]{:S(2)}) collective-permute-start(bf16[2,144,128]{2,1,0:T(8,128)(2,1)S(1)} %get-tuple-element.21), channel_id=1, source_target_pairs={{0,8},{4,12},{8,0},{12,4},{1,9},{5,13},{9,1},{13,5},{2,10},{6,14},... | collective-permute-start | bytes 221192 | tf_op jit(solution)/shard_map/ppermute | solution.py:505
  8.4 0.0 collective-permute-start.2
  8.4 0.0 copy-done
  8.4 0.6 pack_grad.1
  9.0 1.0 %collective-permute-start.3 = (bf16[2,128,512]{2,1,0:T(8,128)(2,1)S(1)}, bf16[2,128,512]{2,1,0:T(8,128)(2,1)S(1)}, u32[]{:S(2)}, u32[]{:S(2)}) collective-permute-start(bf16[2,128,512]{2,1,0:T(8,128)(2,1)S(1)} %get-tuple-element.25), channel_id=1, source_target_pairs={{0,4},{4,0},{8,12},{12,8},{1,5},{5,1},{9,13},{13,9},{2,6},{6,2},{1... | collective-permute-start | bytes 786440 | tf_op jit(solution)/shard_map/ppermute | solution.py:505
  10.0 0.0 copy-start.4
  10.0 0.0 copy-start.5
  10.0 3.5 %collective-permute-start.4 = (bf16[2,128,512]{2,1,0:T(8,128)(2,1)S(1)}, bf16[2,128,512]{2,1,0:T(8,128)(2,1)S(1)}, u32[]{:S(2)}, u32[]{:S(2)}) collective-permute-start(bf16[2,128,512]{2,1,0:T(8,128)(2,1)S(1)} %get-tuple-element.26), channel_id=1, source_target_pairs={{0,8},{4,12},{8,0},{12,4},{1,9},{5,13},{9,1},{13,5},{2,10},{6,14},... | collective-permute-start | bytes 786440 | tf_op jit(solution)/shard_map/ppermute | solution.py:505
  13.5 0.0 collective-permute-done.1.far2_ref
  13.5 1.7 %collective-permute-start.5 = (bf16[2,128,512]{2,1,0:T(8,128)(2,1)S(1)}, bf16[2,128,512]{2,1,0:T(8,128)(2,1)S(1)}, u32[]{:S(2)}, u32[]{:S(2)}) collective-permute-start(bf16[2,128,512]{2,1,0:T(8,128)(2,1)S(1)} %get-tuple-element.27), channel_id=1, source_target_pairs={{0,12},{4,8},{8,4},{12,0},{1,13},{5,9},{9,5},{13,1},{2,14},{6,10},... | collective-permute-start | bytes 786440 | tf_op jit(solution)/shard_map/ppermute | solution.py:505
  15.2 2.1 %collective-permute-done.2.far3_ref = bf16[2,144,128]{2,1,0:T(8,128)(2,1)S(1)} collective-permute-done((bf16[2,144,128]{2,1,0:T(8,128)(2,1)S(1)}, bf16[2,144,128]{2,1,0:T(8,128)(2,1)S(1)}, u32[]{:S(2)}, u32[]{:S(2)}) %collective-permute-start.2) | collective-permute-done | bytes 73760 | tf_op jit(solution)/shard_map/ppermute | solution.py:505
  17.3 0.0 collective-permute-done.near_ref
  17.3 0.0 copy-done.3
  17.3 0.0 copy-done.4
  17.3 0.0 copy-done.5
  17.3 8.9 %roots.1 = (bf16[2,512,512]{2,1,0:T(8,128)(2,1)S(1)}, f32[2]{0:T(128)S(1)}) custom-call(s32[1]{0:T(128)} %bitcast.me_ref, s32[1,8]{1,0:T(1,128)S(1)} %copy-done.2, s32[1,8]{1,0:T(1,128)S(1)} %copy-done.4, s32[1,8]{1,0:T(1,128)S(1)} %copy-done.5, bf16[1,8,128,512]{3,2,1,0:T(8,128)(2,1)S(1)} %copy-done.1, ...), custom_call_target="tpu_custom_call" | custom-call | flops 4831838208 | bytes 3145728 | tf_op jit(solution)/shard_map/roots/pallas_call | solution.py:356
  26.2 0.0 collective-permute-done.3.near_ref
  26.2 6.9 %collective-permute-done.4.far2_ref = bf16[2,128,512]{2,1,0:T(8,128)(2,1)S(1)} collective-permute-done((bf16[2,128,512]{2,1,0:T(8,128)(2,1)S(1)}, bf16[2,128,512]{2,1,0:T(8,128)(2,1)S(1)}, u32[]{:S(2)}, u32[]{:S(2)}) %collective-permute-start.4) | collective-permute-done | bytes 262176 | tf_op jit(solution)/shard_map/ppermute | solution.py:505
  33.1 0.0 collective-permute-done.5.far3_ref
  33.1 1.1 %far_product.1 = (bf16[2,128,512]{2,1,0:T(8,128)(2,1)S(1)}, bf16[2,128,512]{2,1,0:T(8,128)(2,1)S(1)}, f32[8,128]{1,0:T(8,128)S(1)}, bf16[2,512,512]{2,1,0:T(8,128)(2,1)S(1)}) custom-call(s32[1]{0:T(128)} %bitcast.me_ref, s32[1,8]{1,0:T(1,128)S(1)} %copy-done.2, bf16[2,512,512]{2,1,0:T(8,128)(2,1)S(1)} %get-tuple-element.23.root_ref, ...), custom_call_target="tpu_custom_call" | custom-call | flops 268435456 | bytes 2097152 | tf_op jit(solution)/shard_map/far_product/pallas_call | solution.py:440
  34.2 1.1 %near_product.1 = (bf16[2,128,512]{2,1,0:T(8,128)(2,1)S(1)}, bf16[2,128,512]{2,1,0:T(8,128)(2,1)S(1)}, f32[8,128]{1,0:T(8,128)S(1)}) custom-call(s32[1]{0:T(128)} %bitcast.me_ref, bf16[2,512,512]{2,1,0:T(8,128)(2,1)S(1)} %get-tuple-element.23.root_ref, f32[2]{0:T(128)S(1)} %get-tuple-element.24.factor_ref, ...), custom_call_target="tpu_custom_call" | custom-call | flops 268435456 | bytes 2097152 | tf_op jit(solution)/shard_map/near_product/pallas_call | solution.py:448
  35.3 5.8 %collective-permute-start.9 = (bf16[2,128,512]{2,1,0:T(8,128)(2,1)S(1)}, bf16[2,128,512]{2,1,0:T(8,128)(2,1)S(1)}, u32[]{:S(2)}, u32[]{:S(2)}) collective-permute-start(bf16[2,128,512]{2,1,0:T(8,128)(2,1)S(1)} %get-tuple-element.31), channel_id=1, source_target_pairs={{0,4},{4,0},{8,12},{12,8},{1,5},{5,1},{9,13},{13,9},{2,6},{6,2},{1... | collective-permute-start | bytes 786440 | tf_op jit(solution)/shard_map/ppermute | solution.py:505
  41.1 0.5 collective-permute-start.13
  41.6 1.9 %collective-permute-start.14 = (bf16[2,128,512]{2,1,0:T(8,128)(2,1)S(1)}, bf16[2,128,512]{2,1,0:T(8,128)(2,1)S(1)}, u32[]{:S(2)}, u32[]{:S(2)}) collective-permute-start(bf16[2,128,512]{2,1,0:T(8,128)(2,1)S(1)} %get-tuple-element.34), channel_id=1, source_target_pairs={{0,12},{4,8},{8,4},{12,0},{1,13},{5,9},{9,5},{13,1},{2,14},{6,10},... | collective-permute-start | bytes 786440 | tf_op jit(solution)/shard_map/ppermute | solution.py:505
  43.5 0.2 collective-permute-start.8
  43.7 1.3 %collective-permute-start.7 = (f32[8,128]{1,0:T(8,128)S(1)}, f32[8,128]{1,0:T(8,128)S(1)}, u32[]{:S(2)}, u32[]{:S(2)}) collective-permute-start(f32[8,128]{1,0:T(8,128)S(1)} %get-tuple-element.30), channel_id=1, source_target_pairs={{0,2},{1,3},{2,0},{3,1},{4,6},{5,7},{6,4},{7,5},{8,10},{9,11},{10,... | collective-permute-start | bytes 12296 | tf_op jit(solution)/shard_map/ppermute | solution.py:512
  45.0 0.0 collective-permute-done.8
  45.0 1.7 %collective-permute-start.6 = (f32[8,128]{1,0:T(8,128)S(1)}, f32[8,128]{1,0:T(8,128)S(1)}, u32[]{:S(2)}, u32[]{:S(2)}) collective-permute-start(f32[8,128]{1,0:T(8,128)S(1)} %get-tuple-element.30), channel_id=1, source_target_pairs={{0,1},{1,2},{2,3},{3,0},{4,5},{5,6},{6,7},{7,4},{8,9},{9,10},{10,1... | collective-permute-start | bytes 12296 | tf_op jit(solution)/shard_map/ppermute | solution.py:512
  46.7 0.6 collective-permute-done.7
  47.3 1.0 %collective-permute-done.6 = f32[8,128]{1,0:T(8,128)S(1)} collective-permute-done((f32[8,128]{1,0:T(8,128)S(1)}, f32[8,128]{1,0:T(8,128)S(1)}, u32[]{:S(2)}, u32[]{:S(2)}) %collective-permute-start.6) | collective-permute-done | bytes 4128 | tf_op jit(solution)/shard_map/ppermute | solution.py:512
  48.3 2.0 %collective-permute-start.12 = (f32[8,128]{1,0:T(8,128)S(1)}, f32[8,128]{1,0:T(8,128)S(1)}, u32[]{:S(2)}, u32[]{:S(2)}) collective-permute-start(f32[8,128]{1,0:T(8,128)S(1)} %add_add_fusion.value_ref.rest_0_), channel_id=1, source_target_pairs={{0,12},{4,8},{8,4},{12,0},{1,13},{5,9},{9,5},{13,1},{2,14},{6,10},... | collective-permute-start | bytes 12296 | tf_op jit(solution)/shard_map/ppermute | solution.py:505
  50.2 0.4 collective-permute-start.11
  50.6 1.0 %collective-permute-done.9.landed_ref.rest_5_ = bf16[2,128,512]{2,1,0:T(8,128)(2,1)S(1)} collective-permute-done((bf16[2,128,512]{2,1,0:T(8,128)(2,1)S(1)}, bf16[2,128,512]{2,1,0:T(8,128)(2,1)S(1)}, u32[]{:S(2)}, u32[]{:S(2)}) %collective-permute-start.9) | collective-permute-done | bytes 262176 | tf_op jit(solution)/shard_map/ppermute | solution.py:505
  51.6 1.0 %collective-permute-start.10 = (f32[8,128]{1,0:T(8,128)S(1)}, f32[8,128]{1,0:T(8,128)S(1)}, u32[]{:S(2)}, u32[]{:S(2)}) collective-permute-start(f32[8,128]{1,0:T(8,128)S(1)} %after.1), channel_id=1, source_target_pairs={{0,4},{4,0},{8,12},{12,8},{1,5},{5,1},{9,13},{13,9},{2,6},{6,2},{1... | collective-permute-start | bytes 12296 | tf_op jit(solution)/shard_map/ppermute | solution.py:505
  52.7 7.6 %collective-permute-done.12.rest_3_ = f32[8,128]{1,0:T(8,128)S(1)} collective-permute-done((f32[8,128]{1,0:T(8,128)S(1)}, f32[8,128]{1,0:T(8,128)S(1)}, u32[]{:S(2)}, u32[]{:S(2)}) %collective-permute-start.12) | collective-permute-done | bytes 4128 | tf_op jit(solution)/shard_map/ppermute | solution.py:505
  60.3 6.5 %collective-permute-done.11.rest_2_ = f32[8,128]{1,0:T(8,128)S(1)} collective-permute-done((f32[8,128]{1,0:T(8,128)S(1)}, f32[8,128]{1,0:T(8,128)S(1)}, u32[]{:S(2)}, u32[]{:S(2)}) %collective-permute-start.11) | collective-permute-done | bytes 4128 | tf_op jit(solution)/shard_map/ppermute | solution.py:505
  66.8 0.0 collective-permute-done.13.rest_6_
  66.8 0.0 collective-permute-done.14.rest_7_
  66.8 0.0 collective-permute-done.10.rest_1_
  66.8 1.8 %clip.1 = bf16[1,8,128,512]{3,2,1,0:T(8,128)(2,1)} custom-call(s32[1]{0:T(128)} %bitcast.me_ref, s32[1,8]{1,0:T(1,128)S(1)} %copy-done.2, f32[8,128]{1,0:T(8,128)S(1)} %add_add_fusion.value_ref.rest_0_, f32[8,128]{1,0:T(8,128)S(1)} %collective-permute-done.10.rest_1_, f32[8,128]{1,0:T(8,128)S(1)} %collective-permute-done.11.rest_2_, ...), custom_call_target="tpu_custom_call" | custom-call | bytes 2097152 | tf_op jit(solution)/shard_map/clip/pallas_call | solution.py:478
  (2 shorter events, 0.0 us)
Async XLA Ops:
  0.0 8.4 %copy-start = (bf16[1,8,128,512]{3,2,1,0:T(8,128)(2,1)S(1)}, bf16[1,8,128,512]{3,2,1,0:T(8,128)(2,1)}, u32[]{:S(2)}) copy-start(bf16[1,8,128,512]{3,2,1,0:T(8,128)(2,1)} %grad_ref.3) | copy-start | bytes 3145732
  0.0 1.3 %copy-start.1 = (bf16[1,8,128,512]{3,2,1,0:T(8,128)(2,1)S(1)}, bf16[1,8,128,512]{3,2,1,0:T(8,128)(2,1)}, u32[]{:S(2)}) copy-start(bf16[1,8,128,512]{3,2,1,0:T(8,128)(2,1)} %stats_ref.1) | copy-start | bytes 3145732
  1.3 0.7 copy-start.2
  2.0 15.3 %copy-start.3 = (bf16[1,2,512,512]{3,2,1,0:T(8,128)(2,1)S(1)}, bf16[1,2,512,512]{3,2,1,0:T(8,128)(2,1)}, u32[]{:S(2)}) copy-start(bf16[1,2,512,512]{3,2,1,0:T(8,128)(2,1)} %stale_ref.1) | copy-start | bytes 3145732
  2.7 14.5 %collective-permute-start = (bf16[2,128,384]{2,1,0:T(8,128)(2,1)S(1)}, bf16[2,128,384]{2,1,0:T(8,128)(2,1)S(1)}, u32[]{:S(2)}, u32[]{:S(2)}) collective-permute-start(bf16[2,128,384]{2,1,0:T(8,128)(2,1)S(1)} %get-tuple-element.20), channel_id=1, source_target_pairs={{0,4},{4,0},{8,12},{12,8},{1,5},{5,1},{9,13},{13,9},{2,6},{6,2},{1... | collective-permute-start | bytes 589832 | tf_op jit(solution)/shard_map/ppermute | solution.py:505
  5.8 7.7 %collective-permute-start.1 = (bf16[2,144,128]{2,1,0:T(8,128)(2,1)S(1)}, bf16[2,144,128]{2,1,0:T(8,128)(2,1)S(1)}, u32[]{:S(2)}, u32[]{:S(2)}) collective-permute-start(bf16[2,144,128]{2,1,0:T(8,128)(2,1)S(1)} %get-tuple-element.21), channel_id=1, source_target_pairs={{0,8},{4,12},{8,0},{12,4},{1,9},{5,13},{9,1},{13,5},{2,10},{6,14},... | collective-permute-start | bytes 221192 | tf_op jit(solution)/shard_map/ppermute | solution.py:505
  8.4 8.9 %collective-permute-start.2 = (bf16[2,144,128]{2,1,0:T(8,128)(2,1)S(1)}, bf16[2,144,128]{2,1,0:T(8,128)(2,1)S(1)}, u32[]{:S(2)}, u32[]{:S(2)}) collective-permute-start(bf16[2,144,128]{2,1,0:T(8,128)(2,1)S(1)} %get-tuple-element.22), channel_id=1, source_target_pairs={{0,12},{4,8},{8,4},{12,0},{1,13},{5,9},{9,5},{13,1},{2,14},{6,10},... | collective-permute-start | bytes 221192 | tf_op jit(solution)/shard_map/ppermute | solution.py:505
  9.0 17.1 %collective-permute-start.3 = (bf16[2,128,512]{2,1,0:T(8,128)(2,1)S(1)}, bf16[2,128,512]{2,1,0:T(8,128)(2,1)S(1)}, u32[]{:S(2)}, u32[]{:S(2)}) collective-permute-start(bf16[2,128,512]{2,1,0:T(8,128)(2,1)S(1)} %get-tuple-element.25), channel_id=1, source_target_pairs={{0,4},{4,0},{8,12},{12,8},{1,5},{5,1},{9,13},{13,9},{2,6},{6,2},{1... | collective-permute-start | bytes 786440 | tf_op jit(solution)/shard_map/ppermute | solution.py:505
  10.0 7.3 %copy-start.4 = (s32[1,8]{1,0:T(1,128)S(1)}, s32[1,8]{1,0:T(1,128)}, u32[]{:S(2)}) copy-start(s32[1,8]{1,0:T(1,128)} %due_ref.1) | copy-start | bytes 100
  10.0 7.3 %copy-start.5 = (s32[1,8]{1,0:T(1,128)S(1)}, s32[1,8]{1,0:T(1,128)}, u32[]{:S(2)}) copy-start(s32[1,8]{1,0:T(1,128)} %cost_ref.1) | copy-start | bytes 100
  10.0 23.1 %collective-permute-start.4 = (bf16[2,128,512]{2,1,0:T(8,128)(2,1)S(1)}, bf16[2,128,512]{2,1,0:T(8,128)(2,1)S(1)}, u32[]{:S(2)}, u32[]{:S(2)}) collective-permute-start(bf16[2,128,512]{2,1,0:T(8,128)(2,1)S(1)} %get-tuple-element.26), channel_id=1, source_target_pairs={{0,8},{4,12},{8,0},{12,4},{1,9},{5,13},{9,1},{13,5},{2,10},{6,14},... | collective-permute-start | bytes 786440 | tf_op jit(solution)/shard_map/ppermute | solution.py:505
  13.5 19.6 %collective-permute-start.5 = (bf16[2,128,512]{2,1,0:T(8,128)(2,1)S(1)}, bf16[2,128,512]{2,1,0:T(8,128)(2,1)S(1)}, u32[]{:S(2)}, u32[]{:S(2)}) collective-permute-start(bf16[2,128,512]{2,1,0:T(8,128)(2,1)S(1)} %get-tuple-element.27), channel_id=1, source_target_pairs={{0,12},{4,8},{8,4},{12,0},{1,13},{5,9},{9,5},{13,1},{2,14},{6,10},... | collective-permute-start | bytes 786440 | tf_op jit(solution)/shard_map/ppermute | solution.py:505
  35.3 16.4 %collective-permute-start.9 = (bf16[2,128,512]{2,1,0:T(8,128)(2,1)S(1)}, bf16[2,128,512]{2,1,0:T(8,128)(2,1)S(1)}, u32[]{:S(2)}, u32[]{:S(2)}) collective-permute-start(bf16[2,128,512]{2,1,0:T(8,128)(2,1)S(1)} %get-tuple-element.31), channel_id=1, source_target_pairs={{0,4},{4,0},{8,12},{12,8},{1,5},{5,1},{9,13},{13,9},{2,6},{6,2},{1... | collective-permute-start | bytes 786440 | tf_op jit(solution)/shard_map/ppermute | solution.py:505
  41.1 25.7 %collective-permute-start.13 = (bf16[2,128,512]{2,1,0:T(8,128)(2,1)S(1)}, bf16[2,128,512]{2,1,0:T(8,128)(2,1)S(1)}, u32[]{:S(2)}, u32[]{:S(2)}) collective-permute-start(bf16[2,128,512]{2,1,0:T(8,128)(2,1)S(1)} %get-tuple-element.33), channel_id=1, source_target_pairs={{0,8},{4,12},{8,0},{12,4},{1,9},{5,13},{9,1},{13,5},{2,10},{6,14},... | collective-permute-start | bytes 786440 | tf_op jit(solution)/shard_map/ppermute | solution.py:505
  41.6 25.2 %collective-permute-start.14 = (bf16[2,128,512]{2,1,0:T(8,128)(2,1)S(1)}, bf16[2,128,512]{2,1,0:T(8,128)(2,1)S(1)}, u32[]{:S(2)}, u32[]{:S(2)}) collective-permute-start(bf16[2,128,512]{2,1,0:T(8,128)(2,1)S(1)} %get-tuple-element.34), channel_id=1, source_target_pairs={{0,12},{4,8},{8,4},{12,0},{1,13},{5,9},{9,5},{13,1},{2,14},{6,10},... | collective-permute-start | bytes 786440 | tf_op jit(solution)/shard_map/ppermute | solution.py:505
  43.5 1.5 %collective-permute-start.8 = (f32[8,128]{1,0:T(8,128)S(1)}, f32[8,128]{1,0:T(8,128)S(1)}, u32[]{:S(2)}, u32[]{:S(2)}) collective-permute-start(f32[8,128]{1,0:T(8,128)S(1)} %get-tuple-element.30), channel_id=1, source_target_pairs={{0,3},{1,0},{2,1},{3,2},{4,7},{5,4},{6,5},{7,6},{8,11},{9,8},{10,9... | collective-permute-start | bytes 12296 | tf_op jit(solution)/shard_map/ppermute | solution.py:512
  43.7 3.6 %collective-permute-start.7 = (f32[8,128]{1,0:T(8,128)S(1)}, f32[8,128]{1,0:T(8,128)S(1)}, u32[]{:S(2)}, u32[]{:S(2)}) collective-permute-start(f32[8,128]{1,0:T(8,128)S(1)} %get-tuple-element.30), channel_id=1, source_target_pairs={{0,2},{1,3},{2,0},{3,1},{4,6},{5,7},{6,4},{7,5},{8,10},{9,11},{10,... | collective-permute-start | bytes 12296 | tf_op jit(solution)/shard_map/ppermute | solution.py:512
  45.0 3.3 %collective-permute-start.6 = (f32[8,128]{1,0:T(8,128)S(1)}, f32[8,128]{1,0:T(8,128)S(1)}, u32[]{:S(2)}, u32[]{:S(2)}) collective-permute-start(f32[8,128]{1,0:T(8,128)S(1)} %get-tuple-element.30), channel_id=1, source_target_pairs={{0,1},{1,2},{2,3},{3,0},{4,5},{5,6},{6,7},{7,4},{8,9},{9,10},{10,1... | collective-permute-start | bytes 12296 | tf_op jit(solution)/shard_map/ppermute | solution.py:512
  48.3 12.0 %collective-permute-start.12 = (f32[8,128]{1,0:T(8,128)S(1)}, f32[8,128]{1,0:T(8,128)S(1)}, u32[]{:S(2)}, u32[]{:S(2)}) collective-permute-start(f32[8,128]{1,0:T(8,128)S(1)} %add_add_fusion.value_ref.rest_0_), channel_id=1, source_target_pairs={{0,12},{4,8},{8,4},{12,0},{1,13},{5,9},{9,5},{13,1},{2,14},{6,10},... | collective-permute-start | bytes 12296 | tf_op jit(solution)/shard_map/ppermute | solution.py:505
  50.2 16.5 %collective-permute-start.11 = (f32[8,128]{1,0:T(8,128)S(1)}, f32[8,128]{1,0:T(8,128)S(1)}, u32[]{:S(2)}, u32[]{:S(2)}) collective-permute-start(f32[8,128]{1,0:T(8,128)S(1)} %add_add_fusion.value_ref.rest_0_), channel_id=1, source_target_pairs={{0,8},{4,12},{8,0},{12,4},{1,9},{5,13},{9,1},{13,5},{2,10},{6,14},... | collective-permute-start | bytes 12296 | tf_op jit(solution)/shard_map/ppermute | solution.py:505
  51.6 15.1 %collective-permute-start.10 = (f32[8,128]{1,0:T(8,128)S(1)}, f32[8,128]{1,0:T(8,128)S(1)}, u32[]{:S(2)}, u32[]{:S(2)}) collective-permute-start(f32[8,128]{1,0:T(8,128)S(1)} %after.1), channel_id=1, source_target_pairs={{0,4},{4,0},{8,12},{12,8},{1,5},{5,1},{9,13},{13,9},{2,6},{6,2},{1... | collective-permute-start | bytes 12296 | tf_op jit(solution)/shard_map/ppermute | solution.py:505

commit v3 on v2

--- a/solution.py
+++ b/solution.py
@@ -106,11 +106,17 @@
 ANYWHERE = pl.BlockSpec(memory_space=pl.ANY)
 
 
-def block_in_slot(assign_ref, slot):
-    found = jnp.int32(0)
-    for block in range(assign_ref.shape[1]):
-        found = jnp.where(assign_ref[0, block] == slot, jnp.int32(block), found)
-    return found
+def plan_of(table_row):
+    total = table_row.shape[0]
+    blocks = lax.broadcasted_iota(jnp.int32, (total + 1, total), 1)
+    slots = lax.broadcasted_iota(jnp.int32, (total + 1, total), 0)
+    source = jnp.sum(jnp.where(table_row[None, :] == slots, blocks, 0), axis=1)
+    place = lax.axis_index("fsdp").astype(jnp.int32)
+    return jnp.where(jnp.arange(total + 1) == total, place, source)
+
+
+def place_of(plan_ref):
+    return plan_ref[plan_ref.shape[0] - 1]
 
 
 def tile_at(index, width):
@@ -141,80 +147,76 @@
     return jnp.concatenate([top, jnp.where(lane < half, turned[half:, :], last)], axis=0)
 
 
-def pack_stats_kernel(
-    slots, me_ref, assign_hbm, stats_hbm, near_ref, far2_ref, far3_ref, assign_ref, stats_ref, sems
-):
-    table = pltpu.make_async_copy(assign_hbm, assign_ref, sems.at[0])
-    table.start()
-    blocks = pltpu.make_async_copy(stats_hbm, stats_ref, sems.at[1])
-    blocks.start()
-    me = me_ref[0]
+def pack_stats_kernel(slots, plan_ref, stats_ref, near_ref, far2_ref, far3_ref):
+    me = place_of(plan_ref)
     width = stats_ref.shape[2]
     half = width // 2
     odd = me % 2
-    table.wait()
-    blocks.wait()
-    for slot in range(slots):
-        for far, out in ((2, far2_ref), (3, far3_ref)):
-            block = block_in_slot(assign_ref, (me ^ far) * slots + slot)
+    for far, out in ((2, far2_ref), (3, far3_ref)):
+        diagonals = []
+        for slot in range(slots):
+            block = plan_ref[(me ^ far) * slots + slot]
             between = stats_ref[0, block, :, tile_at(me ^ 1, width)].astype(F32)
-            out[slot, :half, :] = jnp.where(odd == 1, between.T[half:, :], between[:half, :]).astype(
+            at = slot * width
+            out[at : at + half, :] = jnp.where(
+                odd == 1, between.T[half:, :], between[:half, :]
+            ).astype(BF16)
+            folded, diagonal = fold(stats_ref[0, block, :, tile_at(me, width)].astype(F32))
+            out[at + half : at + width, :] = folded.astype(BF16)
+            diagonals.append(diagonal)
+        lane = lax.broadcasted_iota(jnp.int32, (1, width), 1)
+        for start in range(0, slots, 2):
+            pair = pltpu.roll(diagonals[start], half, 1)
+            if start + 1 < slots:
+                pair = jnp.where(lane < half, pair, diagonals[start + 1])
+            at = slots * width + start // 2 * DIAGONAL_ROWS
+            out[at : at + DIAGONAL_ROWS, :] = jnp.broadcast_to(pair, (DIAGONAL_ROWS, width)).astype(
                 BF16
             )
-            folded, diagonal = fold(stats_ref[0, block, :, tile_at(me, width)].astype(F32))
-            out[slot, half:width, :] = folded.astype(BF16)
-            out[slot, width:, :] = jnp.broadcast_to(diagonal, (DIAGONAL_ROWS, width)).astype(BF16)
     for slot in range(slots):
-        block = block_in_slot(assign_ref, (me ^ 1) * slots + slot)
+        block = plan_ref[(me ^ 1) * slots + slot]
         for place, other in enumerate((0, 2, 3)):
             near_ref[slot, :, place * width : (place + 1) * width] = stats_ref[
                 0, block, :, tile_at(me ^ other, width)
             ]
 
 
-def pack_stats(me, assign, stats, slots):
+def pack_stats(plan, stats, slots):
     width, order = stats.shape[2:]
     near = jax.ShapeDtypeStruct((slots, width, order - width), BF16)
-    far = jax.ShapeDtypeStruct((slots, width + DIAGONAL_ROWS, width), BF16)
+    far = jax.ShapeDtypeStruct((slots * width + (slots + 1) // 2 * DIAGONAL_ROWS, width), BF16)
     return call(
         functools.partial(pack_stats_kernel, slots),
         (near, far, far),
-        [IN_SMEM, ANYWHERE, ANYWHERE],
+        [IN_SMEM, IN_VMEM],
         (IN_VMEM,) * 3,
         "pack_stats",
-        scratch=[
-            pltpu.SMEM(assign.shape, jnp.int32),
-            pltpu.VMEM(stats.shape, BF16),
-            pltpu.SemaphoreType.DMA((2,)),
-        ],
         moved=2 * stats.size * 2,
-    )(me, assign, stats)
-
-
-def pack_grad_kernel(slots, me_ref, assign_ref, grad_ref, *outs):
-    me = me_ref[0]
-    for far in (3, 2, 1):
+    )(plan, stats)
+
+
+def pack_grad_kernel(slots, plan_ref, grad_ref, *outs):
+    me = place_of(plan_ref)
+    for far in (3, 2, 1, 0):
         for slot in range(slots):
-            block = block_in_slot(assign_ref, (me ^ far) * slots + slot)
-            outs[far - 1][slot] = grad_ref[0, block]
-
-
-def pack_grad(me, assign, grad, slots):
+            outs[far][slot] = grad_ref[0, plan_ref[(me ^ far) * slots + slot]]
+
+
+def pack_grad(plan, grad, slots):
     out = jax.ShapeDtypeStruct((slots, *grad.shape[2:]), BF16)
     return call(
         functools.partial(pack_grad_kernel, slots),
-        (out,) * 3,
-        [IN_SMEM, IN_SMEM, IN_VMEM],
-        (IN_VMEM,) * 3,
+        (out,) * 4,
+        [IN_SMEM, IN_VMEM],
+        (IN_VMEM,) * 4,
         "pack_grad",
         moved=2 * grad.size * 2,
-    )(me, assign, grad)
+    )(plan, grad)
 
 
 def root_kernel(
     slots,
-    me_ref,
-    assign_ref,
+    plan_ref,
     due_ref,
     cost_ref,
     stats_ref,
@@ -231,7 +233,7 @@
     sem,
     stale_sem,
 ):
-    me = me_ref[0]
+    me = place_of(plan_ref)
     order = full.shape[0]
     width = near_ref.shape[1]
     half = width // 2
@@ -249,13 +251,17 @@
         even, odd = (me ^ 2) & 2, ((me ^ 2) & 2) + 1
         at = lambda index: tile_at(index, width)
         two, three = me ^ 2, me ^ 3
+        start = slot * width
+        row = slots * width + slot // 2 * DIAGONAL_ROWS
         for index, far_ref in ((two, far2_ref), (three, far3_ref)):
+            diagonal = far_ref[row : row + 8, :].astype(F32)
+            if slot % 2 == 0:
+                diagonal = pltpu.roll(diagonal, half, 1)
             full[at(index), at(index)] = unfold(
-                far_ref[slot, half:width, :].astype(F32),
-                far_ref[slot, width : width + 1, :].astype(F32),
+                far_ref[start + half : start + width, :].astype(F32), diagonal[:1, :]
             )
-        from_two = far2_ref[slot, :half, :].astype(F32)
-        from_three = far3_ref[slot, :half, :].astype(F32)
+        from_two = far2_ref[start : start + half, :].astype(F32)
+        from_three = far3_ref[start : start + half, :].astype(F32)
         two_is_even = me % 2 == 0
         between = jnp.concatenate(
             [
@@ -278,10 +284,10 @@
             full[at(me ^ other), at(me)] = own[:, at(me ^ other)].astype(F32).T
 
     for slot in range(slots):
-        block = block_in_slot(assign_ref, me * slots + slot)
+        block = plan_ref[me * slots + slot]
         due = due_ref[0, block]
         cost = cost_ref[0, block]
-        factor_ref[slot] = F32(1.0)
+        factor_ref[slot] = jnp.ones((8, 128), F32)
 
         @pl.when(due <= 0)
         def _():
@@ -297,7 +303,7 @@
                 piece = full[start : start + 8, :]
                 total = total + piece * piece
             norm = jnp.sqrt(jnp.full((8, 128), jnp.sum(total), F32))
-            factor_ref[slot] = lax.rsqrt(norm)[0, 0]
+            factor_ref[slot] = lax.rsqrt(norm)
             divisor = jnp.max(norm)
             for i, start in enumerate(range(0, order, chunk)):
                 scaled = (full[rows[i], :] / divisor).astype(BF16)
@@ -350,17 +356,17 @@
                 next_root()
 
 
-def roots(me, assign, due, cost, stats, received, stale, slots):
+def roots(plan, due, cost, stats, received, stale, slots):
     order = stats.shape[3]
     width = stats.shape[2]
     return call(
         functools.partial(root_kernel, slots),
         (
             jax.ShapeDtypeStruct((slots, order, order), BF16),
-            jax.ShapeDtypeStruct((slots,), F32),
+            jax.ShapeDtypeStruct((slots, 8, 128), F32),
         ),
-        [IN_SMEM] * 4 + [ANYWHERE] + [IN_VMEM] * 3 + [ANYWHERE],
-        (IN_VMEM, IN_SMEM),
+        [IN_SMEM] * 3 + [ANYWHERE] + [IN_VMEM] * 3 + [ANYWHERE],
+        (IN_VMEM, IN_VMEM),
         "roots",
         scratch=[
             pltpu.VMEM((width, order), BF16),
@@ -372,93 +378,95 @@
         ],
         flops=slots * 9 * 2 * order**3,
         moved=slots * order * order * 6,
-    )(me, assign, due, cost, stats, *received, stale)
-
-
-def pair_product(slots, pair, odd, root_ref, factor_ref, whole_ref, first_ref, second_ref, sum_ref):
-    rows, columns = first_ref.shape[1:]
-    at = tile_at(pair, 2 * rows)
-    total = jnp.zeros(sum_ref.shape, F32)
+    )(plan, due, cost, stats, *received, stale)
+
+
+def start_kernel(
+    slots,
+    plan_ref,
+    root_ref,
+    own_ref,
+    grad1_ref,
+    far_root_ref,
+    near_root_ref,
+    far_ref,
+    near_ref,
+    columns_ref,
+):
+    me = place_of(plan_ref)
+    width = grad1_ref.shape[1]
     for slot in range(slots):
-        piece = jnp.dot(root_ref[slot, at, :], whole_ref[slot], preferred_element_type=F32)
-        rounded = (piece * factor_ref[slot]).astype(BF16)
-        low, high = rounded[:rows, :], rounded[rows:, :]
-        first_ref[slot] = jnp.where(odd, high, low)
-        second_ref[slot] = jnp.where(odd, low, high)
-        terms = rounded.astype(F32) * whole_ref[slot, at, :].astype(F32)
-        for start in range(0, 2 * rows, 8):
-            for column in range(0, columns, 128):
-                total = total + terms[start : start + 8, column : column + 128]
-    sum_ref[...] = total
-
-
-def far_kernel(
-    slots,
-    me_ref,
-    assign_ref,
-    root_ref,
-    factor_ref,
-    grad_ref,
-    near_ref,
-    far2_ref,
-    far3_ref,
-    out2_ref,
-    out3_ref,
-    sum_ref,
-    whole_ref,
-):
-    me = me_ref[0]
-    rows = near_ref.shape[1]
+        here = jnp.concatenate([own_ref[slot], grad1_ref[slot]], axis=0)
+        for places, root_out, out in (((2, 3), far_root_ref, far_ref), ((0, 1), near_root_ref, near_ref)):
+            for i, row in enumerate(places):
+                rows = tile_at(me ^ row, width)
+                for j in range(2):
+                    at = (slice(i * width, (i + 1) * width), slice(j * width, (j + 1) * width))
+                    root_out[slot, at[0], at[1]] = root_ref[slot, rows, tile_at(me ^ (2 + j), width)]
+                    columns_ref[at[0], at[1]] = root_ref[slot, rows, tile_at(me ^ j, width)]
+            out[slot] = jnp.dot(columns_ref[...], here, preferred_element_type=F32)
+
+
+def start_product(plan, root, own_grad, grad1):
+    slots, width, columns = grad1.shape
+    pair = jax.ShapeDtypeStruct((slots, 2 * width, 2 * width), BF16)
+    total = jax.ShapeDtypeStruct((slots, 2 * width, columns), F32)
+    return call(
+        functools.partial(start_kernel, slots),
+        (pair, pair, total, total),
+        [IN_SMEM] + [IN_VMEM] * 3,
+        (IN_VMEM,) * 4,
+        "start_product",
+        scratch=[pltpu.VMEM((2 * width, 2 * width), BF16)],
+        flops=slots * 16 * width * width * columns,
+        moved=slots * 16 * width * columns,
+    )(plan, root, own_grad, grad1)
+
+
+def finish_kernel(root_ref, begun_ref, factor_ref, grad2_ref, grad3_ref, *rest):
+    first_ref, second_ref = rest[-2:] if len(rest) == 2 else rest[-3:-1]
+    slots, width, columns = first_ref.shape
+    total = jnp.zeros((8, 128), F32)
     for slot in range(slots):
-        block = block_in_slot(assign_ref, me * slots + slot)
-        whole_ref[slot, tile_at(me, rows), :] = grad_ref[0, block]
-        for far, piece_ref in ((1, near_ref), (2, far2_ref), (3, far3_ref)):
-            whole_ref[slot, tile_at(me ^ far, rows), :] = piece_ref[slot]
-    pair_product(
-        slots, 1 - me // 2, me % 2 == 1, root_ref, factor_ref, whole_ref, out2_ref, out3_ref, sum_ref
-    )
-
-
-def near_kernel(
-    slots, me_ref, root_ref, factor_ref, whole_ref, far_sum_ref, own_ref, out1_ref, sum_ref
-):
-    me = me_ref[0]
-    pair_product(
-        slots, me // 2, me % 2 == 1, root_ref, factor_ref, whole_ref, own_ref, out1_ref, sum_ref
-    )
-    sum_ref[...] += far_sum_ref[...]
-
-
-def products(slots, me, assign, root, factor, grad, pieces):
-    rows, columns = pieces[0].shape[1:]
-    order = root.shape[1]
-    half = jax.ShapeDtypeStruct((slots, rows, columns), BF16)
-    part = jax.ShapeDtypeStruct((8, 128), F32)
-    cost = dict(
-        flops=slots * order * order * columns, moved=slots * (order + columns) * order * 2
-    )
-    out2, out3, far_sum, whole = call(
-        functools.partial(far_kernel, slots),
-        (half, half, part, jax.ShapeDtypeStruct((slots, order, columns), BF16)),
-        [IN_SMEM, IN_SMEM, IN_VMEM, IN_SMEM] + [IN_VMEM] * 4,
-        (IN_VMEM,) * 4,
-        "far_product",
-        **cost,
-    )(me, assign, root, factor, grad, *pieces)
-    own, out1, total = call(
-        functools.partial(near_kernel, slots),
-        (half, half, part),
-        [IN_SMEM, IN_VMEM, IN_SMEM, IN_VMEM, IN_VMEM],
-        (IN_VMEM,) * 3,
-        "near_product",
-        **cost,
-    )(me, root, factor, whole, far_sum)
-    return (own, out1, out2, out3), total
-
-
-def clip_kernel(slots, elements, me_ref, assign_ref, *rest):
+        there = jnp.concatenate([grad2_ref[slot], grad3_ref[slot]], axis=0)
+        product = begun_ref[slot] + jnp.dot(root_ref[slot], there, preferred_element_type=F32)
+        rounded = (product * factor_ref[slot, :1, :1]).astype(BF16)
+        first_ref[slot] = rounded[:width, :]
+        second_ref[slot] = rounded[width:, :]
+    if len(rest) > 2:
+        own_ref, grad1_ref, out2_ref, out3_ref = rest[:4]
+        for slot in range(slots):
+            for result_ref, with_ref in (
+                (first_ref, own_ref),
+                (second_ref, grad1_ref),
+                (out2_ref, grad2_ref),
+                (out3_ref, grad3_ref),
+            ):
+                terms = result_ref[slot].astype(F32) * with_ref[slot].astype(F32)
+                for start in range(0, width, 8):
+                    for column in range(0, columns, 128):
+                        total = total + terms[start : start + 8, column : column + 128]
+        rest[-1][...] = total
+
+
+def finish_product(root, begun, factor, grad2, grad3, *others):
+    slots, width, columns = grad2.shape
+    out = jax.ShapeDtypeStruct(grad2.shape, BF16)
+    shapes = (out, out) + ((jax.ShapeDtypeStruct((8, 128), F32),) if others else ())
+    return call(
+        finish_kernel,
+        shapes,
+        [IN_VMEM] * (5 + len(others)),
+        (IN_VMEM,) * len(shapes),
+        "near_product" if others else "far_product",
+        flops=slots * 8 * width * width * columns,
+        moved=slots * 16 * width * columns,
+    )(root, begun, factor, grad2, grad3, *others)
+
+
+def clip_kernel(slots, elements, plan_ref, *rest):
     sums, rows, out_hbm, out_ref, sems = rest[:4], rest[4:8], *rest[8:]
-    me = me_ref[0]
+    me = place_of(plan_ref)
     quadratic = jnp.sum(sums[0][...] + sums[1][...] + sums[2][...] + sums[3][...])
     ratio = jnp.full((8, 128), F32(KL_BOUND * elements)) / quadratic
     clip_factor = jnp.max(jnp.minimum(F32(1.0), jnp.sqrt(ratio)))
@@ -466,7 +474,7 @@
     for far in range(4):
         for slot in range(slots):
             at = far * slots + slot
-            block = block_in_slot(assign_ref, (me ^ far) * slots + slot)
+            block = plan_ref[(me ^ far) * slots + slot]
             out_ref[at] = (clip_factor * rows[far][slot].astype(F32)).astype(BF16)
             copies.append(pltpu.make_async_copy(out_ref.at[at], out_hbm.at[0, block], sems.at[at]))
             copies[-1].start()
@@ -474,16 +482,16 @@
         copy.wait()
 
 
-def clip(me, assign, sums, rows, shape, slots, elements):
+def clip(plan, sums, rows, shape, slots, elements):
     return call(
         functools.partial(clip_kernel, slots, elements),
         jax.ShapeDtypeStruct(shape, BF16),
-        [IN_SMEM, IN_SMEM] + [IN_VMEM] * (len(sums) + len(rows)),
+        [IN_SMEM] + [IN_VMEM] * (len(sums) + len(rows)),
         ANYWHERE,
         "clip",
         scratch=[pltpu.VMEM(shape[1:], BF16), pltpu.SemaphoreType.DMA((shape[1],))],
         moved=4 * shape[1] * shape[2] * shape[3],
-    )(me, assign, *sums, *rows)
+    )(plan, *sums, *rows)
 
 
 def after_kernel(value_ref, landed_ref, out_ref):
@@ -516,20 +524,24 @@
 
 
 def exchange_four(stats, grad, due, cost, assign, stale):
-    me = lax.axis_index("fsdp").astype(jnp.int32).reshape(1)
     slots = assign.shape[1] // 4
-    near, far2, far3 = pack_stats(me, assign, stats, slots)
+    plan = plan_of(assign[0])
+    near, far2, far3 = pack_stats(plan, stats, slots)
     received = [partner_of(near, "fsdp", 1), partner_of(far2, "fsdp", 2), partner_of(far3, "fsdp", 3)]
-    sent = pack_grad(me, assign, grad, slots)
-    pieces = [partner_of(piece, "fsdp", far) for far, piece in enumerate(sent, 1)]
-    root, factor = roots(me, assign, due, cost, stats, received, stale, slots)
-    solved, total = products(slots, me, assign, root, factor, grad, pieces)
-    rows = [solved[0]] + [partner_of(solved[far], "fsdp", far) for far in (1, 2, 3)]
+    own_grad, *sent = pack_grad(plan, grad, slots)
+    grad1, grad2, grad3 = [partner_of(piece, "fsdp", far) for far, piece in enumerate(sent, 1)]
+    root, factor = roots(plan, due, cost, stats, received, stale, slots)
+    far_root, near_root, far, near = start_product(plan, root, own_grad, grad1)
+    out2, out3 = finish_product(far_root, far, factor, grad2, grad3)
+    own, out1, total = finish_product(
+        near_root, near, factor, grad2, grad3, own_grad, grad1, out2, out3
+    )
+    rows = [own] + [partner_of(out, "fsdp", far) for far, out in enumerate((out1, out2, out3), 1)]
     total = sum_over(total, "dp")
-    sums = [total, partner_of(after(total, rows[1]), "fsdp", 1)]
+    sums = [total, partner_of(after(total, rows[2]), "fsdp", 1)]
     sums += [partner_of(total, "fsdp", far) for far in (2, 3)]
     elements = lax.axis_size("dp") * assign.shape[1] * stats.shape[3] * grad.shape[3]
-    return clip(me, assign, sums, rows, grad.shape, slots, elements)
+    return clip(plan, sums, rows, grad.shape, slots, elements)
 
 
 def solution(mesh):

time: 68.7 us -> 64.3 us (0.936)
  Pallas kernels: 14.2 us -> 5.98 us
  waiting for transfers between devices: 25.7 us -> 30.5 us
  starting transfers between devices: 26.6 us -> 25.5 us
  other arithmetic: 0.01 us -> 0.84 us
  local copies, waits for them, and re-layouts: 1.98 us -> 1.24 us
    pallas_call x1, Pallas kernels: 8.87 us -> 0.68 us  [roots(): call(functools.partial(root_kernel, slots), (jax.ShapeDtypeStruct((slots,...]
    ppermute x12, waiting for transfers between devices: 24.1 us -> 29 us  [partner_of(): return lax.ppermute(value, axis, [(i, i ^ far) for i in range(count)])]
    ppermute x12, starting transfers between devices: 23.4 us -> 22.3 us  [partner_of(): return lax.ppermute(value, axis, [(i, i ^ far) for i in range(count)])]
    reduce_sum x0 -> x1, other arithmetic: none -> 0.83 us  [plan_of(): source = jnp.sum(jnp.where(table_row[None, :] == slots, blocks, 0), axis=1)]
    unnamed x12 -> x10, local copies, waits for them, and re-layouts: 1.98 us -> 1.24 us
    pallas_call x3 -> x4, Pallas kernels: 2.81 us -> 2.83 us  [the longest x2 1.11 us: finish_product(): call(finish_kernel, shapes, [IN_VMEM] * (5 + len(others)), (IN_VMEM,) * l...]
  transfers between devices with their start and end apart: 15 -> 15, of which waited for: 7 -> 8; matrix products, arithmetic and copies ran while one was open for 0% -> 0% of each run, Pallas kernels for 14% -> 5%
where the time goes in v3:
time: 64.3 us; the launch traced here: 64.2 us
  waiting for transfers between devices  30.5 us (47%)
  starting transfers between devices  25.5 us (40%)
  Pallas kernels  5.98 us (9%)
  local copies, waits for them, and re-layouts  1.24 us (2%)
  other arithmetic  0.84 us (1%)
    ppermute x12, waiting for transfers between devices, partner_of(): return lax.ppermute(value, axis, [(i, i ^ far) for i in range(count)])  29 us
    ppermute x12, starting transfers between devices, partner_of(): return lax.ppermute(value, axis, [(i, i ^ far) for i in range(count)])  22.3 us
    ppermute x3, starting transfers between devices, sum_over(): lax.ppermute(value, axis, [(i, (i + shift) % count) for i in range(count)])  3.19 us
    pallas_call x1, Pallas kernels, clip(): call(functools.partial(clip_kernel, slots, elements), jax.ShapeDtypeStruc...  1.76 us
    ppermute x3, waiting for transfers between devices, sum_over(): lax.ppermute(value, axis, [(i, (i + shift) % count) for i in range(count)])  1.51 us
  transfers between devices with their start and end apart: 15, of which 8 were waited for; matrix products, arithmetic and copies ran while one was open for 0% of the time, Pallas kernels for 5%

profile of v3, /device:TPU:0, one launch (start us, length us, event | category | flops | bytes accessed | tf_op | source)
XLA Modules:
  0.0 64.2 jit_solution(409272776786190845)
XLA Ops:
  0.0 0.0 copy-start
  0.0 0.8 %select_reduce_fusion = s32[9]{0:T(128)S(1)} fusion(s32[8]{0:T(128)} %bitcast.1), kind=kLoop, calls=%fused_computation.1 | loop fusion | flops 207 | bytes 68 | tf_op jit(solution)/shard_map/reduce_sum | solution.py:113
  0.8 0.0 copy-start.1
  0.8 1.2 %copy-done.1 = bf16[1,8,128,512]{3,2,1,0:T(8,128)(2,1)S(1)} copy-done((bf16[1,8,128,512]{3,2,1,0:T(8,128)(2,1)S(1)}, bf16[1,8,128,512]{3,2,1,0:T(8,128)(2,1)}, u32[]{:S(2)}) %copy-start.1) | copy-done | bytes 1048600
  2.1 0.0 copy-start.2
  2.1 0.7 %pack_stats.1 = (bf16[2,128,384]{2,1,0:T(8,128)(2,1)S(1)}, bf16[272,128]{1,0:T(8,128)(2,1)S(1)}, bf16[272,128]{1,0:T(8,128)(2,1)S(1)}) custom-call(s32[9]{0:T(128)S(1)} %compare_select_fusion.plan_ref, bf16[1,8,128,512]{3,2,1,0:T(8,128)(2,1)S(1)} %copy-done.1), custom_call_target="tpu_custom_call" | custom-call | bytes 2097152 | tf_op jit(solution)/shard_map/pack_stats/pallas_call | solution.py:188
  2.8 3.1 %collective-permute-start = (bf16[2,128,384]{2,1,0:T(8,128)(2,1)S(1)}, bf16[2,128,384]{2,1,0:T(8,128)(2,1)S(1)}, u32[]{:S(2)}, u32[]{:S(2)}) collective-permute-start(bf16[2,128,384]{2,1,0:T(8,128)(2,1)S(1)} %get-tuple-element.23), channel_id=1, source_target_pairs={{0,4},{4,0},{8,12},{12,8},{1,5},{5,1},{9,13},{13,9},{2,6},{6,2},{1... | collective-permute-start | bytes 589832 | tf_op jit(solution)/shard_map/ppermute | solution.py:513
  5.9 2.6 %collective-permute-start.1 = (bf16[272,128]{1,0:T(8,128)(2,1)S(1)}, bf16[272,128]{1,0:T(8,128)(2,1)S(1)}, u32[]{:S(2)}, u32[]{:S(2)}) collective-permute-start(bf16[272,128]{1,0:T(8,128)(2,1)S(1)} %get-tuple-element.24), channel_id=1, source_target_pairs={{0,8},{4,12},{8,0},{12,4},{1,9},{5,13},{9,1},{13,5},{2,10},{6,14},... | collective-permute-start | bytes 208904 | tf_op jit(solution)/shard_map/ppermute | solution.py:513
  8.5 0.0 collective-permute-start.2
  8.5 0.0 copy-done
  8.5 0.6 pack_grad.1
  9.1 1.0 %collective-permute-start.3 = (bf16[2,128,512]{2,1,0:T(8,128)(2,1)S(1)}, bf16[2,128,512]{2,1,0:T(8,128)(2,1)S(1)}, u32[]{:S(2)}, u32[]{:S(2)}) collective-permute-start(bf16[2,128,512]{2,1,0:T(8,128)(2,1)S(1)} %get-tuple-element.28), channel_id=1, source_target_pairs={{0,4},{4,0},{8,12},{12,8},{1,5},{5,1},{9,13},{13,9},{2,6},{6,2},{1... | collective-permute-start | bytes 786440 | tf_op jit(solution)/shard_map/ppermute | solution.py:513
  10.0 0.0 copy-start.3
  10.1 0.0 copy-start.4
  10.1 3.5 %collective-permute-start.4 = (bf16[2,128,512]{2,1,0:T(8,128)(2,1)S(1)}, bf16[2,128,512]{2,1,0:T(8,128)(2,1)S(1)}, u32[]{:S(2)}, u32[]{:S(2)}) collective-permute-start(bf16[2,128,512]{2,1,0:T(8,128)(2,1)S(1)} %get-tuple-element.32), channel_id=1, source_target_pairs={{0,8},{4,12},{8,0},{12,4},{1,9},{5,13},{9,1},{13,5},{2,10},{6,14},... | collective-permute-start | bytes 786440 | tf_op jit(solution)/shard_map/ppermute | solution.py:513
  13.5 0.0 collective-permute-done.1.far2_ref
  13.5 1.6 %collective-permute-start.5 = (bf16[2,128,512]{2,1,0:T(8,128)(2,1)S(1)}, bf16[2,128,512]{2,1,0:T(8,128)(2,1)S(1)}, u32[]{:S(2)}, u32[]{:S(2)}) collective-permute-start(bf16[2,128,512]{2,1,0:T(8,128)(2,1)S(1)} %get-tuple-element.33), channel_id=1, source_target_pairs={{0,12},{4,8},{8,4},{12,0},{1,13},{5,9},{9,5},{13,1},{2,14},{6,10},... | collective-permute-start | bytes 786440 | tf_op jit(solution)/shard_map/ppermute | solution.py:513
  15.1 2.0 %collective-permute-done.2.far3_ref = bf16[272,128]{1,0:T(8,128)(2,1)S(1)} collective-permute-done((bf16[272,128]{1,0:T(8,128)(2,1)S(1)}, bf16[272,128]{1,0:T(8,128)(2,1)S(1)}, u32[]{:S(2)}, u32[]{:S(2)}) %collective-permute-start.2) | collective-permute-done | bytes 69664 | tf_op jit(solution)/shard_map/ppermute | solution.py:513
  17.1 0.0 collective-permute-done.near_ref
  17.1 0.0 copy-done.2
  17.1 0.0 copy-done.3
  17.2 0.0 copy-done.4
  17.2 0.7 %roots.1 = (bf16[2,512,512]{2,1,0:T(8,128)(2,1)S(1)}, f32[2,8,128]{2,1,0:T(8,128)S(1)}) custom-call(s32[9]{0:T(128)S(1)} %compare_select_fusion.plan_ref, s32[1,8]{1,0:T(1,128)S(1)} %copy-done.3, s32[1,8]{1,0:T(1,128)S(1)} %copy-done.4, bf16[1,8,128,512]{3,2,1,0:T(8,128)(2,1)S(1)} %copy-done.1, bf16[2,128,384]{2,1,0:T(8,128)(2,1)S(1)} %collective-permute-done.near_ref, ...), custom_call_target="tpu_custom_call" | custom-call | flops 4831838208 | bytes 3145728 | tf_op jit(solution)/shard_map/roots/pallas_call | solution.py:362
  17.8 7.1 %collective-permute-done.3.grad1_ref.rest_1_ = bf16[2,128,512]{2,1,0:T(8,128)(2,1)S(1)} collective-permute-done((bf16[2,128,512]{2,1,0:T(8,128)(2,1)S(1)}, bf16[2,128,512]{2,1,0:T(8,128)(2,1)S(1)}, u32[]{:S(2)}, u32[]{:S(2)}) %collective-permute-start.3) | collective-permute-done | bytes 262176 | tf_op jit(solution)/shard_map/ppermute | solution.py:513
  24.9 1.1 %start_product.1 = (bf16[2,256,256]{2,1,0:T(8,128)(2,1)S(1)}, bf16[2,256,256]{2,1,0:T(8,128)(2,1)S(1)}, f32[2,256,512]{2,1,0:T(8,128)S(1)}, f32[2,256,512]{2,1,0:T(8,128)S(1)}) custom-call(s32[9]{0:T(128)S(1)} %compare_select_fusion.plan_ref, bf16[2,512,512]{2,1,0:T(8,128)(2,1)S(1)} %get-tuple-element.26.root_ref, ...), custom_call_target="tpu_custom_call" | custom-call | flops 268435456 | bytes 2097152 | tf_op jit(solution)/shard_map/start_product/pallas_call | solution.py:414
  26.0 7.0 %collective-permute-done.4.grad2_ref = bf16[2,128,512]{2,1,0:T(8,128)(2,1)S(1)} collective-permute-done((bf16[2,128,512]{2,1,0:T(8,128)(2,1)S(1)}, bf16[2,128,512]{2,1,0:T(8,128)(2,1)S(1)}, u32[]{:S(2)}, u32[]{:S(2)}) %collective-permute-start.4) | collective-permute-done | bytes 262176 | tf_op jit(solution)/shard_map/ppermute | solution.py:513
  33.0 0.0 collective-permute-done.5.grad3_ref
  33.0 0.3 far_product.1
  33.3 6.0 %collective-permute-start.9 = (bf16[2,128,512]{2,1,0:T(8,128)(2,1)S(1)}, bf16[2,128,512]{2,1,0:T(8,128)(2,1)S(1)}, u32[]{:S(2)}, u32[]{:S(2)}) collective-permute-start(bf16[2,128,512]{2,1,0:T(8,128)(2,1)S(1)} %get-tuple-element.36.rest_2_), channel_id=1, source_target_pairs={{0,8},{4,12},{8,0},{12,4},{1,9},{5,13},{9,1},{13,5},{2,10},{6,14},... | collective-permute-start | bytes 786440 | tf_op jit(solution)/shard_map/ppermute | solution.py:513
  39.3 0.8 %near_product.1 = (bf16[2,128,512]{2,1,0:T(8,128)(2,1)S(1)}, bf16[2,128,512]{2,1,0:T(8,128)(2,1)S(1)}, f32[8,128]{1,0:T(8,128)S(1)}) custom-call(bf16[2,256,256]{2,1,0:T(8,128)(2,1)S(1)} %get-tuple-element.29.root_ref, f32[2,256,512]{2,1,0:T(8,128)S(1)} %get-tuple-element.30.begun_ref, f32[2,8,128]{2,1,0:T(8,128)S(1)} %get-tuple-element.31.factor_ref, ...), custom_call_target="tpu_custom_call" | custom-call | flops 134217728 | bytes 2097152 | tf_op jit(solution)/shard_map/near_product/pallas_call | solution.py:456
  40.1 0.1 collective-permute-start.13
  40.2 2.1 %collective-permute-start.14 = (bf16[2,128,512]{2,1,0:T(8,128)(2,1)S(1)}, bf16[2,128,512]{2,1,0:T(8,128)(2,1)S(1)}, u32[]{:S(2)}, u32[]{:S(2)}) collective-permute-start(bf16[2,128,512]{2,1,0:T(8,128)(2,1)S(1)} %get-tuple-element.37.rest_3_), channel_id=1, source_target_pairs={{0,12},{4,8},{8,4},{12,0},{1,13},{5,9},{9,5},{13,1},{2,14},{6,10},... | collective-permute-start | bytes 786440 | tf_op jit(solution)/shard_map/ppermute | solution.py:513
  42.3 0.1 collective-permute-start.8
  42.4 1.4 %collective-permute-start.7 = (f32[8,128]{1,0:T(8,128)S(1)}, f32[8,128]{1,0:T(8,128)S(1)}, u32[]{:S(2)}, u32[]{:S(2)}) collective-permute-start(f32[8,128]{1,0:T(8,128)S(1)} %get-tuple-element.38), channel_id=1, source_target_pairs={{0,2},{1,3},{2,0},{3,1},{4,6},{5,7},{6,4},{7,5},{8,10},{9,11},{10,... | collective-permute-start | bytes 12296 | tf_op jit(solution)/shard_map/ppermute | solution.py:520
  43.8 0.0 collective-permute-done.8
  43.8 1.7 %collective-permute-start.6 = (f32[8,128]{1,0:T(8,128)S(1)}, f32[8,128]{1,0:T(8,128)S(1)}, u32[]{:S(2)}, u32[]{:S(2)}) collective-permute-start(f32[8,128]{1,0:T(8,128)S(1)} %get-tuple-element.38), channel_id=1, source_target_pairs={{0,1},{1,2},{2,3},{3,0},{4,5},{5,6},{6,7},{7,4},{8,9},{9,10},{10,1... | collective-permute-start | bytes 12296 | tf_op jit(solution)/shard_map/ppermute | solution.py:520
  45.5 0.5 collective-permute-done.7
  46.0 1.0 %collective-permute-done.6 = f32[8,128]{1,0:T(8,128)S(1)} collective-permute-done((f32[8,128]{1,0:T(8,128)S(1)}, f32[8,128]{1,0:T(8,128)S(1)}, u32[]{:S(2)}, u32[]{:S(2)}) %collective-permute-start.6) | collective-permute-done | bytes 4128 | tf_op jit(solution)/shard_map/ppermute | solution.py:520
  47.0 1.7 %collective-permute-start.12 = (f32[8,128]{1,0:T(8,128)S(1)}, f32[8,128]{1,0:T(8,128)S(1)}, u32[]{:S(2)}, u32[]{:S(2)}) collective-permute-start(f32[8,128]{1,0:T(8,128)S(1)} %add_add_fusion.value_ref.rest_0_), channel_id=1, source_target_pairs={{0,12},{4,8},{8,4},{12,0},{1,13},{5,9},{9,5},{13,1},{2,14},{6,10},... | collective-permute-start | bytes 12296 | tf_op jit(solution)/shard_map/ppermute | solution.py:513
  48.7 0.7 %collective-permute-start.11 = (f32[8,128]{1,0:T(8,128)S(1)}, f32[8,128]{1,0:T(8,128)S(1)}, u32[]{:S(2)}, u32[]{:S(2)}) collective-permute-start(f32[8,128]{1,0:T(8,128)S(1)} %add_add_fusion.value_ref.rest_0_), channel_id=1, source_target_pairs={{0,8},{4,12},{8,0},{12,4},{1,9},{5,13},{9,1},{13,5},{2,10},{6,14},... | collective-permute-start | bytes 12296 | tf_op jit(solution)/shard_map/ppermute | solution.py:513
  49.4 3.5 %collective-permute-done.9.landed_ref.rest_6_ = bf16[2,128,512]{2,1,0:T(8,128)(2,1)S(1)} collective-permute-done((bf16[2,128,512]{2,1,0:T(8,128)(2,1)S(1)}, bf16[2,128,512]{2,1,0:T(8,128)(2,1)S(1)}, u32[]{:S(2)}, u32[]{:S(2)}) %collective-permute-start.9) | collective-permute-done | bytes 262176 | tf_op jit(solution)/shard_map/ppermute | solution.py:513
  52.9 0.0 collective-permute-start.10
  52.9 5.7 %collective-permute-done.12.rest_3_ = f32[8,128]{1,0:T(8,128)S(1)} collective-permute-done((f32[8,128]{1,0:T(8,128)S(1)}, f32[8,128]{1,0:T(8,128)S(1)}, u32[]{:S(2)}, u32[]{:S(2)}) %collective-permute-start.12) | collective-permute-done | bytes 4128 | tf_op jit(solution)/shard_map/ppermute | solution.py:513
  58.6 3.8 %collective-permute-done.11.rest_2_ = f32[8,128]{1,0:T(8,128)S(1)} collective-permute-done((f32[8,128]{1,0:T(8,128)S(1)}, f32[8,128]{1,0:T(8,128)S(1)}, u32[]{:S(2)}, u32[]{:S(2)}) %collective-permute-start.11) | collective-permute-done | bytes 4128 | tf_op jit(solution)/shard_map/ppermute | solution.py:513
  62.4 0.0 collective-permute-done.13.rest_5_
  62.4 0.0 collective-permute-done.14.rest_7_
  62.4 0.0 collective-permute-done.10.rest_1_
  62.4 1.8 %clip.1 = bf16[1,8,128,512]{3,2,1,0:T(8,128)(2,1)} custom-call(s32[9]{0:T(128)S(1)} %compare_select_fusion.plan_ref, f32[8,128]{1,0:T(8,128)S(1)} %add_add_fusion.value_ref.rest_0_, f32[8,128]{1,0:T(8,128)S(1)} %collective-permute-done.10.rest_1_, f32[8,128]{1,0:T(8,128)S(1)} %collective-permute-done.11.rest_2_, ...), custom_call_target="tpu_custom_call" | custom-call | bytes 2097152 | tf_op jit(solution)/shard_map/clip/pallas_call | solution.py:486
  (3 shorter events, 0.0 us)
Async XLA Ops:
  0.0 8.5 %copy-start = (bf16[1,8,128,512]{3,2,1,0:T(8,128)(2,1)S(1)}, bf16[1,8,128,512]{3,2,1,0:T(8,128)(2,1)}, u32[]{:S(2)}) copy-start(bf16[1,8,128,512]{3,2,1,0:T(8,128)(2,1)} %grad_ref.1) | copy-start | bytes 3145732
  0.8 1.2 %copy-start.1 = (bf16[1,8,128,512]{3,2,1,0:T(8,128)(2,1)S(1)}, bf16[1,8,128,512]{3,2,1,0:T(8,128)(2,1)}, u32[]{:S(2)}) copy-start(bf16[1,8,128,512]{3,2,1,0:T(8,128)(2,1)} %stats_ref.3) | copy-start | bytes 3145732
  2.1 15.1 %copy-start.2 = (bf16[1,2,512,512]{3,2,1,0:T(8,128)(2,1)S(1)}, bf16[1,2,512,512]{3,2,1,0:T(8,128)(2,1)}, u32[]{:S(2)}) copy-start(bf16[1,2,512,512]{3,2,1,0:T(8,128)(2,1)} %stale_ref.1) | copy-start | bytes 3145732
  2.8 14.4 %collective-permute-start = (bf16[2,128,384]{2,1,0:T(8,128)(2,1)S(1)}, bf16[2,128,384]{2,1,0:T(8,128)(2,1)S(1)}, u32[]{:S(2)}, u32[]{:S(2)}) collective-permute-start(bf16[2,128,384]{2,1,0:T(8,128)(2,1)S(1)} %get-tuple-element.23), channel_id=1, source_target_pairs={{0,4},{4,0},{8,12},{12,8},{1,5},{5,1},{9,13},{13,9},{2,6},{6,2},{1... | collective-permute-start | bytes 589832 | tf_op jit(solution)/shard_map/ppermute | solution.py:513
  5.9 7.7 %collective-permute-start.1 = (bf16[272,128]{1,0:T(8,128)(2,1)S(1)}, bf16[272,128]{1,0:T(8,128)(2,1)S(1)}, u32[]{:S(2)}, u32[]{:S(2)}) collective-permute-start(bf16[272,128]{1,0:T(8,128)(2,1)S(1)} %get-tuple-element.24), channel_id=1, source_target_pairs={{0,8},{4,12},{8,0},{12,4},{1,9},{5,13},{9,1},{13,5},{2,10},{6,14},... | collective-permute-start | bytes 208904 | tf_op jit(solution)/shard_map/ppermute | solution.py:513
  8.5 8.7 %collective-permute-start.2 = (bf16[272,128]{1,0:T(8,128)(2,1)S(1)}, bf16[272,128]{1,0:T(8,128)(2,1)S(1)}, u32[]{:S(2)}, u32[]{:S(2)}) collective-permute-start(bf16[272,128]{1,0:T(8,128)(2,1)S(1)} %get-tuple-element.25), channel_id=1, source_target_pairs={{0,12},{4,8},{8,4},{12,0},{1,13},{5,9},{9,5},{13,1},{2,14},{6,10},... | collective-permute-start | bytes 208904 | tf_op jit(solution)/shard_map/ppermute | solution.py:513
  9.1 15.8 %collective-permute-start.3 = (bf16[2,128,512]{2,1,0:T(8,128)(2,1)S(1)}, bf16[2,128,512]{2,1,0:T(8,128)(2,1)S(1)}, u32[]{:S(2)}, u32[]{:S(2)}) collective-permute-start(bf16[2,128,512]{2,1,0:T(8,128)(2,1)S(1)} %get-tuple-element.28), channel_id=1, source_target_pairs={{0,4},{4,0},{8,12},{12,8},{1,5},{5,1},{9,13},{13,9},{2,6},{6,2},{1... | collective-permute-start | bytes 786440 | tf_op jit(solution)/shard_map/ppermute | solution.py:513
  10.0 7.1 %copy-start.3 = (s32[1,8]{1,0:T(1,128)S(1)}, s32[1,8]{1,0:T(1,128)}, u32[]{:S(2)}) copy-start(s32[1,8]{1,0:T(1,128)} %due_ref.1) | copy-start | bytes 100
  10.1 7.1 %copy-start.4 = (s32[1,8]{1,0:T(1,128)S(1)}, s32[1,8]{1,0:T(1,128)}, u32[]{:S(2)}) copy-start(s32[1,8]{1,0:T(1,128)} %cost_ref.1) | copy-start | bytes 100
  10.1 22.9 %collective-permute-start.4 = (bf16[2,128,512]{2,1,0:T(8,128)(2,1)S(1)}, bf16[2,128,512]{2,1,0:T(8,128)(2,1)S(1)}, u32[]{:S(2)}, u32[]{:S(2)}) collective-permute-start(bf16[2,128,512]{2,1,0:T(8,128)(2,1)S(1)} %get-tuple-element.32), channel_id=1, source_target_pairs={{0,8},{4,12},{8,0},{12,4},{1,9},{5,13},{9,1},{13,5},{2,10},{6,14},... | collective-permute-start | bytes 786440 | tf_op jit(solution)/shard_map/ppermute | solution.py:513
  13.5 19.5 %collective-permute-start.5 = (bf16[2,128,512]{2,1,0:T(8,128)(2,1)S(1)}, bf16[2,128,512]{2,1,0:T(8,128)(2,1)S(1)}, u32[]{:S(2)}, u32[]{:S(2)}) collective-permute-start(bf16[2,128,512]{2,1,0:T(8,128)(2,1)S(1)} %get-tuple-element.33), channel_id=1, source_target_pairs={{0,12},{4,8},{8,4},{12,0},{1,13},{5,9},{9,5},{13,1},{2,14},{6,10},... | collective-permute-start | bytes 786440 | tf_op jit(solution)/shard_map/ppermute | solution.py:513
  33.3 19.6 %collective-permute-start.9 = (bf16[2,128,512]{2,1,0:T(8,128)(2,1)S(1)}, bf16[2,128,512]{2,1,0:T(8,128)(2,1)S(1)}, u32[]{:S(2)}, u32[]{:S(2)}) collective-permute-start(bf16[2,128,512]{2,1,0:T(8,128)(2,1)S(1)} %get-tuple-element.36.rest_2_), channel_id=1, source_target_pairs={{0,8},{4,12},{8,0},{12,4},{1,9},{5,13},{9,1},{13,5},{2,10},{6,14},... | collective-permute-start | bytes 786440 | tf_op jit(solution)/shard_map/ppermute | solution.py:513
  40.1 22.3 %collective-permute-start.13 = (bf16[2,128,512]{2,1,0:T(8,128)(2,1)S(1)}, bf16[2,128,512]{2,1,0:T(8,128)(2,1)S(1)}, u32[]{:S(2)}, u32[]{:S(2)}) collective-permute-start(bf16[2,128,512]{2,1,0:T(8,128)(2,1)S(1)} %get-tuple-element.40), channel_id=1, source_target_pairs={{0,4},{4,0},{8,12},{12,8},{1,5},{5,1},{9,13},{13,9},{2,6},{6,2},{1... | collective-permute-start | bytes 786440 | tf_op jit(solution)/shard_map/ppermute | solution.py:513
  40.2 22.2 %collective-permute-start.14 = (bf16[2,128,512]{2,1,0:T(8,128)(2,1)S(1)}, bf16[2,128,512]{2,1,0:T(8,128)(2,1)S(1)}, u32[]{:S(2)}, u32[]{:S(2)}) collective-permute-start(bf16[2,128,512]{2,1,0:T(8,128)(2,1)S(1)} %get-tuple-element.37.rest_3_), channel_id=1, source_target_pairs={{0,12},{4,8},{8,4},{12,0},{1,13},{5,9},{9,5},{13,1},{2,14},{6,10},... | collective-permute-start | bytes 786440 | tf_op jit(solution)/shard_map/ppermute | solution.py:513
  42.3 1.5 %collective-permute-start.8 = (f32[8,128]{1,0:T(8,128)S(1)}, f32[8,128]{1,0:T(8,128)S(1)}, u32[]{:S(2)}, u32[]{:S(2)}) collective-permute-start(f32[8,128]{1,0:T(8,128)S(1)} %get-tuple-element.38), channel_id=1, source_target_pairs={{0,3},{1,0},{2,1},{3,2},{4,7},{5,4},{6,5},{7,6},{8,11},{9,8},{10,9... | collective-permute-start | bytes 12296 | tf_op jit(solution)/shard_map/ppermute | solution.py:520
  42.4 3.6 %collective-permute-start.7 = (f32[8,128]{1,0:T(8,128)S(1)}, f32[8,128]{1,0:T(8,128)S(1)}, u32[]{:S(2)}, u32[]{:S(2)}) collective-permute-start(f32[8,128]{1,0:T(8,128)S(1)} %get-tuple-element.38), channel_id=1, source_target_pairs={{0,2},{1,3},{2,0},{3,1},{4,6},{5,7},{6,4},{7,5},{8,10},{9,11},{10,... | collective-permute-start | bytes 12296 | tf_op jit(solution)/shard_map/ppermute | solution.py:520
  43.8 3.2 %collective-permute-start.6 = (f32[8,128]{1,0:T(8,128)S(1)}, f32[8,128]{1,0:T(8,128)S(1)}, u32[]{:S(2)}, u32[]{:S(2)}) collective-permute-start(f32[8,128]{1,0:T(8,128)S(1)} %get-tuple-element.38), channel_id=1, source_target_pairs={{0,1},{1,2},{2,3},{3,0},{4,5},{5,6},{6,7},{7,4},{8,9},{9,10},{10,1... | collective-permute-start | bytes 12296 | tf_op jit(solution)/shard_map/ppermute | solution.py:520
  47.0 11.6 %collective-permute-start.12 = (f32[8,128]{1,0:T(8,128)S(1)}, f32[8,128]{1,0:T(8,128)S(1)}, u32[]{:S(2)}, u32[]{:S(2)}) collective-permute-start(f32[8,128]{1,0:T(8,128)S(1)} %add_add_fusion.value_ref.rest_0_), channel_id=1, source_target_pairs={{0,12},{4,8},{8,4},{12,0},{1,13},{5,9},{9,5},{13,1},{2,14},{6,10},... | collective-permute-start | bytes 12296 | tf_op jit(solution)/shard_map/ppermute | solution.py:513
  48.7 13.7 %collective-permute-start.11 = (f32[8,128]{1,0:T(8,128)S(1)}, f32[8,128]{1,0:T(8,128)S(1)}, u32[]{:S(2)}, u32[]{:S(2)}) collective-permute-start(f32[8,128]{1,0:T(8,128)S(1)} %add_add_fusion.value_ref.rest_0_), channel_id=1, source_target_pairs={{0,8},{4,12},{8,0},{12,4},{1,9},{5,13},{9,1},{13,5},{2,10},{6,14},... | collective-permute-start | bytes 12296 | tf_op jit(solution)/shard_map/ppermute | solution.py:513
  52.9 9.5 %collective-permute-start.10 = (f32[8,128]{1,0:T(8,128)S(1)}, f32[8,128]{1,0:T(8,128)S(1)}, u32[]{:S(2)}, u32[]{:S(2)}) collective-permute-start(f32[8,128]{1,0:T(8,128)S(1)} %after.1), channel_id=1, source_target_pairs={{0,4},{4,0},{8,12},{12,8},{1,5},{5,1},{9,13},{13,9},{2,6},{6,2},{1... | collective-permute-start | bytes 12296 | tf_op jit(solution)/shard_map/ppermute | solution.py:513

commit v4 on v3

--- a/solution.py
+++ b/solution.py
@@ -9,6 +9,7 @@
 
 KL_BOUND = 1.0
 VMEM_BYTES = 40 * 2**20
+PACK_VMEM_BYTES = int(59 * 2**20)
 DIAGONAL_ROWS = 16
 F32 = jnp.float32
 BF16 = jnp.bfloat16
@@ -88,14 +89,14 @@
     return (clip_factor * owner_rows.astype(F32)).astype(BF16)[None]
 
 
-def call(kernel, out_shape, in_specs, out_specs, name, scratch=(), flops=0, moved=0):
+def call(kernel, out_shape, in_specs, out_specs, name, scratch=(), flops=0, moved=0, vmem=VMEM_BYTES):
     return pl.pallas_call(
         kernel,
         out_shape=out_shape,
         in_specs=in_specs,
         out_specs=out_specs,
         scratch_shapes=list(scratch),
-        compiler_params=pltpu.CompilerParams(vmem_limit_bytes=VMEM_BYTES),
+        compiler_params=pltpu.CompilerParams(vmem_limit_bytes=vmem),
         cost_estimate=pl.CostEstimate(flops=flops, bytes_accessed=moved, transcendentals=0),
         name=name,
     )
@@ -106,12 +107,11 @@
 ANYWHERE = pl.BlockSpec(memory_space=pl.ANY)
 
 
-def plan_of(table_row):
+def plan_of(table_row, place):
     total = table_row.shape[0]
     blocks = lax.broadcasted_iota(jnp.int32, (total + 1, total), 1)
     slots = lax.broadcasted_iota(jnp.int32, (total + 1, total), 0)
     source = jnp.sum(jnp.where(table_row[None, :] == slots, blocks, 0), axis=1)
-    place = lax.axis_index("fsdp").astype(jnp.int32)
     return jnp.where(jnp.arange(total + 1) == total, place, source)
 
 
@@ -147,15 +147,36 @@
     return jnp.concatenate([top, jnp.where(lane < half, turned[half:, :], last)], axis=0)
 
 
-def pack_stats_kernel(slots, plan_ref, stats_ref, near_ref, far2_ref, far3_ref):
-    me = place_of(plan_ref)
+def block_in_slot(assign_ref, slot):
+    found = jnp.int32(0)
+    for block in range(assign_ref.shape[1]):
+        found = jnp.where(assign_ref[0, block] == slot, jnp.int32(block), found)
+    return found
+
+
+def pack_stats_kernel(
+    slots, me_ref, assign_hbm, stats_hbm, near_ref, far2_ref, far3_ref, assign_ref, stats_ref, sems
+):
+    blocks = stats_ref.shape[1]
+    table = pltpu.make_async_copy(assign_hbm, assign_ref, sems.at[blocks])
+    table.start()
+    copies = [
+        pltpu.make_async_copy(stats_hbm.at[0, block], stats_ref.at[0, block], sems.at[block])
+        for block in range(blocks)
+    ]
+    for copy in copies:
+        copy.start()
+    me = me_ref[0]
     width = stats_ref.shape[2]
+    table.wait()
+    for copy in copies:
+        copy.wait()
     half = width // 2
     odd = me % 2
     for far, out in ((2, far2_ref), (3, far3_ref)):
         diagonals = []
         for slot in range(slots):
-            block = plan_ref[(me ^ far) * slots + slot]
+            block = block_in_slot(assign_ref, (me ^ far) * slots + slot)
             between = stats_ref[0, block, :, tile_at(me ^ 1, width)].astype(F32)
             at = slot * width
             out[at : at + half, :] = jnp.where(
@@ -174,25 +195,31 @@
                 BF16
             )
     for slot in range(slots):
-        block = plan_ref[(me ^ 1) * slots + slot]
+        block = block_in_slot(assign_ref, (me ^ 1) * slots + slot)
         for place, other in enumerate((0, 2, 3)):
             near_ref[slot, :, place * width : (place + 1) * width] = stats_ref[
                 0, block, :, tile_at(me ^ other, width)
             ]
 
 
-def pack_stats(plan, stats, slots):
+def pack_stats(me, assign, stats, slots):
     width, order = stats.shape[2:]
     near = jax.ShapeDtypeStruct((slots, width, order - width), BF16)
     far = jax.ShapeDtypeStruct((slots * width + (slots + 1) // 2 * DIAGONAL_ROWS, width), BF16)
     return call(
         functools.partial(pack_stats_kernel, slots),
         (near, far, far),
-        [IN_SMEM, IN_VMEM],
+        [IN_SMEM, ANYWHERE, ANYWHERE],
         (IN_VMEM,) * 3,
         "pack_stats",
+        scratch=[
+            pltpu.SMEM(assign.shape, jnp.int32),
+            pltpu.VMEM(stats.shape, BF16),
+            pltpu.SemaphoreType.DMA((stats.shape[1] + 1,)),
+        ],
         moved=2 * stats.size * 2,
-    )(plan, stats)
+        vmem=PACK_VMEM_BYTES,
+    )(me, assign, stats)
 
 
 def pack_grad_kernel(slots, plan_ref, grad_ref, *outs):
@@ -221,8 +248,8 @@
     cost_ref,
     stats_ref,
     near_ref,
+    far3_ref,
     far2_ref,
-    far3_ref,
     stale_ref,
     root_ref,
     factor_ref,
@@ -423,7 +450,7 @@
     )(plan, root, own_grad, grad1)
 
 
-def finish_kernel(root_ref, begun_ref, factor_ref, grad2_ref, grad3_ref, *rest):
+def finish_kernel(root_ref, begun_ref, factor_ref, grad3_ref, grad2_ref, *rest):
     first_ref, second_ref = rest[-2:] if len(rest) == 2 else rest[-3:-1]
     slots, width, columns = first_ref.shape
     total = jnp.zeros((8, 128), F32)
@@ -461,7 +488,7 @@
         "near_product" if others else "far_product",
         flops=slots * 8 * width * width * columns,
         moved=slots * 16 * width * columns,
-    )(root, begun, factor, grad2, grad3, *others)
+    )(root, begun, factor, grad3, grad2, *others)
 
 
 def clip_kernel(slots, elements, plan_ref, *rest):
@@ -525,9 +552,10 @@
 
 def exchange_four(stats, grad, due, cost, assign, stale):
     slots = assign.shape[1] // 4
-    plan = plan_of(assign[0])
-    near, far2, far3 = pack_stats(plan, stats, slots)
-    received = [partner_of(near, "fsdp", 1), partner_of(far2, "fsdp", 2), partner_of(far3, "fsdp", 3)]
+    me = lax.axis_index("fsdp").astype(jnp.int32)
+    plan = plan_of(assign[0], me)
+    near, far2, far3 = pack_stats(me.reshape(1), assign, stats, slots)
+    received = [partner_of(near, "fsdp", 1), partner_of(far3, "fsdp", 3), partner_of(far2, "fsdp", 2)]
     own_grad, *sent = pack_grad(plan, grad, slots)
     grad1, grad2, grad3 = [partner_of(piece, "fsdp", far) for far, piece in enumerate(sent, 1)]
     root, factor = roots(plan, due, cost, stats, received, stale, slots)
@@ -538,7 +566,7 @@
     )
     rows = [own] + [partner_of(out, "fsdp", far) for far, out in enumerate((out1, out2, out3), 1)]
     total = sum_over(total, "dp")
-    sums = [total, partner_of(after(total, rows[2]), "fsdp", 1)]
+    sums = [total, partner_of(after(total, rows[3]), "fsdp", 1)]
     sums += [partner_of(total, "fsdp", far) for far in (2, 3)]
     elements = lax.axis_size("dp") * assign.shape[1] * stats.shape[3] * grad.shape[3]
     return clip(plan, sums, rows, grad.shape, slots, elements)

time: 64.3 us -> 61 us (0.949)
  waiting for transfers between devices: 30.5 us -> 23.7 us
  Pallas kernels: 5.98 us -> 9.75 us
    ppermute x12, waiting for transfers between devices: 29 us -> 22.3 us  [partner_of(): return lax.ppermute(value, axis, [(i, i ^ far) for i in range(count)])]
    pallas_call x1, Pallas kernels: 0.68 us -> 2.88 us  [roots(): call(functools.partial(root_kernel, slots), (jax.ShapeDtypeStruct((slots,...]
    pallas_call x1, Pallas kernels: 0.71 us -> 2.3 us  [pack_stats(): call(functools.partial(pack_stats_kernel, slots), (near, far, far), [IN_S...]
  transfers between devices with their start and end apart: 15 -> 15, of which waited for: 8 -> 7; matrix products, arithmetic and copies ran while one was open for 0% -> 1% of each run, Pallas kernels for 5% -> 9%
where the time goes in v4:
time: 61 us; the launch traced here: 60.8 us
  starting transfers between devices  25.3 us (41%)
  waiting for transfers between devices  23.7 us (39%)
  Pallas kernels  9.75 us (16%)
  local copies, waits for them, and re-layouts  1.23 us (2%)
  other arithmetic  0.75 us (1%)
    ppermute x12, waiting for transfers between devices, partner_of(): return lax.ppermute(value, axis, [(i, i ^ far) for i in range(count)])  22.3 us
    ppermute x12, starting transfers between devices, partner_of(): return lax.ppermute(value, axis, [(i, i ^ far) for i in range(count)])  22 us
    ppermute x3, starting transfers between devices, sum_over(): lax.ppermute(value, axis, [(i, (i + shift) % count) for i in range(count)])  3.25 us
    pallas_call x1, Pallas kernels, roots(): call(functools.partial(root_kernel, slots), (jax.ShapeDtypeStruct((slots,...  2.88 us
    pallas_call x1, Pallas kernels, pack_stats(): call(functools.partial(pack_stats_kernel, slots), (near, far, far), [IN_S...  2.3 us
    pallas_call x1, Pallas kernels, clip(): call(functools.partial(clip_kernel, slots, elements), jax.ShapeDtypeStruc...  1.76 us
    ppermute x3, waiting for transfers between devices, sum_over(): lax.ppermute(value, axis, [(i, (i + shift) % count) for i in range(count)])  1.37 us
    unnamed x10, local copies, waits for them, and re-layouts  1.23 us
  transfers between devices with their start and end apart: 15, of which 7 were waited for; matrix products, arithmetic and copies ran while one was open for 1% of the time, Pallas kernels for 9%

profile of v4, /device:TPU:0, one launch (start us, length us, event | category | flops | bytes accessed | tf_op | source)
XLA Modules:
  0.0 60.8 jit_solution(7230232765511285380)
XLA Ops:
  0.0 0.0 copy-start.1
  0.0 0.0 copy-start
  0.0 2.3 %pack_stats.1 = (bf16[2,128,384]{2,1,0:T(8,128)(2,1)}, bf16[272,128]{1,0:T(8,128)(2,1)}, bf16[272,128]{1,0:T(8,128)(2,1)}) custom-call(s32[1]{0:T(128)} %bitcast.1.me_ref, s32[1,8]{1,0:T(1,128)} %assign_hbm.1, bf16[1,8,128,512]{3,2,1,0:T(8,128)(2,1)} %stats_ref.1), custom_call_target="tpu_custom_call" | custom-call | bytes 2097152 | tf_op jit(solution)/shard_map/pack_stats/pallas_call | solution.py:209
  2.3 5.1 %collective-permute-start.1 = (bf16[272,128]{1,0:T(8,128)(2,1)}, bf16[272,128]{1,0:T(8,128)(2,1)S(1)}, u32[]{:S(2)}, u32[]{:S(2)}) collective-permute-start(bf16[272,128]{1,0:T(8,128)(2,1)} %get-tuple-element.24), channel_id=1, source_target_pairs={{0,12},{4,8},{8,4},{12,0},{1,13},{5,9},{9,5},{13,1},{2,14},{6,10},... | collective-permute-start | bytes 208904 | tf_op jit(solution)/shard_map/ppermute | solution.py:540
  7.4 0.0 collective-permute-start.2
  7.4 0.6 %collective-permute-start = (bf16[2,128,384]{2,1,0:T(8,128)(2,1)}, bf16[2,128,384]{2,1,0:T(8,128)(2,1)S(1)}, u32[]{:S(2)}, u32[]{:S(2)}) collective-permute-start(bf16[2,128,384]{2,1,0:T(8,128)(2,1)} %get-tuple-element.23), channel_id=1, source_target_pairs={{0,4},{4,0},{8,12},{12,8},{1,5},{5,1},{9,13},{13,9},{2,6},{6,2},{1... | collective-permute-start | bytes 589832 | tf_op jit(solution)/shard_map/ppermute | solution.py:540
  8.1 0.7 %select_reduce_fusion = s32[9]{0:T(128)S(1)} fusion(s32[8]{0:T(128)} %bitcast.2), kind=kLoop, calls=%fused_computation.1 | loop fusion | flops 207 | bytes 68 | tf_op jit(solution)/shard_map/reduce_sum | solution.py:114
  8.8 0.0 copy-done.1
  8.8 0.6 %pack_grad.1 = (bf16[2,128,512]{2,1,0:T(8,128)(2,1)S(1)}, bf16[2,128,512]{2,1,0:T(8,128)(2,1)S(1)}, bf16[2,128,512]{2,1,0:T(8,128)(2,1)S(1)}, bf16[2,128,512]{2,1,0:T(8,128)(2,1)S(1)}) custom-call(s32[9]{0:T(128)S(1)} %compare_select_fusion.plan_ref, bf16[1,8,128,512]{3,2,1,0:T(8,128)(2,1)S(1)} %copy-done.1), custom_call_target="tpu_custom_call" | custom-call | bytes 2097152 | tf_op jit(solution)/shard_map/pack_grad/pallas_call | solution.py:234
  9.4 1.5 %collective-permute-start.3 = (bf16[2,128,512]{2,1,0:T(8,128)(2,1)S(1)}, bf16[2,128,512]{2,1,0:T(8,128)(2,1)S(1)}, u32[]{:S(2)}, u32[]{:S(2)}) collective-permute-start(bf16[2,128,512]{2,1,0:T(8,128)(2,1)S(1)} %get-tuple-element.28), channel_id=1, source_target_pairs={{0,4},{4,0},{8,12},{12,8},{1,5},{5,1},{9,13},{13,9},{2,6},{6,2},{1... | collective-permute-start | bytes 786440 | tf_op jit(solution)/shard_map/ppermute | solution.py:540
  10.9 0.0 copy-start.3
  10.9 0.0 copy-start.4
  10.9 2.5 %collective-permute-start.4 = (bf16[2,128,512]{2,1,0:T(8,128)(2,1)S(1)}, bf16[2,128,512]{2,1,0:T(8,128)(2,1)S(1)}, u32[]{:S(2)}, u32[]{:S(2)}) collective-permute-start(bf16[2,128,512]{2,1,0:T(8,128)(2,1)S(1)} %get-tuple-element.32), channel_id=1, source_target_pairs={{0,12},{4,8},{8,4},{12,0},{1,13},{5,9},{9,5},{13,1},{2,14},{6,10},... | collective-permute-start | bytes 786440 | tf_op jit(solution)/shard_map/ppermute | solution.py:540
  13.4 0.0 collective-permute-done.1.far3_ref
  13.4 0.8 %collective-permute-start.5 = (bf16[2,128,512]{2,1,0:T(8,128)(2,1)S(1)}, bf16[2,128,512]{2,1,0:T(8,128)(2,1)S(1)}, u32[]{:S(2)}, u32[]{:S(2)}) collective-permute-start(bf16[2,128,512]{2,1,0:T(8,128)(2,1)S(1)} %get-tuple-element.33), channel_id=1, source_target_pairs={{0,8},{4,12},{8,0},{12,4},{1,9},{5,13},{9,1},{13,5},{2,10},{6,14},... | collective-permute-start | bytes 786440 | tf_op jit(solution)/shard_map/ppermute | solution.py:540
  14.1 0.0 collective-permute-done.2.far2_ref
  14.1 2.6 %collective-permute-done.near_ref = bf16[2,128,384]{2,1,0:T(8,128)(2,1)S(1)} collective-permute-done((bf16[2,128,384]{2,1,0:T(8,128)(2,1)}, bf16[2,128,384]{2,1,0:T(8,128)(2,1)S(1)}, u32[]{:S(2)}, u32[]{:S(2)}) %collective-permute-start) | collective-permute-done | bytes 196640 | tf_op jit(solution)/shard_map/ppermute | solution.py:540
  16.8 0.0 copy-done
  16.8 0.0 copy-done.3
  16.8 0.0 copy-done.4
  16.8 0.0 copy-start.2
  16.8 1.2 %copy-done.2 = bf16[1,2,512,512]{3,2,1,0:T(8,128)(2,1)S(1)} copy-done((bf16[1,2,512,512]{3,2,1,0:T(8,128)(2,1)S(1)}, bf16[1,2,512,512]{3,2,1,0:T(8,128)(2,1)}, u32[]{:S(2)}) %copy-start.2) | copy-done | bytes 1048600
  18.0 2.9 %roots.1 = (bf16[2,512,512]{2,1,0:T(8,128)(2,1)S(1)}, f32[2,8,128]{2,1,0:T(8,128)S(1)}) custom-call(s32[9]{0:T(128)S(1)} %compare_select_fusion.plan_ref, s32[1,8]{1,0:T(1,128)S(1)} %copy-done.3, s32[1,8]{1,0:T(1,128)S(1)} %copy-done.4, bf16[1,8,128,512]{3,2,1,0:T(8,128)(2,1)S(1)} %copy-done, bf16[2,128,384]{2,1,0:T(8,128)(2,1)S(1)} %collective-permute-done.near_ref, ...), custom_call_target="tpu_custom_call" | custom-call | flops 4831838208 | bytes 3145728 | tf_op jit(solution)/shard_map/roots/pallas_call | solution.py:389
  20.9 8.7 %collective-permute-done.3.grad1_ref.rest_1_ = bf16[2,128,512]{2,1,0:T(8,128)(2,1)S(1)} collective-permute-done((bf16[2,128,512]{2,1,0:T(8,128)(2,1)S(1)}, bf16[2,128,512]{2,1,0:T(8,128)(2,1)S(1)}, u32[]{:S(2)}, u32[]{:S(2)}) %collective-permute-start.3) | collective-permute-done | bytes 262176 | tf_op jit(solution)/shard_map/ppermute | solution.py:540
  29.6 1.1 %start_product.1 = (bf16[2,256,256]{2,1,0:T(8,128)(2,1)S(1)}, bf16[2,256,256]{2,1,0:T(8,128)(2,1)S(1)}, f32[2,256,512]{2,1,0:T(8,128)S(1)}, f32[2,256,512]{2,1,0:T(8,128)S(1)}) custom-call(s32[9]{0:T(128)S(1)} %compare_select_fusion.plan_ref, bf16[2,512,512]{2,1,0:T(8,128)(2,1)S(1)} %get-tuple-element.26.root_ref, ...), custom_call_target="tpu_custom_call" | custom-call | flops 268435456 | bytes 2097152 | tf_op jit(solution)/shard_map/start_product/pallas_call | solution.py:441
  30.7 0.0 collective-permute-done.4.grad3_ref
  30.7 5.3 %collective-permute-done.5.grad2_ref = bf16[2,128,512]{2,1,0:T(8,128)(2,1)S(1)} collective-permute-done((bf16[2,128,512]{2,1,0:T(8,128)(2,1)S(1)}, bf16[2,128,512]{2,1,0:T(8,128)(2,1)S(1)}, u32[]{:S(2)}, u32[]{:S(2)}) %collective-permute-start.5) | collective-permute-done | bytes 262176 | tf_op jit(solution)/shard_map/ppermute | solution.py:540
  36.0 0.3 far_product.1
  36.3 3.5 %collective-permute-start.9 = (bf16[2,128,512]{2,1,0:T(8,128)(2,1)S(1)}, bf16[2,128,512]{2,1,0:T(8,128)(2,1)S(1)}, u32[]{:S(2)}, u32[]{:S(2)}) collective-permute-start(bf16[2,128,512]{2,1,0:T(8,128)(2,1)S(1)} %get-tuple-element.37.rest_3_), channel_id=1, source_target_pairs={{0,12},{4,8},{8,4},{12,0},{1,13},{5,9},{9,5},{13,1},{2,14},{6,10},... | collective-permute-start | bytes 786440 | tf_op jit(solution)/shard_map/ppermute | solution.py:540
  39.8 0.8 %near_product.1 = (bf16[2,128,512]{2,1,0:T(8,128)(2,1)S(1)}, bf16[2,128,512]{2,1,0:T(8,128)(2,1)S(1)}, f32[8,128]{1,0:T(8,128)S(1)}) custom-call(bf16[2,256,256]{2,1,0:T(8,128)(2,1)S(1)} %get-tuple-element.29.root_ref, f32[2,256,512]{2,1,0:T(8,128)S(1)} %get-tuple-element.30.begun_ref, f32[2,8,128]{2,1,0:T(8,128)S(1)} %get-tuple-element.31.factor_ref, ...), custom_call_target="tpu_custom_call" | custom-call | flops 134217728 | bytes 2097152 | tf_op jit(solution)/shard_map/near_product/pallas_call | solution.py:483
  40.6 0.1 collective-permute-start.13
  40.7 1.0 %collective-permute-start.14 = (bf16[2,128,512]{2,1,0:T(8,128)(2,1)S(1)}, bf16[2,128,512]{2,1,0:T(8,128)(2,1)S(1)}, u32[]{:S(2)}, u32[]{:S(2)}) collective-permute-start(bf16[2,128,512]{2,1,0:T(8,128)(2,1)S(1)} %get-tuple-element.36.rest_2_), channel_id=1, source_target_pairs={{0,8},{4,12},{8,0},{12,4},{1,9},{5,13},{9,1},{13,5},{2,10},{6,14},... | collective-permute-start | bytes 786440 | tf_op jit(solution)/shard_map/ppermute | solution.py:540
  41.6 0.0 collective-permute-start.8
  41.6 1.5 %collective-permute-start.7 = (f32[8,128]{1,0:T(8,128)S(1)}, f32[8,128]{1,0:T(8,128)S(1)}, u32[]{:S(2)}, u32[]{:S(2)}) collective-permute-start(f32[8,128]{1,0:T(8,128)S(1)} %get-tuple-element.38), channel_id=1, source_target_pairs={{0,2},{1,3},{2,0},{3,1},{4,6},{5,7},{6,4},{7,5},{8,10},{9,11},{10,... | collective-permute-start | bytes 12296 | tf_op jit(solution)/shard_map/ppermute | solution.py:547
  43.2 0.0 collective-permute-done.8
  43.2 1.7 %collective-permute-start.6 = (f32[8,128]{1,0:T(8,128)S(1)}, f32[8,128]{1,0:T(8,128)S(1)}, u32[]{:S(2)}, u32[]{:S(2)}) collective-permute-start(f32[8,128]{1,0:T(8,128)S(1)} %get-tuple-element.38), channel_id=1, source_target_pairs={{0,1},{1,2},{2,3},{3,0},{4,5},{5,6},{6,7},{7,4},{8,9},{9,10},{10,1... | collective-permute-start | bytes 12296 | tf_op jit(solution)/shard_map/ppermute | solution.py:547
  44.9 0.4 collective-permute-done.7
  45.3 1.0 %collective-permute-done.6 = f32[8,128]{1,0:T(8,128)S(1)} collective-permute-done((f32[8,128]{1,0:T(8,128)S(1)}, f32[8,128]{1,0:T(8,128)S(1)}, u32[]{:S(2)}, u32[]{:S(2)}) %collective-permute-start.6) | collective-permute-done | bytes 4128 | tf_op jit(solution)/shard_map/ppermute | solution.py:547
  46.3 3.4 %collective-permute-start.12 = (f32[8,128]{1,0:T(8,128)S(1)}, f32[8,128]{1,0:T(8,128)S(1)}, u32[]{:S(2)}, u32[]{:S(2)}) collective-permute-start(f32[8,128]{1,0:T(8,128)S(1)} %add_add_fusion.value_ref.rest_0_), channel_id=1, source_target_pairs={{0,12},{4,8},{8,4},{12,0},{1,13},{5,9},{9,5},{13,1},{2,14},{6,10},... | collective-permute-start | bytes 12296 | tf_op jit(solution)/shard_map/ppermute | solution.py:540
  49.7 0.0 collective-permute-start.11
  49.7 0.0 collective-permute-done.9.landed_ref.rest_7_
  49.7 3.7 %collective-permute-start.10 = (f32[8,128]{1,0:T(8,128)S(1)}, f32[8,128]{1,0:T(8,128)S(1)}, u32[]{:S(2)}, u32[]{:S(2)}) collective-permute-start(f32[8,128]{1,0:T(8,128)S(1)} %after.1), channel_id=1, source_target_pairs={{0,4},{4,0},{8,12},{12,8},{1,5},{5,1},{9,13},{13,9},{2,6},{6,2},{1... | collective-permute-start | bytes 12296 | tf_op jit(solution)/shard_map/ppermute | solution.py:540
  53.3 2.7 %collective-permute-done.12.rest_3_ = f32[8,128]{1,0:T(8,128)S(1)} collective-permute-done((f32[8,128]{1,0:T(8,128)S(1)}, f32[8,128]{1,0:T(8,128)S(1)}, u32[]{:S(2)}, u32[]{:S(2)}) %collective-permute-start.12) | collective-permute-done | bytes 4128 | tf_op jit(solution)/shard_map/ppermute | solution.py:540
  56.1 2.9 %collective-permute-done.11.rest_2_ = f32[8,128]{1,0:T(8,128)S(1)} collective-permute-done((f32[8,128]{1,0:T(8,128)S(1)}, f32[8,128]{1,0:T(8,128)S(1)}, u32[]{:S(2)}, u32[]{:S(2)}) %collective-permute-start.11) | collective-permute-done | bytes 4128 | tf_op jit(solution)/shard_map/ppermute | solution.py:540
  59.0 0.0 collective-permute-done.13.rest_5_
  59.0 0.0 collective-permute-done.14.rest_6_
  59.0 0.0 collective-permute-done.10.rest_1_
  59.0 1.8 %clip.1 = bf16[1,8,128,512]{3,2,1,0:T(8,128)(2,1)} custom-call(s32[9]{0:T(128)S(1)} %compare_select_fusion.plan_ref, f32[8,128]{1,0:T(8,128)S(1)} %add_add_fusion.value_ref.rest_0_, f32[8,128]{1,0:T(8,128)S(1)} %collective-permute-done.10.rest_1_, f32[8,128]{1,0:T(8,128)S(1)} %collective-permute-done.11.rest_2_, ...), custom_call_target="tpu_custom_call" | custom-call | bytes 2097152 | tf_op jit(solution)/shard_map/clip/pallas_call | solution.py:513
  (3 shorter events, 0.0 us)
Async XLA Ops:
  0.0 8.8 %copy-start.1 = (bf16[1,8,128,512]{3,2,1,0:T(8,128)(2,1)S(1)}, bf16[1,8,128,512]{3,2,1,0:T(8,128)(2,1)}, u32[]{:S(2)}) copy-start(bf16[1,8,128,512]{3,2,1,0:T(8,128)(2,1)} %grad_ref.1) | copy-start | bytes 3145732
  0.0 16.8 %copy-start = (bf16[1,8,128,512]{3,2,1,0:T(8,128)(2,1)S(1)}, bf16[1,8,128,512]{3,2,1,0:T(8,128)(2,1)}, u32[]{:S(2)}) copy-start(bf16[1,8,128,512]{3,2,1,0:T(8,128)(2,1)} %stats_ref.1) | copy-start | bytes 3145732
  2.3 11.0 %collective-permute-start.1 = (bf16[272,128]{1,0:T(8,128)(2,1)}, bf16[272,128]{1,0:T(8,128)(2,1)S(1)}, u32[]{:S(2)}, u32[]{:S(2)}) collective-permute-start(bf16[272,128]{1,0:T(8,128)(2,1)} %get-tuple-element.24), channel_id=1, source_target_pairs={{0,12},{4,8},{8,4},{12,0},{1,13},{5,9},{9,5},{13,1},{2,14},{6,10},... | collective-permute-start | bytes 208904 | tf_op jit(solution)/shard_map/ppermute | solution.py:540
  7.4 6.7 %collective-permute-start.2 = (bf16[272,128]{1,0:T(8,128)(2,1)}, bf16[272,128]{1,0:T(8,128)(2,1)S(1)}, u32[]{:S(2)}, u32[]{:S(2)}) collective-permute-start(bf16[272,128]{1,0:T(8,128)(2,1)} %get-tuple-element.25), channel_id=1, source_target_pairs={{0,8},{4,12},{8,0},{12,4},{1,9},{5,13},{9,1},{13,5},{2,10},{6,14},... | collective-permute-start | bytes 208904 | tf_op jit(solution)/shard_map/ppermute | solution.py:540
  7.4 9.3 %collective-permute-start = (bf16[2,128,384]{2,1,0:T(8,128)(2,1)}, bf16[2,128,384]{2,1,0:T(8,128)(2,1)S(1)}, u32[]{:S(2)}, u32[]{:S(2)}) collective-permute-start(bf16[2,128,384]{2,1,0:T(8,128)(2,1)} %get-tuple-element.23), channel_id=1, source_target_pairs={{0,4},{4,0},{8,12},{12,8},{1,5},{5,1},{9,13},{13,9},{2,6},{6,2},{1... | collective-permute-start | bytes 589832 | tf_op jit(solution)/shard_map/ppermute | solution.py:540
  9.4 20.2 %collective-permute-start.3 = (bf16[2,128,512]{2,1,0:T(8,128)(2,1)S(1)}, bf16[2,128,512]{2,1,0:T(8,128)(2,1)S(1)}, u32[]{:S(2)}, u32[]{:S(2)}) collective-permute-start(bf16[2,128,512]{2,1,0:T(8,128)(2,1)S(1)} %get-tuple-element.28), channel_id=1, source_target_pairs={{0,4},{4,0},{8,12},{12,8},{1,5},{5,1},{9,13},{13,9},{2,6},{6,2},{1... | collective-permute-start | bytes 786440 | tf_op jit(solution)/shard_map/ppermute | solution.py:540
  10.9 5.9 %copy-start.3 = (s32[1,8]{1,0:T(1,128)S(1)}, s32[1,8]{1,0:T(1,128)}, u32[]{:S(2)}) copy-start(s32[1,8]{1,0:T(1,128)} %due_ref.1) | copy-start | bytes 100
  10.9 5.9 %copy-start.4 = (s32[1,8]{1,0:T(1,128)S(1)}, s32[1,8]{1,0:T(1,128)}, u32[]{:S(2)}) copy-start(s32[1,8]{1,0:T(1,128)} %cost_ref.1) | copy-start | bytes 100
  10.9 19.8 %collective-permute-start.4 = (bf16[2,128,512]{2,1,0:T(8,128)(2,1)S(1)}, bf16[2,128,512]{2,1,0:T(8,128)(2,1)S(1)}, u32[]{:S(2)}, u32[]{:S(2)}) collective-permute-start(bf16[2,128,512]{2,1,0:T(8,128)(2,1)S(1)} %get-tuple-element.32), channel_id=1, source_target_pairs={{0,12},{4,8},{8,4},{12,0},{1,13},{5,9},{9,5},{13,1},{2,14},{6,10},... | collective-permute-start | bytes 786440 | tf_op jit(solution)/shard_map/ppermute | solution.py:540
  13.4 22.7 %collective-permute-start.5 = (bf16[2,128,512]{2,1,0:T(8,128)(2,1)S(1)}, bf16[2,128,512]{2,1,0:T(8,128)(2,1)S(1)}, u32[]{:S(2)}, u32[]{:S(2)}) collective-permute-start(bf16[2,128,512]{2,1,0:T(8,128)(2,1)S(1)} %get-tuple-element.33), channel_id=1, source_target_pairs={{0,8},{4,12},{8,0},{12,4},{1,9},{5,13},{9,1},{13,5},{2,10},{6,14},... | collective-permute-start | bytes 786440 | tf_op jit(solution)/shard_map/ppermute | solution.py:540
  16.8 1.2 %copy-start.2 = (bf16[1,2,512,512]{3,2,1,0:T(8,128)(2,1)S(1)}, bf16[1,2,512,512]{3,2,1,0:T(8,128)(2,1)}, u32[]{:S(2)}) copy-start(bf16[1,2,512,512]{3,2,1,0:T(8,128)(2,1)} %stale_ref.1) | copy-start | bytes 3145732
  36.3 13.4 %collective-permute-start.9 = (bf16[2,128,512]{2,1,0:T(8,128)(2,1)S(1)}, bf16[2,128,512]{2,1,0:T(8,128)(2,1)S(1)}, u32[]{:S(2)}, u32[]{:S(2)}) collective-permute-start(bf16[2,128,512]{2,1,0:T(8,128)(2,1)S(1)} %get-tuple-element.37.rest_3_), channel_id=1, source_target_pairs={{0,12},{4,8},{8,4},{12,0},{1,13},{5,9},{9,5},{13,1},{2,14},{6,10},... | collective-permute-start | bytes 786440 | tf_op jit(solution)/shard_map/ppermute | solution.py:540
  40.6 18.4 %collective-permute-start.13 = (bf16[2,128,512]{2,1,0:T(8,128)(2,1)S(1)}, bf16[2,128,512]{2,1,0:T(8,128)(2,1)S(1)}, u32[]{:S(2)}, u32[]{:S(2)}) collective-permute-start(bf16[2,128,512]{2,1,0:T(8,128)(2,1)S(1)} %get-tuple-element.40), channel_id=1, source_target_pairs={{0,4},{4,0},{8,12},{12,8},{1,5},{5,1},{9,13},{13,9},{2,6},{6,2},{1... | collective-permute-start | bytes 786440 | tf_op jit(solution)/shard_map/ppermute | solution.py:540
  40.7 18.4 %collective-permute-start.14 = (bf16[2,128,512]{2,1,0:T(8,128)(2,1)S(1)}, bf16[2,128,512]{2,1,0:T(8,128)(2,1)S(1)}, u32[]{:S(2)}, u32[]{:S(2)}) collective-permute-start(bf16[2,128,512]{2,1,0:T(8,128)(2,1)S(1)} %get-tuple-element.36.rest_2_), channel_id=1, source_target_pairs={{0,8},{4,12},{8,0},{12,4},{1,9},{5,13},{9,1},{13,5},{2,10},{6,14},... | collective-permute-start | bytes 786440 | tf_op jit(solution)/shard_map/ppermute | solution.py:540
  41.6 1.5 %collective-permute-start.8 = (f32[8,128]{1,0:T(8,128)S(1)}, f32[8,128]{1,0:T(8,128)S(1)}, u32[]{:S(2)}, u32[]{:S(2)}) collective-permute-start(f32[8,128]{1,0:T(8,128)S(1)} %get-tuple-element.38), channel_id=1, source_target_pairs={{0,3},{1,0},{2,1},{3,2},{4,7},{5,4},{6,5},{7,6},{8,11},{9,8},{10,9... | collective-permute-start | bytes 12296 | tf_op jit(solution)/shard_map/ppermute | solution.py:547
  41.6 3.6 %collective-permute-start.7 = (f32[8,128]{1,0:T(8,128)S(1)}, f32[8,128]{1,0:T(8,128)S(1)}, u32[]{:S(2)}, u32[]{:S(2)}) collective-permute-start(f32[8,128]{1,0:T(8,128)S(1)} %get-tuple-element.38), channel_id=1, source_target_pairs={{0,2},{1,3},{2,0},{3,1},{4,6},{5,7},{6,4},{7,5},{8,10},{9,11},{10,... | collective-permute-start | bytes 12296 | tf_op jit(solution)/shard_map/ppermute | solution.py:547
  43.2 3.1 %collective-permute-start.6 = (f32[8,128]{1,0:T(8,128)S(1)}, f32[8,128]{1,0:T(8,128)S(1)}, u32[]{:S(2)}, u32[]{:S(2)}) collective-permute-start(f32[8,128]{1,0:T(8,128)S(1)} %get-tuple-element.38), channel_id=1, source_target_pairs={{0,1},{1,2},{2,3},{3,0},{4,5},{5,6},{6,7},{7,4},{8,9},{9,10},{10,1... | collective-permute-start | bytes 12296 | tf_op jit(solution)/shard_map/ppermute | solution.py:547
  46.3 9.8 %collective-permute-start.12 = (f32[8,128]{1,0:T(8,128)S(1)}, f32[8,128]{1,0:T(8,128)S(1)}, u32[]{:S(2)}, u32[]{:S(2)}) collective-permute-start(f32[8,128]{1,0:T(8,128)S(1)} %add_add_fusion.value_ref.rest_0_), channel_id=1, source_target_pairs={{0,12},{4,8},{8,4},{12,0},{1,13},{5,9},{9,5},{13,1},{2,14},{6,10},... | collective-permute-start | bytes 12296 | tf_op jit(solution)/shard_map/ppermute | solution.py:540
  49.7 9.4 %collective-permute-start.11 = (f32[8,128]{1,0:T(8,128)S(1)}, f32[8,128]{1,0:T(8,128)S(1)}, u32[]{:S(2)}, u32[]{:S(2)}) collective-permute-start(f32[8,128]{1,0:T(8,128)S(1)} %add_add_fusion.value_ref.rest_0_), channel_id=1, source_target_pairs={{0,8},{4,12},{8,0},{12,4},{1,9},{5,13},{9,1},{13,5},{2,10},{6,14},... | collective-permute-start | bytes 12296 | tf_op jit(solution)/shard_map/ppermute | solution.py:540
  49.7 9.4 %collective-permute-start.10 = (f32[8,128]{1,0:T(8,128)S(1)}, f32[8,128]{1,0:T(8,128)S(1)}, u32[]{:S(2)}, u32[]{:S(2)}) collective-permute-start(f32[8,128]{1,0:T(8,128)S(1)} %after.1), channel_id=1, source_target_pairs={{0,4},{4,0},{8,12},{12,8},{1,5},{5,1},{9,13},{13,9},{2,6},{6,2},{1... | collective-permute-start | bytes 12296 | tf_op jit(solution)/shard_map/ppermute | solution.py:540

commit v5 on v4

--- a/solution.py
+++ b/solution.py
@@ -9,7 +9,6 @@
 
 KL_BOUND = 1.0
 VMEM_BYTES = 40 * 2**20
-PACK_VMEM_BYTES = int(59 * 2**20)
 DIAGONAL_ROWS = 16
 F32 = jnp.float32
 BF16 = jnp.bfloat16
@@ -89,14 +88,14 @@
     return (clip_factor * owner_rows.astype(F32)).astype(BF16)[None]
 
 
-def call(kernel, out_shape, in_specs, out_specs, name, scratch=(), flops=0, moved=0, vmem=VMEM_BYTES):
+def call(kernel, out_shape, in_specs, out_specs, name, scratch=(), flops=0, moved=0):
     return pl.pallas_call(
         kernel,
         out_shape=out_shape,
         in_specs=in_specs,
         out_specs=out_specs,
         scratch_shapes=list(scratch),
-        compiler_params=pltpu.CompilerParams(vmem_limit_bytes=vmem),
+        compiler_params=pltpu.CompilerParams(vmem_limit_bytes=VMEM_BYTES),
         cost_estimate=pl.CostEstimate(flops=flops, bytes_accessed=moved, transcendentals=0),
         name=name,
     )
@@ -107,11 +106,12 @@
 ANYWHERE = pl.BlockSpec(memory_space=pl.ANY)
 
 
-def plan_of(table_row, place):
+def plan_of(table_row, place, slots):
     total = table_row.shape[0]
+    entry = lax.broadcasted_iota(jnp.int32, (total + 1, total), 0)
+    wanted = (place ^ (entry // slots)) * slots + entry % slots
     blocks = lax.broadcasted_iota(jnp.int32, (total + 1, total), 1)
-    slots = lax.broadcasted_iota(jnp.int32, (total + 1, total), 0)
-    source = jnp.sum(jnp.where(table_row[None, :] == slots, blocks, 0), axis=1)
+    source = jnp.sum(jnp.where(table_row[None, :] == wanted, blocks, 0), axis=1)
     return jnp.where(jnp.arange(total + 1) == total, place, source)
 
 
@@ -218,15 +218,13 @@
             pltpu.SemaphoreType.DMA((stats.shape[1] + 1,)),
         ],
         moved=2 * stats.size * 2,
-        vmem=PACK_VMEM_BYTES,
-    )(me, assign, stats)
+    )(me, *(pltpu.with_memory_space_constraint(x, pltpu.HBM) for x in (assign, stats)))
 
 
 def pack_grad_kernel(slots, plan_ref, grad_ref, *outs):
-    me = place_of(plan_ref)
     for far in (3, 2, 1, 0):
         for slot in range(slots):
-            outs[far][slot] = grad_ref[0, plan_ref[(me ^ far) * slots + slot]]
+            outs[far][slot] = grad_ref[0, plan_ref[far * slots + slot]]
 
 
 def pack_grad(plan, grad, slots):
@@ -311,7 +309,7 @@
             full[at(me ^ other), at(me)] = own[:, at(me ^ other)].astype(F32).T
 
     for slot in range(slots):
-        block = plan_ref[me * slots + slot]
+        block = plan_ref[slot]
         due = due_ref[0, block]
         cost = cost_ref[0, block]
         factor_ref[slot] = jnp.ones((8, 128), F32)
@@ -473,13 +471,13 @@
                 for start in range(0, width, 8):
                     for column in range(0, columns, 128):
                         total = total + terms[start : start + 8, column : column + 128]
-        rest[-1][...] = total
+        rest[-1][...] = jnp.sum(total, axis=0, keepdims=True)
 
 
 def finish_product(root, begun, factor, grad2, grad3, *others):
     slots, width, columns = grad2.shape
     out = jax.ShapeDtypeStruct(grad2.shape, BF16)
-    shapes = (out, out) + ((jax.ShapeDtypeStruct((8, 128), F32),) if others else ())
+    shapes = (out, out) + ((jax.ShapeDtypeStruct((1, 128), F32),) if others else ())
     return call(
         finish_kernel,
         shapes,
@@ -493,17 +491,20 @@
 
 def clip_kernel(slots, elements, plan_ref, *rest):
     sums, rows, out_hbm, out_ref, sems = rest[:4], rest[4:8], *rest[8:]
-    me = place_of(plan_ref)
-    quadratic = jnp.sum(sums[0][...] + sums[1][...] + sums[2][...] + sums[3][...])
-    ratio = jnp.full((8, 128), F32(KL_BOUND * elements)) / quadratic
-    clip_factor = jnp.max(jnp.minimum(F32(1.0), jnp.sqrt(ratio)))
+    plan = plan_ref[...]
+    entry = lax.broadcasted_iota(jnp.int32, plan.shape, 1)
+    blocks = [jnp.sum(jnp.where(entry == at, plan, 0)) for at in range(4 * slots)]
+    lanes = sums[0][...] + sums[1][...] + sums[2][...] + sums[3][...]
+    quadratic = jnp.sum(lanes, axis=1, keepdims=True)
+    clip_factor = jnp.minimum(F32(1.0), jnp.sqrt(F32(KL_BOUND * elements) / quadratic))
     copies = []
     for far in range(4):
         for slot in range(slots):
             at = far * slots + slot
-            block = plan_ref[(me ^ far) * slots + slot]
             out_ref[at] = (clip_factor * rows[far][slot].astype(F32)).astype(BF16)
-            copies.append(pltpu.make_async_copy(out_ref.at[at], out_hbm.at[0, block], sems.at[at]))
+            copies.append(
+                pltpu.make_async_copy(out_ref.at[at], out_hbm.at[0, blocks[at]], sems.at[at])
+            )
             copies[-1].start()
     for copy in copies:
         copy.wait()
@@ -513,12 +514,12 @@
     return call(
         functools.partial(clip_kernel, slots, elements),
         jax.ShapeDtypeStruct(shape, BF16),
-        [IN_SMEM] + [IN_VMEM] * (len(sums) + len(rows)),
+        [IN_VMEM] * (1 + len(sums) + len(rows)),
         ANYWHERE,
         "clip",
         scratch=[pltpu.VMEM(shape[1:], BF16), pltpu.SemaphoreType.DMA((shape[1],))],
         moved=4 * shape[1] * shape[2] * shape[3],
-    )(plan, *sums, *rows)
+    )(plan[None], *sums, *rows)
 
 
 def after_kernel(value_ref, landed_ref, out_ref):
@@ -553,7 +554,7 @@
 def exchange_four(stats, grad, due, cost, assign, stale):
     slots = assign.shape[1] // 4
     me = lax.axis_index("fsdp").astype(jnp.int32)
-    plan = plan_of(assign[0], me)
+    plan = plan_of(assign[0], me, slots)
     near, far2, far3 = pack_stats(me.reshape(1), assign, stats, slots)
     received = [partner_of(near, "fsdp", 1), partner_of(far3, "fsdp", 3), partner_of(far2, "fsdp", 2)]
     own_grad, *sent = pack_grad(plan, grad, slots)

time: 61 us -> 59.2 us (0.970)
  waiting for transfers between devices: 23.7 us -> 21.1 us
  starting transfers between devices: 25.3 us -> 27.4 us
  Pallas kernels: 9.75 us -> 8.44 us
    ppermute x12, starting transfers between devices: 22 us -> 25.6 us  [partner_of(): return lax.ppermute(value, axis, [(i, i ^ far) for i in range(count)])]
    ppermute x12, waiting for transfers between devices: 22.3 us -> 19.4 us  [partner_of(): return lax.ppermute(value, axis, [(i, i ^ far) for i in range(count)])]
    ppermute x3, starting transfers between devices: 3.25 us -> 1.77 us  [sum_over(): lax.ppermute(value, axis, [(i, (i + shift) % count) for i in range(count)])]
    pallas_call x1, Pallas kernels: 2.3 us -> 1.66 us  [pack_stats(): call(functools.partial(pack_stats_kernel, slots), (near, far, far), [IN_S...]
  transfers between devices with their start and end apart: 15 -> 15, of which waited for: 7 -> 6; matrix products, arithmetic and copies ran while one was open for 1% -> 1% of each run, Pallas kernels for 9% -> 9%
where the time goes in v5:
time: 59.2 us; the launch traced here: 59 us
  starting transfers between devices  27.4 us (46%)
  waiting for transfers between devices  21.1 us (36%)
  Pallas kernels  8.44 us (14%)
  local copies, waits for them, and re-layouts  1.23 us (2%)
  other arithmetic  0.77 us (1%)
    ppermute x12, starting transfers between devices, partner_of(): return lax.ppermute(value, axis, [(i, i ^ far) for i in range(count)])  25.6 us
    ppermute x12, waiting for transfers between devices, partner_of(): return lax.ppermute(value, axis, [(i, i ^ far) for i in range(count)])  19.4 us
    pallas_call x1, Pallas kernels, roots(): call(functools.partial(root_kernel, slots), (jax.ShapeDtypeStruct((slots,...  2.78 us
    ppermute x3, starting transfers between devices, sum_over(): lax.ppermute(value, axis, [(i, (i + shift) % count) for i in range(count)])  1.77 us
    ppermute x3, waiting for transfers between devices, sum_over(): lax.ppermute(value, axis, [(i, (i + shift) % count) for i in range(count)])  1.71 us
    pallas_call x1, Pallas kernels, pack_stats(): call(functools.partial(pack_stats_kernel, slots), (near, far, far), [IN_S...  1.66 us
    unnamed x10, local copies, waits for them, and re-layouts  1.23 us
  transfers between devices with their start and end apart: 15, of which 6 were waited for; matrix products, arithmetic and copies ran while one was open for 1% of the time, Pallas kernels for 9%

profile of v5, /device:TPU:0, one launch (start us, length us, event | category | flops | bytes accessed | tf_op | source)
XLA Modules:
  0.0 59.0 jit_solution(13342347202904636709)
XLA Ops:
  0.0 0.0 copy-start.1
  0.0 0.0 copy-start
  0.0 1.7 %pack_stats.1 = (bf16[2,128,384]{2,1,0:T(8,128)(2,1)S(1)}, bf16[272,128]{1,0:T(8,128)(2,1)S(1)}, bf16[272,128]{1,0:T(8,128)(2,1)S(1)}) custom-call(s32[1]{0:T(128)} %bitcast.2.me_ref, s32[1,8]{1,0:T(1,128)} %assign_hbm.1, bf16[1,8,128,512]{3,2,1,0:T(8,128)(2,1)} %stats_ref.1), custom_call_target="tpu_custom_call" | custom-call | bytes 2097152 | tf_op jit(solution)/shard_map/pack_stats/pallas_call | solution.py:209
  1.7 5.1 %collective-permute-start.1 = (bf16[272,128]{1,0:T(8,128)(2,1)S(1)}, bf16[272,128]{1,0:T(8,128)(2,1)S(1)}, u32[]{:S(2)}, u32[]{:S(2)}) collective-permute-start(bf16[272,128]{1,0:T(8,128)(2,1)S(1)} %get-tuple-element.24), channel_id=1, source_target_pairs={{0,12},{4,8},{8,4},{12,0},{1,13},{5,9},{9,5},{13,1},{2,14},{6,10},... | collective-permute-start | bytes 208904 | tf_op jit(solution)/shard_map/ppermute | solution.py:541
  6.8 0.0 collective-permute-start.2
  6.8 0.6 %collective-permute-start = (bf16[2,128,384]{2,1,0:T(8,128)(2,1)S(1)}, bf16[2,128,384]{2,1,0:T(8,128)(2,1)S(1)}, u32[]{:S(2)}, u32[]{:S(2)}) collective-permute-start(bf16[2,128,384]{2,1,0:T(8,128)(2,1)S(1)} %get-tuple-element.23), channel_id=1, source_target_pairs={{0,4},{4,0},{8,12},{12,8},{1,5},{5,1},{9,13},{13,9},{2,6},{6,2},{1... | collective-permute-start | bytes 589832 | tf_op jit(solution)/shard_map/ppermute | solution.py:541
  7.4 0.7 %select_reduce_fusion = s32[9]{0:T(128)S(1)} fusion(s32[9]{0:T(128)S(1)} %get-tuple-element.44, s32[9]{0:T(128)S(1)} %get-tuple-element.45, s32[9]{0:T(128)S(1)} %get-tuple-element.43, s32[9]{0:T(128)S(1)} %get-tuple-element.46, s32[]{:T(128)} %axis_index.15, s32[8]{0:T(128)} %bitcast.4, pred[9]{0:T(512)(128)(4,1)S(1)} %get-tuple-element.41, ...), kind=kLoop, calls=%fused_computation | loop fusion | flops 567 | bytes 234 | tf_op jit(solution)/shard_map/reduce_sum | solution.py:114
  8.2 0.0 copy-done.1
  8.2 0.6 %pack_grad.1 = (bf16[2,128,512]{2,1,0:T(8,128)(2,1)S(1)}, bf16[2,128,512]{2,1,0:T(8,128)(2,1)S(1)}, bf16[2,128,512]{2,1,0:T(8,128)(2,1)S(1)}, bf16[2,128,512]{2,1,0:T(8,128)(2,1)S(1)}) custom-call(s32[9]{0:T(128)S(1)} %compare_select_fusion.plan_ref, bf16[1,8,128,512]{3,2,1,0:T(8,128)(2,1)S(1)} %copy-done.1), custom_call_target="tpu_custom_call" | custom-call | bytes 2097152 | tf_op jit(solution)/shard_map/pack_grad/pallas_call | solution.py:232
  8.8 1.5 %collective-permute-start.3 = (bf16[2,128,512]{2,1,0:T(8,128)(2,1)S(1)}, bf16[2,128,512]{2,1,0:T(8,128)(2,1)S(1)}, u32[]{:S(2)}, u32[]{:S(2)}) collective-permute-start(bf16[2,128,512]{2,1,0:T(8,128)(2,1)S(1)} %get-tuple-element.28), channel_id=1, source_target_pairs={{0,4},{4,0},{8,12},{12,8},{1,5},{5,1},{9,13},{13,9},{2,6},{6,2},{1... | collective-permute-start | bytes 786440 | tf_op jit(solution)/shard_map/ppermute | solution.py:541
  10.3 0.0 copy-start.3
  10.3 0.0 copy-start.4
  10.3 2.5 %collective-permute-start.4 = (bf16[2,128,512]{2,1,0:T(8,128)(2,1)S(1)}, bf16[2,128,512]{2,1,0:T(8,128)(2,1)S(1)}, u32[]{:S(2)}, u32[]{:S(2)}) collective-permute-start(bf16[2,128,512]{2,1,0:T(8,128)(2,1)S(1)} %get-tuple-element.32), channel_id=1, source_target_pairs={{0,12},{4,8},{8,4},{12,0},{1,13},{5,9},{9,5},{13,1},{2,14},{6,10},... | collective-permute-start | bytes 786440 | tf_op jit(solution)/shard_map/ppermute | solution.py:541
  12.7 0.0 collective-permute-done.1.far3_ref
  12.7 0.6 collective-permute-start.5
  13.3 0.0 collective-permute-done.2.far2_ref
  13.3 2.6 %collective-permute-done.near_ref = bf16[2,128,384]{2,1,0:T(8,128)(2,1)S(1)} collective-permute-done((bf16[2,128,384]{2,1,0:T(8,128)(2,1)S(1)}, bf16[2,128,384]{2,1,0:T(8,128)(2,1)S(1)}, u32[]{:S(2)}, u32[]{:S(2)}) %collective-permute-start) | collective-permute-done | bytes 196640 | tf_op jit(solution)/shard_map/ppermute | solution.py:541
  15.9 0.0 copy-done
  15.9 0.0 copy-done.3
  15.9 0.0 copy-done.4
  15.9 0.0 copy-start.2
  15.9 1.2 %copy-done.2 = bf16[1,2,512,512]{3,2,1,0:T(8,128)(2,1)S(1)} copy-done((bf16[1,2,512,512]{3,2,1,0:T(8,128)(2,1)S(1)}, bf16[1,2,512,512]{3,2,1,0:T(8,128)(2,1)}, u32[]{:S(2)}) %copy-start.2) | copy-done | bytes 1048600
  17.2 2.8 %roots.1 = (bf16[2,512,512]{2,1,0:T(8,128)(2,1)S(1)}, f32[2,8,128]{2,1,0:T(8,128)S(1)}) custom-call(s32[9]{0:T(128)S(1)} %compare_select_fusion.plan_ref, s32[1,8]{1,0:T(1,128)S(1)} %copy-done.3, s32[1,8]{1,0:T(1,128)S(1)} %copy-done.4, bf16[1,8,128,512]{3,2,1,0:T(8,128)(2,1)S(1)} %copy-done, bf16[2,128,384]{2,1,0:T(8,128)(2,1)S(1)} %collective-permute-done.near_ref, ...), custom_call_target="tpu_custom_call" | custom-call | flops 4831838208 | bytes 3145728 | tf_op jit(solution)/shard_map/roots/pallas_call | solution.py:387
  19.9 8.8 %collective-permute-done.3.grad1_ref.rest_1_ = bf16[2,128,512]{2,1,0:T(8,128)(2,1)S(1)} collective-permute-done((bf16[2,128,512]{2,1,0:T(8,128)(2,1)S(1)}, bf16[2,128,512]{2,1,0:T(8,128)(2,1)S(1)}, u32[]{:S(2)}, u32[]{:S(2)}) %collective-permute-start.3) | collective-permute-done | bytes 262176 | tf_op jit(solution)/shard_map/ppermute | solution.py:541
  28.7 1.1 %start_product.1 = (bf16[2,256,256]{2,1,0:T(8,128)(2,1)S(1)}, bf16[2,256,256]{2,1,0:T(8,128)(2,1)S(1)}, f32[2,256,512]{2,1,0:T(8,128)S(1)}, f32[2,256,512]{2,1,0:T(8,128)S(1)}) custom-call(s32[9]{0:T(128)S(1)} %compare_select_fusion.plan_ref, bf16[2,512,512]{2,1,0:T(8,128)(2,1)S(1)} %get-tuple-element.26.root_ref, ...), custom_call_target="tpu_custom_call" | custom-call | flops 268435456 | bytes 2097152 | tf_op jit(solution)/shard_map/start_product/pallas_call | solution.py:439
  29.8 0.0 collective-permute-done.4.grad3_ref
  29.8 5.5 %collective-permute-done.5.grad2_ref = bf16[2,128,512]{2,1,0:T(8,128)(2,1)S(1)} collective-permute-done((bf16[2,128,512]{2,1,0:T(8,128)(2,1)S(1)}, bf16[2,128,512]{2,1,0:T(8,128)(2,1)S(1)}, u32[]{:S(2)}, u32[]{:S(2)}) %collective-permute-start.5) | collective-permute-done | bytes 262176 | tf_op jit(solution)/shard_map/ppermute | solution.py:541
  35.3 0.3 far_product.1
  35.6 3.4 %collective-permute-start.9 = (bf16[2,128,512]{2,1,0:T(8,128)(2,1)S(1)}, bf16[2,128,512]{2,1,0:T(8,128)(2,1)S(1)}, u32[]{:S(2)}, u32[]{:S(2)}) collective-permute-start(bf16[2,128,512]{2,1,0:T(8,128)(2,1)S(1)} %get-tuple-element.37.rest_3_), channel_id=1, source_target_pairs={{0,12},{4,8},{8,4},{12,0},{1,13},{5,9},{9,5},{13,1},{2,14},{6,10},... | collective-permute-start | bytes 786440 | tf_op jit(solution)/shard_map/ppermute | solution.py:541
  38.9 0.8 %near_product.1 = (bf16[2,128,512]{2,1,0:T(8,128)(2,1)S(1)}, bf16[2,128,512]{2,1,0:T(8,128)(2,1)S(1)}, f32[1,128]{1,0:T(1,128)S(1)}) custom-call(bf16[2,256,256]{2,1,0:T(8,128)(2,1)S(1)} %get-tuple-element.29.root_ref, f32[2,256,512]{2,1,0:T(8,128)S(1)} %get-tuple-element.30.begun_ref, f32[2,8,128]{2,1,0:T(8,128)S(1)} %get-tuple-element.31.factor_ref, ...), custom_call_target="tpu_custom_call" | custom-call | flops 134217728 | bytes 2097152 | tf_op jit(solution)/shard_map/near_product/pallas_call | solution.py:481
  39.8 0.1 collective-permute-start.8
  39.8 1.6 %collective-permute-start.7 = (f32[1,128]{1,0:T(1,128)S(1)}, f32[1,128]{1,0:T(1,128)S(1)}, u32[]{:S(2)}, u32[]{:S(2)}) collective-permute-start(f32[1,128]{1,0:T(1,128)S(1)} %get-tuple-element.38), channel_id=1, source_target_pairs={{0,2},{1,3},{2,0},{3,1},{4,6},{5,7},{6,4},{7,5},{8,10},{9,11},{10,... | collective-permute-start | bytes 1544 | tf_op jit(solution)/shard_map/ppermute | solution.py:548
  41.4 0.2 collective-permute-start.6
  41.5 0.0 collective-permute-start.14
  41.5 0.0 collective-permute-done.8
  41.5 1.1 %collective-permute-start.13 = (bf16[2,128,512]{2,1,0:T(8,128)(2,1)S(1)}, bf16[2,128,512]{2,1,0:T(8,128)(2,1)S(1)}, u32[]{:S(2)}, u32[]{:S(2)}) collective-permute-start(bf16[2,128,512]{2,1,0:T(8,128)(2,1)S(1)} %get-tuple-element.40), channel_id=1, source_target_pairs={{0,4},{4,0},{8,12},{12,8},{1,5},{5,1},{9,13},{13,9},{2,6},{6,2},{1... | collective-permute-start | bytes 786440 | tf_op jit(solution)/shard_map/ppermute | solution.py:541
  42.6 0.8 %collective-permute-done.7 = f32[1,128]{1,0:T(1,128)S(1)} collective-permute-done((f32[1,128]{1,0:T(1,128)S(1)}, f32[1,128]{1,0:T(1,128)S(1)}, u32[]{:S(2)}, u32[]{:S(2)}) %collective-permute-start.7) | collective-permute-done | bytes 544 | tf_op jit(solution)/shard_map/ppermute | solution.py:548
  43.4 0.9 %collective-permute-done.6 = f32[1,128]{1,0:T(1,128)S(1)} collective-permute-done((f32[1,128]{1,0:T(1,128)S(1)}, f32[1,128]{1,0:T(1,128)S(1)}, u32[]{:S(2)}, u32[]{:S(2)}) %collective-permute-start.6) | collective-permute-done | bytes 544 | tf_op jit(solution)/shard_map/ppermute | solution.py:548
  44.3 1.7 %collective-permute-start.12 = (f32[1,128]{1,0:T(1,128)S(1)}, f32[1,128]{1,0:T(1,128)S(1)}, u32[]{:S(2)}, u32[]{:S(2)}) collective-permute-start(f32[1,128]{1,0:T(1,128)S(1)} %add_add_fusion.value_ref.rest_0_), channel_id=1, source_target_pairs={{0,12},{4,8},{8,4},{12,0},{1,13},{5,9},{9,5},{13,1},{2,14},{6,10},... | collective-permute-start | bytes 1544 | tf_op jit(solution)/shard_map/ppermute | solution.py:541
  46.0 0.0 collective-permute-start.11
  46.0 0.0 collective-permute-done.9.landed_ref.rest_7_
  46.0 9.3 %collective-permute-start.10 = (f32[1,128]{1,0:T(1,128)S(1)}, f32[1,128]{1,0:T(1,128)S(1)}, u32[]{:S(2)}, u32[]{:S(2)}) collective-permute-start(f32[1,128]{1,0:T(1,128)S(1)} %after.1), channel_id=1, source_target_pairs={{0,4},{4,0},{8,12},{12,8},{1,5},{5,1},{9,13},{13,9},{2,6},{6,2},{1... | collective-permute-start | bytes 1544 | tf_op jit(solution)/shard_map/ppermute | solution.py:541
  55.3 0.0 collective-permute-done.12.rest_3_
  55.3 2.5 %collective-permute-done.11.rest_2_ = f32[1,128]{1,0:T(1,128)S(1)} collective-permute-done((f32[1,128]{1,0:T(1,128)S(1)}, f32[1,128]{1,0:T(1,128)S(1)}, u32[]{:S(2)}, u32[]{:S(2)}) %collective-permute-start.11) | collective-permute-done | bytes 544 | tf_op jit(solution)/shard_map/ppermute | solution.py:541
  57.8 0.0 collective-permute-done.13.rest_5_
  57.8 0.0 collective-permute-done.14.rest_6_
  57.8 0.0 collective-permute-done.10.rest_1_
  57.8 1.2 %clip.1 = bf16[1,8,128,512]{3,2,1,0:T(8,128)(2,1)} custom-call(s32[1,9]{1,0:T(1,128)S(1)} %compare_select_fusion.1.plan_ref, f32[1,128]{1,0:T(1,128)S(1)} %add_add_fusion.value_ref.rest_0_, f32[1,128]{1,0:T(1,128)S(1)} %collective-permute-done.10.rest_1_, f32[1,128]{1,0:T(1,128)S(1)} %collective-permute-done.11.rest_2_, ...), custom_call_target="tpu_custom_call" | custom-call | bytes 2097152 | tf_op jit(solution)/shard_map/clip/pallas_call | solution.py:514
  (7 shorter events, 0.0 us)
Async XLA Ops:
  0.0 8.2 %copy-start.1 = (bf16[1,8,128,512]{3,2,1,0:T(8,128)(2,1)S(1)}, bf16[1,8,128,512]{3,2,1,0:T(8,128)(2,1)}, u32[]{:S(2)}) copy-start(bf16[1,8,128,512]{3,2,1,0:T(8,128)(2,1)} %grad_ref.1) | copy-start | bytes 3145732
  0.0 15.9 %copy-start = (bf16[1,8,128,512]{3,2,1,0:T(8,128)(2,1)S(1)}, bf16[1,8,128,512]{3,2,1,0:T(8,128)(2,1)}, u32[]{:S(2)}) copy-start(bf16[1,8,128,512]{3,2,1,0:T(8,128)(2,1)} %stats_ref.1) | copy-start | bytes 3145732
  1.7 11.1 %collective-permute-start.1 = (bf16[272,128]{1,0:T(8,128)(2,1)S(1)}, bf16[272,128]{1,0:T(8,128)(2,1)S(1)}, u32[]{:S(2)}, u32[]{:S(2)}) collective-permute-start(bf16[272,128]{1,0:T(8,128)(2,1)S(1)} %get-tuple-element.24), channel_id=1, source_target_pairs={{0,12},{4,8},{8,4},{12,0},{1,13},{5,9},{9,5},{13,1},{2,14},{6,10},... | collective-permute-start | bytes 208904 | tf_op jit(solution)/shard_map/ppermute | solution.py:541
  6.8 6.5 %collective-permute-start.2 = (bf16[272,128]{1,0:T(8,128)(2,1)S(1)}, bf16[272,128]{1,0:T(8,128)(2,1)S(1)}, u32[]{:S(2)}, u32[]{:S(2)}) collective-permute-start(bf16[272,128]{1,0:T(8,128)(2,1)S(1)} %get-tuple-element.25), channel_id=1, source_target_pairs={{0,8},{4,12},{8,0},{12,4},{1,9},{5,13},{9,1},{13,5},{2,10},{6,14},... | collective-permute-start | bytes 208904 | tf_op jit(solution)/shard_map/ppermute | solution.py:541
  6.8 9.1 %collective-permute-start = (bf16[2,128,384]{2,1,0:T(8,128)(2,1)S(1)}, bf16[2,128,384]{2,1,0:T(8,128)(2,1)S(1)}, u32[]{:S(2)}, u32[]{:S(2)}) collective-permute-start(bf16[2,128,384]{2,1,0:T(8,128)(2,1)S(1)} %get-tuple-element.23), channel_id=1, source_target_pairs={{0,4},{4,0},{8,12},{12,8},{1,5},{5,1},{9,13},{13,9},{2,6},{6,2},{1... | collective-permute-start | bytes 589832 | tf_op jit(solution)/shard_map/ppermute | solution.py:541
  8.8 19.9 %collective-permute-start.3 = (bf16[2,128,512]{2,1,0:T(8,128)(2,1)S(1)}, bf16[2,128,512]{2,1,0:T(8,128)(2,1)S(1)}, u32[]{:S(2)}, u32[]{:S(2)}) collective-permute-start(bf16[2,128,512]{2,1,0:T(8,128)(2,1)S(1)} %get-tuple-element.28), channel_id=1, source_target_pairs={{0,4},{4,0},{8,12},{12,8},{1,5},{5,1},{9,13},{13,9},{2,6},{6,2},{1... | collective-permute-start | bytes 786440 | tf_op jit(solution)/shard_map/ppermute | solution.py:541
  10.3 5.7 %copy-start.3 = (s32[1,8]{1,0:T(1,128)S(1)}, s32[1,8]{1,0:T(1,128)}, u32[]{:S(2)}) copy-start(s32[1,8]{1,0:T(1,128)} %due_ref.1) | copy-start | bytes 100
  10.3 5.7 %copy-start.4 = (s32[1,8]{1,0:T(1,128)S(1)}, s32[1,8]{1,0:T(1,128)}, u32[]{:S(2)}) copy-start(s32[1,8]{1,0:T(1,128)} %cost_ref.1) | copy-start | bytes 100
  10.3 19.5 %collective-permute-start.4 = (bf16[2,128,512]{2,1,0:T(8,128)(2,1)S(1)}, bf16[2,128,512]{2,1,0:T(8,128)(2,1)S(1)}, u32[]{:S(2)}, u32[]{:S(2)}) collective-permute-start(bf16[2,128,512]{2,1,0:T(8,128)(2,1)S(1)} %get-tuple-element.32), channel_id=1, source_target_pairs={{0,12},{4,8},{8,4},{12,0},{1,13},{5,9},{9,5},{13,1},{2,14},{6,10},... | collective-permute-start | bytes 786440 | tf_op jit(solution)/shard_map/ppermute | solution.py:541
  12.7 22.5 %collective-permute-start.5 = (bf16[2,128,512]{2,1,0:T(8,128)(2,1)S(1)}, bf16[2,128,512]{2,1,0:T(8,128)(2,1)S(1)}, u32[]{:S(2)}, u32[]{:S(2)}) collective-permute-start(bf16[2,128,512]{2,1,0:T(8,128)(2,1)S(1)} %get-tuple-element.33), channel_id=1, source_target_pairs={{0,8},{4,12},{8,0},{12,4},{1,9},{5,13},{9,1},{13,5},{2,10},{6,14},... | collective-permute-start | bytes 786440 | tf_op jit(solution)/shard_map/ppermute | solution.py:541
  15.9 1.2 %copy-start.2 = (bf16[1,2,512,512]{3,2,1,0:T(8,128)(2,1)S(1)}, bf16[1,2,512,512]{3,2,1,0:T(8,128)(2,1)}, u32[]{:S(2)}) copy-start(bf16[1,2,512,512]{3,2,1,0:T(8,128)(2,1)} %stale_ref.1) | copy-start | bytes 3145732
  35.6 10.4 %collective-permute-start.9 = (bf16[2,128,512]{2,1,0:T(8,128)(2,1)S(1)}, bf16[2,128,512]{2,1,0:T(8,128)(2,1)S(1)}, u32[]{:S(2)}, u32[]{:S(2)}) collective-permute-start(bf16[2,128,512]{2,1,0:T(8,128)(2,1)S(1)} %get-tuple-element.37.rest_3_), channel_id=1, source_target_pairs={{0,12},{4,8},{8,4},{12,0},{1,13},{5,9},{9,5},{13,1},{2,14},{6,10},... | collective-permute-start | bytes 786440 | tf_op jit(solution)/shard_map/ppermute | solution.py:541
  39.8 1.8 %collective-permute-start.8 = (f32[1,128]{1,0:T(1,128)S(1)}, f32[1,128]{1,0:T(1,128)S(1)}, u32[]{:S(2)}, u32[]{:S(2)}) collective-permute-start(f32[1,128]{1,0:T(1,128)S(1)} %get-tuple-element.38), channel_id=1, source_target_pairs={{0,3},{1,0},{2,1},{3,2},{4,7},{5,4},{6,5},{7,6},{8,11},{9,8},{10,9... | collective-permute-start | bytes 1544 | tf_op jit(solution)/shard_map/ppermute | solution.py:548
  39.8 3.6 %collective-permute-start.7 = (f32[1,128]{1,0:T(1,128)S(1)}, f32[1,128]{1,0:T(1,128)S(1)}, u32[]{:S(2)}, u32[]{:S(2)}) collective-permute-start(f32[1,128]{1,0:T(1,128)S(1)} %get-tuple-element.38), channel_id=1, source_target_pairs={{0,2},{1,3},{2,0},{3,1},{4,6},{5,7},{6,4},{7,5},{8,10},{9,11},{10,... | collective-permute-start | bytes 1544 | tf_op jit(solution)/shard_map/ppermute | solution.py:548
  41.4 3.0 %collective-permute-start.6 = (f32[1,128]{1,0:T(1,128)S(1)}, f32[1,128]{1,0:T(1,128)S(1)}, u32[]{:S(2)}, u32[]{:S(2)}) collective-permute-start(f32[1,128]{1,0:T(1,128)S(1)} %get-tuple-element.38), channel_id=1, source_target_pairs={{0,1},{1,2},{2,3},{3,0},{4,5},{5,6},{6,7},{7,4},{8,9},{9,10},{10,1... | collective-permute-start | bytes 1544 | tf_op jit(solution)/shard_map/ppermute | solution.py:548
  41.5 16.3 %collective-permute-start.14 = (bf16[2,128,512]{2,1,0:T(8,128)(2,1)S(1)}, bf16[2,128,512]{2,1,0:T(8,128)(2,1)S(1)}, u32[]{:S(2)}, u32[]{:S(2)}) collective-permute-start(bf16[2,128,512]{2,1,0:T(8,128)(2,1)S(1)} %get-tuple-element.36.rest_2_), channel_id=1, source_target_pairs={{0,8},{4,12},{8,0},{12,4},{1,9},{5,13},{9,1},{13,5},{2,10},{6,14},... | collective-permute-start | bytes 786440 | tf_op jit(solution)/shard_map/ppermute | solution.py:541
  41.5 16.3 %collective-permute-start.13 = (bf16[2,128,512]{2,1,0:T(8,128)(2,1)S(1)}, bf16[2,128,512]{2,1,0:T(8,128)(2,1)S(1)}, u32[]{:S(2)}, u32[]{:S(2)}) collective-permute-start(bf16[2,128,512]{2,1,0:T(8,128)(2,1)S(1)} %get-tuple-element.40), channel_id=1, source_target_pairs={{0,4},{4,0},{8,12},{12,8},{1,5},{5,1},{9,13},{13,9},{2,6},{6,2},{1... | collective-permute-start | bytes 786440 | tf_op jit(solution)/shard_map/ppermute | solution.py:541
  44.3 11.0 %collective-permute-start.12 = (f32[1,128]{1,0:T(1,128)S(1)}, f32[1,128]{1,0:T(1,128)S(1)}, u32[]{:S(2)}, u32[]{:S(2)}) collective-permute-start(f32[1,128]{1,0:T(1,128)S(1)} %add_add_fusion.value_ref.rest_0_), channel_id=1, source_target_pairs={{0,12},{4,8},{8,4},{12,0},{1,13},{5,9},{9,5},{13,1},{2,14},{6,10},... | collective-permute-start | bytes 1544 | tf_op jit(solution)/shard_map/ppermute | solution.py:541
  46.0 11.8 %collective-permute-start.11 = (f32[1,128]{1,0:T(1,128)S(1)}, f32[1,128]{1,0:T(1,128)S(1)}, u32[]{:S(2)}, u32[]{:S(2)}) collective-permute-start(f32[1,128]{1,0:T(1,128)S(1)} %add_add_fusion.value_ref.rest_0_), channel_id=1, source_target_pairs={{0,8},{4,12},{8,0},{12,4},{1,9},{5,13},{9,1},{13,5},{2,10},{6,14},... | collective-permute-start | bytes 1544 | tf_op jit(solution)/shard_map/ppermute | solution.py:541
  46.0 11.8 %collective-permute-start.10 = (f32[1,128]{1,0:T(1,128)S(1)}, f32[1,128]{1,0:T(1,128)S(1)}, u32[]{:S(2)}, u32[]{:S(2)}) collective-permute-start(f32[1,128]{1,0:T(1,128)S(1)} %after.1), channel_id=1, source_target_pairs={{0,4},{4,0},{8,12},{12,8},{1,5},{5,1},{9,13},{13,9},{2,6},{6,2},{1... | collective-permute-start | bytes 1544 | tf_op jit(solution)/shard_map/ppermute | solution.py:541

commit v6 on v5

--- a/solution.py
+++ b/solution.py
@@ -279,7 +279,7 @@
         start = slot * width
         row = slots * width + slot // 2 * DIAGONAL_ROWS
         for index, far_ref in ((two, far2_ref), (three, far3_ref)):
-            diagonal = far_ref[row : row + 8, :].astype(F32)
+            diagonal = far_ref[row : row + DIAGONAL_ROWS, :].astype(F32)
             if slot % 2 == 0:
                 diagonal = pltpu.roll(diagonal, half, 1)
             full[at(index), at(index)] = unfold(

time: 59.2 us -> 59.2 us (level)
  waiting for transfers between devices: 21.1 us -> 19.9 us
  Pallas kernels: 8.44 us -> 9.6 us
    ppermute x12, waiting for transfers between devices: 19.4 us -> 18.2 us  [partner_of(): return lax.ppermute(value, axis, [(i, i ^ far) for i in range(count)])]
    pallas_call x1, Pallas kernels: 2.78 us -> 3.94 us  [roots(): call(functools.partial(root_kernel, slots), (jax.ShapeDtypeStruct((slots,...]
  transfers between devices with their start and end apart: 15 -> 15, of which waited for: 6 -> 6; matrix products, arithmetic and copies ran while one was open for 1% -> 1% of each run, Pallas kernels for 9% -> 11%
where the time goes in v6:
time: 59.2 us; the launch traced here: 59 us
  starting transfers between devices  27.4 us (46%)
  waiting for transfers between devices  19.9 us (34%)
  Pallas kernels  9.6 us (16%)
  local copies, waits for them, and re-layouts  1.23 us (2%)
  other arithmetic  0.77 us (1%)
    ppermute x12, starting transfers between devices, partner_of(): return lax.ppermute(value, axis, [(i, i ^ far) for i in range(count)])  25.6 us
    ppermute x12, waiting for transfers between devices, partner_of(): return lax.ppermute(value, axis, [(i, i ^ far) for i in range(count)])  18.2 us
    pallas_call x1, Pallas kernels, roots(): call(functools.partial(root_kernel, slots), (jax.ShapeDtypeStruct((slots,...  3.94 us
    ppermute x3, starting transfers between devices, sum_over(): lax.ppermute(value, axis, [(i, (i + shift) % count) for i in range(count)])  1.77 us
    ppermute x3, waiting for transfers between devices, sum_over(): lax.ppermute(value, axis, [(i, (i + shift) % count) for i in range(count)])  1.71 us
    pallas_call x1, Pallas kernels, pack_stats(): call(functools.partial(pack_stats_kernel, slots), (near, far, far), [IN_S...  1.66 us
    unnamed x10, local copies, waits for them, and re-layouts  1.23 us
  transfers between devices with their start and end apart: 15, of which 6 were waited for; matrix products, arithmetic and copies ran while one was open for 1% of the time, Pallas kernels for 11%

profile of v6, /device:TPU:0, one launch (start us, length us, event | category | flops | bytes accessed | tf_op | source)
XLA Modules:
  0.0 59.0 jit_solution(13342347202904636709)
XLA Ops:
  0.0 0.0 copy-start.1
  0.0 0.0 copy-start
  0.0 1.7 %pack_stats.1 = (bf16[2,128,384]{2,1,0:T(8,128)(2,1)S(1)}, bf16[272,128]{1,0:T(8,128)(2,1)S(1)}, bf16[272,128]{1,0:T(8,128)(2,1)S(1)}) custom-call(s32[1]{0:T(128)} %bitcast.2.me_ref, s32[1,8]{1,0:T(1,128)} %assign_hbm.1, bf16[1,8,128,512]{3,2,1,0:T(8,128)(2,1)} %stats_ref.1), custom_call_target="tpu_custom_call" | custom-call | bytes 2097152 | tf_op jit(solution)/shard_map/pack_stats/pallas_call | solution.py:209
  1.7 5.1 %collective-permute-start.1 = (bf16[272,128]{1,0:T(8,128)(2,1)S(1)}, bf16[272,128]{1,0:T(8,128)(2,1)S(1)}, u32[]{:S(2)}, u32[]{:S(2)}) collective-permute-start(bf16[272,128]{1,0:T(8,128)(2,1)S(1)} %get-tuple-element.24), channel_id=1, source_target_pairs={{0,12},{4,8},{8,4},{12,0},{1,13},{5,9},{9,5},{13,1},{2,14},{6,10},... | collective-permute-start | bytes 208904 | tf_op jit(solution)/shard_map/ppermute | solution.py:541
  6.8 0.0 collective-permute-start.2
  6.8 0.6 %collective-permute-start = (bf16[2,128,384]{2,1,0:T(8,128)(2,1)S(1)}, bf16[2,128,384]{2,1,0:T(8,128)(2,1)S(1)}, u32[]{:S(2)}, u32[]{:S(2)}) collective-permute-start(bf16[2,128,384]{2,1,0:T(8,128)(2,1)S(1)} %get-tuple-element.23), channel_id=1, source_target_pairs={{0,4},{4,0},{8,12},{12,8},{1,5},{5,1},{9,13},{13,9},{2,6},{6,2},{1... | collective-permute-start | bytes 589832 | tf_op jit(solution)/shard_map/ppermute | solution.py:541
  7.4 0.7 %select_reduce_fusion = s32[9]{0:T(128)S(1)} fusion(s32[9]{0:T(128)S(1)} %get-tuple-element.44, s32[9]{0:T(128)S(1)} %get-tuple-element.45, s32[9]{0:T(128)S(1)} %get-tuple-element.43, s32[9]{0:T(128)S(1)} %get-tuple-element.46, s32[]{:T(128)} %axis_index.15, s32[8]{0:T(128)} %bitcast.4, pred[9]{0:T(512)(128)(4,1)S(1)} %get-tuple-element.41, ...), kind=kLoop, calls=%fused_computation | loop fusion | flops 567 | bytes 234 | tf_op jit(solution)/shard_map/reduce_sum | solution.py:114
  8.2 0.0 copy-done.1
  8.2 0.6 %pack_grad.1 = (bf16[2,128,512]{2,1,0:T(8,128)(2,1)S(1)}, bf16[2,128,512]{2,1,0:T(8,128)(2,1)S(1)}, bf16[2,128,512]{2,1,0:T(8,128)(2,1)S(1)}, bf16[2,128,512]{2,1,0:T(8,128)(2,1)S(1)}) custom-call(s32[9]{0:T(128)S(1)} %compare_select_fusion.plan_ref, bf16[1,8,128,512]{3,2,1,0:T(8,128)(2,1)S(1)} %copy-done.1), custom_call_target="tpu_custom_call" | custom-call | bytes 2097152 | tf_op jit(solution)/shard_map/pack_grad/pallas_call | solution.py:232
  8.8 1.5 %collective-permute-start.3 = (bf16[2,128,512]{2,1,0:T(8,128)(2,1)S(1)}, bf16[2,128,512]{2,1,0:T(8,128)(2,1)S(1)}, u32[]{:S(2)}, u32[]{:S(2)}) collective-permute-start(bf16[2,128,512]{2,1,0:T(8,128)(2,1)S(1)} %get-tuple-element.28), channel_id=1, source_target_pairs={{0,4},{4,0},{8,12},{12,8},{1,5},{5,1},{9,13},{13,9},{2,6},{6,2},{1... | collective-permute-start | bytes 786440 | tf_op jit(solution)/shard_map/ppermute | solution.py:541
  10.3 0.0 copy-start.3
  10.3 0.0 copy-start.4
  10.3 2.5 %collective-permute-start.4 = (bf16[2,128,512]{2,1,0:T(8,128)(2,1)S(1)}, bf16[2,128,512]{2,1,0:T(8,128)(2,1)S(1)}, u32[]{:S(2)}, u32[]{:S(2)}) collective-permute-start(bf16[2,128,512]{2,1,0:T(8,128)(2,1)S(1)} %get-tuple-element.32), channel_id=1, source_target_pairs={{0,12},{4,8},{8,4},{12,0},{1,13},{5,9},{9,5},{13,1},{2,14},{6,10},... | collective-permute-start | bytes 786440 | tf_op jit(solution)/shard_map/ppermute | solution.py:541
  12.7 0.0 collective-permute-done.1.far3_ref
  12.7 0.6 collective-permute-start.5
  13.3 0.0 collective-permute-done.2.far2_ref
  13.3 2.6 %collective-permute-done.near_ref = bf16[2,128,384]{2,1,0:T(8,128)(2,1)S(1)} collective-permute-done((bf16[2,128,384]{2,1,0:T(8,128)(2,1)S(1)}, bf16[2,128,384]{2,1,0:T(8,128)(2,1)S(1)}, u32[]{:S(2)}, u32[]{:S(2)}) %collective-permute-start) | collective-permute-done | bytes 196640 | tf_op jit(solution)/shard_map/ppermute | solution.py:541
  15.9 0.0 copy-done
  15.9 0.0 copy-done.3
  15.9 0.0 copy-done.4
  15.9 0.0 copy-start.2
  15.9 1.2 %copy-done.2 = bf16[1,2,512,512]{3,2,1,0:T(8,128)(2,1)S(1)} copy-done((bf16[1,2,512,512]{3,2,1,0:T(8,128)(2,1)S(1)}, bf16[1,2,512,512]{3,2,1,0:T(8,128)(2,1)}, u32[]{:S(2)}) %copy-start.2) | copy-done | bytes 1048600
  17.2 3.9 %roots.1 = (bf16[2,512,512]{2,1,0:T(8,128)(2,1)S(1)}, f32[2,8,128]{2,1,0:T(8,128)S(1)}) custom-call(s32[9]{0:T(128)S(1)} %compare_select_fusion.plan_ref, s32[1,8]{1,0:T(1,128)S(1)} %copy-done.3, s32[1,8]{1,0:T(1,128)S(1)} %copy-done.4, bf16[1,8,128,512]{3,2,1,0:T(8,128)(2,1)S(1)} %copy-done, bf16[2,128,384]{2,1,0:T(8,128)(2,1)S(1)} %collective-permute-done.near_ref, ...), custom_call_target="tpu_custom_call" | custom-call | flops 4831838208 | bytes 3145728 | tf_op jit(solution)/shard_map/roots/pallas_call | solution.py:387
  21.1 7.6 %collective-permute-done.3.grad1_ref.rest_1_ = bf16[2,128,512]{2,1,0:T(8,128)(2,1)S(1)} collective-permute-done((bf16[2,128,512]{2,1,0:T(8,128)(2,1)S(1)}, bf16[2,128,512]{2,1,0:T(8,128)(2,1)S(1)}, u32[]{:S(2)}, u32[]{:S(2)}) %collective-permute-start.3) | collective-permute-done | bytes 262176 | tf_op jit(solution)/shard_map/ppermute | solution.py:541
  28.7 1.1 %start_product.1 = (bf16[2,256,256]{2,1,0:T(8,128)(2,1)S(1)}, bf16[2,256,256]{2,1,0:T(8,128)(2,1)S(1)}, f32[2,256,512]{2,1,0:T(8,128)S(1)}, f32[2,256,512]{2,1,0:T(8,128)S(1)}) custom-call(s32[9]{0:T(128)S(1)} %compare_select_fusion.plan_ref, bf16[2,512,512]{2,1,0:T(8,128)(2,1)S(1)} %get-tuple-element.26.root_ref, ...), custom_call_target="tpu_custom_call" | custom-call | flops 268435456 | bytes 2097152 | tf_op jit(solution)/shard_map/start_product/pallas_call | solution.py:439
  29.8 0.0 collective-permute-done.4.grad3_ref
  29.8 5.5 %collective-permute-done.5.grad2_ref = bf16[2,128,512]{2,1,0:T(8,128)(2,1)S(1)} collective-permute-done((bf16[2,128,512]{2,1,0:T(8,128)(2,1)S(1)}, bf16[2,128,512]{2,1,0:T(8,128)(2,1)S(1)}, u32[]{:S(2)}, u32[]{:S(2)}) %collective-permute-start.5) | collective-permute-done | bytes 262176 | tf_op jit(solution)/shard_map/ppermute | solution.py:541
  35.3 0.3 far_product.1
  35.6 3.4 %collective-permute-start.9 = (bf16[2,128,512]{2,1,0:T(8,128)(2,1)S(1)}, bf16[2,128,512]{2,1,0:T(8,128)(2,1)S(1)}, u32[]{:S(2)}, u32[]{:S(2)}) collective-permute-start(bf16[2,128,512]{2,1,0:T(8,128)(2,1)S(1)} %get-tuple-element.37.rest_3_), channel_id=1, source_target_pairs={{0,12},{4,8},{8,4},{12,0},{1,13},{5,9},{9,5},{13,1},{2,14},{6,10},... | collective-permute-start | bytes 786440 | tf_op jit(solution)/shard_map/ppermute | solution.py:541
  38.9 0.8 %near_product.1 = (bf16[2,128,512]{2,1,0:T(8,128)(2,1)S(1)}, bf16[2,128,512]{2,1,0:T(8,128)(2,1)S(1)}, f32[1,128]{1,0:T(1,128)S(1)}) custom-call(bf16[2,256,256]{2,1,0:T(8,128)(2,1)S(1)} %get-tuple-element.29.root_ref, f32[2,256,512]{2,1,0:T(8,128)S(1)} %get-tuple-element.30.begun_ref, f32[2,8,128]{2,1,0:T(8,128)S(1)} %get-tuple-element.31.factor_ref, ...), custom_call_target="tpu_custom_call" | custom-call | flops 134217728 | bytes 2097152 | tf_op jit(solution)/shard_map/near_product/pallas_call | solution.py:481
  39.8 0.1 collective-permute-start.8
  39.8 1.6 %collective-permute-start.7 = (f32[1,128]{1,0:T(1,128)S(1)}, f32[1,128]{1,0:T(1,128)S(1)}, u32[]{:S(2)}, u32[]{:S(2)}) collective-permute-start(f32[1,128]{1,0:T(1,128)S(1)} %get-tuple-element.38), channel_id=1, source_target_pairs={{0,2},{1,3},{2,0},{3,1},{4,6},{5,7},{6,4},{7,5},{8,10},{9,11},{10,... | collective-permute-start | bytes 1544 | tf_op jit(solution)/shard_map/ppermute | solution.py:548
  41.4 0.2 collective-permute-start.6
  41.5 0.0 collective-permute-start.14
  41.5 0.0 collective-permute-done.8
  41.5 1.1 %collective-permute-start.13 = (bf16[2,128,512]{2,1,0:T(8,128)(2,1)S(1)}, bf16[2,128,512]{2,1,0:T(8,128)(2,1)S(1)}, u32[]{:S(2)}, u32[]{:S(2)}) collective-permute-start(bf16[2,128,512]{2,1,0:T(8,128)(2,1)S(1)} %get-tuple-element.40), channel_id=1, source_target_pairs={{0,4},{4,0},{8,12},{12,8},{1,5},{5,1},{9,13},{13,9},{2,6},{6,2},{1... | collective-permute-start | bytes 786440 | tf_op jit(solution)/shard_map/ppermute | solution.py:541
  42.6 0.8 %collective-permute-done.7 = f32[1,128]{1,0:T(1,128)S(1)} collective-permute-done((f32[1,128]{1,0:T(1,128)S(1)}, f32[1,128]{1,0:T(1,128)S(1)}, u32[]{:S(2)}, u32[]{:S(2)}) %collective-permute-start.7) | collective-permute-done | bytes 544 | tf_op jit(solution)/shard_map/ppermute | solution.py:548
  43.4 0.9 %collective-permute-done.6 = f32[1,128]{1,0:T(1,128)S(1)} collective-permute-done((f32[1,128]{1,0:T(1,128)S(1)}, f32[1,128]{1,0:T(1,128)S(1)}, u32[]{:S(2)}, u32[]{:S(2)}) %collective-permute-start.6) | collective-permute-done | bytes 544 | tf_op jit(solution)/shard_map/ppermute | solution.py:548
  44.3 1.7 %collective-permute-start.12 = (f32[1,128]{1,0:T(1,128)S(1)}, f32[1,128]{1,0:T(1,128)S(1)}, u32[]{:S(2)}, u32[]{:S(2)}) collective-permute-start(f32[1,128]{1,0:T(1,128)S(1)} %add_add_fusion.value_ref.rest_0_), channel_id=1, source_target_pairs={{0,12},{4,8},{8,4},{12,0},{1,13},{5,9},{9,5},{13,1},{2,14},{6,10},... | collective-permute-start | bytes 1544 | tf_op jit(solution)/shard_map/ppermute | solution.py:541
  46.0 0.0 collective-permute-start.11
  46.0 0.0 collective-permute-done.9.landed_ref.rest_7_
  46.0 9.3 %collective-permute-start.10 = (f32[1,128]{1,0:T(1,128)S(1)}, f32[1,128]{1,0:T(1,128)S(1)}, u32[]{:S(2)}, u32[]{:S(2)}) collective-permute-start(f32[1,128]{1,0:T(1,128)S(1)} %after.1), channel_id=1, source_target_pairs={{0,4},{4,0},{8,12},{12,8},{1,5},{5,1},{9,13},{13,9},{2,6},{6,2},{1... | collective-permute-start | bytes 1544 | tf_op jit(solution)/shard_map/ppermute | solution.py:541
  55.3 0.0 collective-permute-done.12.rest_3_
  55.3 2.5 %collective-permute-done.11.rest_2_ = f32[1,128]{1,0:T(1,128)S(1)} collective-permute-done((f32[1,128]{1,0:T(1,128)S(1)}, f32[1,128]{1,0:T(1,128)S(1)}, u32[]{:S(2)}, u32[]{:S(2)}) %collective-permute-start.11) | collective-permute-done | bytes 544 | tf_op jit(solution)/shard_map/ppermute | solution.py:541
  57.8 0.0 collective-permute-done.13.rest_5_
  57.8 0.0 collective-permute-done.14.rest_6_
  57.8 0.0 collective-permute-done.10.rest_1_
  57.8 1.2 %clip.1 = bf16[1,8,128,512]{3,2,1,0:T(8,128)(2,1)} custom-call(s32[1,9]{1,0:T(1,128)S(1)} %compare_select_fusion.1.plan_ref, f32[1,128]{1,0:T(1,128)S(1)} %add_add_fusion.value_ref.rest_0_, f32[1,128]{1,0:T(1,128)S(1)} %collective-permute-done.10.rest_1_, f32[1,128]{1,0:T(1,128)S(1)} %collective-permute-done.11.rest_2_, ...), custom_call_target="tpu_custom_call" | custom-call | bytes 2097152 | tf_op jit(solution)/shard_map/clip/pallas_call | solution.py:514
  (7 shorter events, 0.0 us)
Async XLA Ops:
  0.0 8.2 %copy-start.1 = (bf16[1,8,128,512]{3,2,1,0:T(8,128)(2,1)S(1)}, bf16[1,8,128,512]{3,2,1,0:T(8,128)(2,1)}, u32[]{:S(2)}) copy-start(bf16[1,8,128,512]{3,2,1,0:T(8,128)(2,1)} %grad_ref.1) | copy-start | bytes 3145732
  0.0 15.9 %copy-start = (bf16[1,8,128,512]{3,2,1,0:T(8,128)(2,1)S(1)}, bf16[1,8,128,512]{3,2,1,0:T(8,128)(2,1)}, u32[]{:S(2)}) copy-start(bf16[1,8,128,512]{3,2,1,0:T(8,128)(2,1)} %stats_ref.1) | copy-start | bytes 3145732
  1.7 11.1 %collective-permute-start.1 = (bf16[272,128]{1,0:T(8,128)(2,1)S(1)}, bf16[272,128]{1,0:T(8,128)(2,1)S(1)}, u32[]{:S(2)}, u32[]{:S(2)}) collective-permute-start(bf16[272,128]{1,0:T(8,128)(2,1)S(1)} %get-tuple-element.24), channel_id=1, source_target_pairs={{0,12},{4,8},{8,4},{12,0},{1,13},{5,9},{9,5},{13,1},{2,14},{6,10},... | collective-permute-start | bytes 208904 | tf_op jit(solution)/shard_map/ppermute | solution.py:541
  6.8 6.5 %collective-permute-start.2 = (bf16[272,128]{1,0:T(8,128)(2,1)S(1)}, bf16[272,128]{1,0:T(8,128)(2,1)S(1)}, u32[]{:S(2)}, u32[]{:S(2)}) collective-permute-start(bf16[272,128]{1,0:T(8,128)(2,1)S(1)} %get-tuple-element.25), channel_id=1, source_target_pairs={{0,8},{4,12},{8,0},{12,4},{1,9},{5,13},{9,1},{13,5},{2,10},{6,14},... | collective-permute-start | bytes 208904 | tf_op jit(solution)/shard_map/ppermute | solution.py:541
  6.8 9.1 %collective-permute-start = (bf16[2,128,384]{2,1,0:T(8,128)(2,1)S(1)}, bf16[2,128,384]{2,1,0:T(8,128)(2,1)S(1)}, u32[]{:S(2)}, u32[]{:S(2)}) collective-permute-start(bf16[2,128,384]{2,1,0:T(8,128)(2,1)S(1)} %get-tuple-element.23), channel_id=1, source_target_pairs={{0,4},{4,0},{8,12},{12,8},{1,5},{5,1},{9,13},{13,9},{2,6},{6,2},{1... | collective-permute-start | bytes 589832 | tf_op jit(solution)/shard_map/ppermute | solution.py:541
  8.8 19.9 %collective-permute-start.3 = (bf16[2,128,512]{2,1,0:T(8,128)(2,1)S(1)}, bf16[2,128,512]{2,1,0:T(8,128)(2,1)S(1)}, u32[]{:S(2)}, u32[]{:S(2)}) collective-permute-start(bf16[2,128,512]{2,1,0:T(8,128)(2,1)S(1)} %get-tuple-element.28), channel_id=1, source_target_pairs={{0,4},{4,0},{8,12},{12,8},{1,5},{5,1},{9,13},{13,9},{2,6},{6,2},{1... | collective-permute-start | bytes 786440 | tf_op jit(solution)/shard_map/ppermute | solution.py:541
  10.3 5.7 %copy-start.3 = (s32[1,8]{1,0:T(1,128)S(1)}, s32[1,8]{1,0:T(1,128)}, u32[]{:S(2)}) copy-start(s32[1,8]{1,0:T(1,128)} %due_ref.1) | copy-start | bytes 100
  10.3 5.7 %copy-start.4 = (s32[1,8]{1,0:T(1,128)S(1)}, s32[1,8]{1,0:T(1,128)}, u32[]{:S(2)}) copy-start(s32[1,8]{1,0:T(1,128)} %cost_ref.1) | copy-start | bytes 100
  10.3 19.5 %collective-permute-start.4 = (bf16[2,128,512]{2,1,0:T(8,128)(2,1)S(1)}, bf16[2,128,512]{2,1,0:T(8,128)(2,1)S(1)}, u32[]{:S(2)}, u32[]{:S(2)}) collective-permute-start(bf16[2,128,512]{2,1,0:T(8,128)(2,1)S(1)} %get-tuple-element.32), channel_id=1, source_target_pairs={{0,12},{4,8},{8,4},{12,0},{1,13},{5,9},{9,5},{13,1},{2,14},{6,10},... | collective-permute-start | bytes 786440 | tf_op jit(solution)/shard_map/ppermute | solution.py:541
  12.7 22.5 %collective-permute-start.5 = (bf16[2,128,512]{2,1,0:T(8,128)(2,1)S(1)}, bf16[2,128,512]{2,1,0:T(8,128)(2,1)S(1)}, u32[]{:S(2)}, u32[]{:S(2)}) collective-permute-start(bf16[2,128,512]{2,1,0:T(8,128)(2,1)S(1)} %get-tuple-element.33), channel_id=1, source_target_pairs={{0,8},{4,12},{8,0},{12,4},{1,9},{5,13},{9,1},{13,5},{2,10},{6,14},... | collective-permute-start | bytes 786440 | tf_op jit(solution)/shard_map/ppermute | solution.py:541
  15.9 1.2 %copy-start.2 = (bf16[1,2,512,512]{3,2,1,0:T(8,128)(2,1)S(1)}, bf16[1,2,512,512]{3,2,1,0:T(8,128)(2,1)}, u32[]{:S(2)}) copy-start(bf16[1,2,512,512]{3,2,1,0:T(8,128)(2,1)} %stale_ref.1) | copy-start | bytes 3145732
  35.6 10.4 %collective-permute-start.9 = (bf16[2,128,512]{2,1,0:T(8,128)(2,1)S(1)}, bf16[2,128,512]{2,1,0:T(8,128)(2,1)S(1)}, u32[]{:S(2)}, u32[]{:S(2)}) collective-permute-start(bf16[2,128,512]{2,1,0:T(8,128)(2,1)S(1)} %get-tuple-element.37.rest_3_), channel_id=1, source_target_pairs={{0,12},{4,8},{8,4},{12,0},{1,13},{5,9},{9,5},{13,1},{2,14},{6,10},... | collective-permute-start | bytes 786440 | tf_op jit(solution)/shard_map/ppermute | solution.py:541
  39.8 1.8 %collective-permute-start.8 = (f32[1,128]{1,0:T(1,128)S(1)}, f32[1,128]{1,0:T(1,128)S(1)}, u32[]{:S(2)}, u32[]{:S(2)}) collective-permute-start(f32[1,128]{1,0:T(1,128)S(1)} %get-tuple-element.38), channel_id=1, source_target_pairs={{0,3},{1,0},{2,1},{3,2},{4,7},{5,4},{6,5},{7,6},{8,11},{9,8},{10,9... | collective-permute-start | bytes 1544 | tf_op jit(solution)/shard_map/ppermute | solution.py:548
  39.8 3.6 %collective-permute-start.7 = (f32[1,128]{1,0:T(1,128)S(1)}, f32[1,128]{1,0:T(1,128)S(1)}, u32[]{:S(2)}, u32[]{:S(2)}) collective-permute-start(f32[1,128]{1,0:T(1,128)S(1)} %get-tuple-element.38), channel_id=1, source_target_pairs={{0,2},{1,3},{2,0},{3,1},{4,6},{5,7},{6,4},{7,5},{8,10},{9,11},{10,... | collective-permute-start | bytes 1544 | tf_op jit(solution)/shard_map/ppermute | solution.py:548
  41.4 3.0 %collective-permute-start.6 = (f32[1,128]{1,0:T(1,128)S(1)}, f32[1,128]{1,0:T(1,128)S(1)}, u32[]{:S(2)}, u32[]{:S(2)}) collective-permute-start(f32[1,128]{1,0:T(1,128)S(1)} %get-tuple-element.38), channel_id=1, source_target_pairs={{0,1},{1,2},{2,3},{3,0},{4,5},{5,6},{6,7},{7,4},{8,9},{9,10},{10,1... | collective-permute-start | bytes 1544 | tf_op jit(solution)/shard_map/ppermute | solution.py:548
  41.5 16.3 %collective-permute-start.14 = (bf16[2,128,512]{2,1,0:T(8,128)(2,1)S(1)}, bf16[2,128,512]{2,1,0:T(8,128)(2,1)S(1)}, u32[]{:S(2)}, u32[]{:S(2)}) collective-permute-start(bf16[2,128,512]{2,1,0:T(8,128)(2,1)S(1)} %get-tuple-element.36.rest_2_), channel_id=1, source_target_pairs={{0,8},{4,12},{8,0},{12,4},{1,9},{5,13},{9,1},{13,5},{2,10},{6,14},... | collective-permute-start | bytes 786440 | tf_op jit(solution)/shard_map/ppermute | solution.py:541
  41.5 16.3 %collective-permute-start.13 = (bf16[2,128,512]{2,1,0:T(8,128)(2,1)S(1)}, bf16[2,128,512]{2,1,0:T(8,128)(2,1)S(1)}, u32[]{:S(2)}, u32[]{:S(2)}) collective-permute-start(bf16[2,128,512]{2,1,0:T(8,128)(2,1)S(1)} %get-tuple-element.40), channel_id=1, source_target_pairs={{0,4},{4,0},{8,12},{12,8},{1,5},{5,1},{9,13},{13,9},{2,6},{6,2},{1... | collective-permute-start | bytes 786440 | tf_op jit(solution)/shard_map/ppermute | solution.py:541
  44.3 11.0 %collective-permute-start.12 = (f32[1,128]{1,0:T(1,128)S(1)}, f32[1,128]{1,0:T(1,128)S(1)}, u32[]{:S(2)}, u32[]{:S(2)}) collective-permute-start(f32[1,128]{1,0:T(1,128)S(1)} %add_add_fusion.value_ref.rest_0_), channel_id=1, source_target_pairs={{0,12},{4,8},{8,4},{12,0},{1,13},{5,9},{9,5},{13,1},{2,14},{6,10},... | collective-permute-start | bytes 1544 | tf_op jit(solution)/shard_map/ppermute | solution.py:541
  46.0 11.8 %collective-permute-start.11 = (f32[1,128]{1,0:T(1,128)S(1)}, f32[1,128]{1,0:T(1,128)S(1)}, u32[]{:S(2)}, u32[]{:S(2)}) collective-permute-start(f32[1,128]{1,0:T(1,128)S(1)} %add_add_fusion.value_ref.rest_0_), channel_id=1, source_target_pairs={{0,8},{4,12},{8,0},{12,4},{1,9},{5,13},{9,1},{13,5},{2,10},{6,14},... | collective-permute-start | bytes 1544 | tf_op jit(solution)/shard_map/ppermute | solution.py:541
  46.0 11.8 %collective-permute-start.10 = (f32[1,128]{1,0:T(1,128)S(1)}, f32[1,128]{1,0:T(1,128)S(1)}, u32[]{:S(2)}, u32[]{:S(2)}) collective-permute-start(f32[1,128]{1,0:T(1,128)S(1)} %after.1), channel_id=1, source_target_pairs={{0,4},{4,0},{8,12},{12,8},{1,5},{5,1},{9,13},{13,9},{2,6},{6,2},{1... | collective-permute-start | bytes 1544 | tf_op jit(solution)/shard_map/ppermute | solution.py:541
